TPU v7x, 128 devices: a whole 4x4x4 slice. The times are simulated.
128 devices in a mesh: ulysses: 8 (over y_hi, x), blk: 16 (over z, y_lo, core).
Axes of the slice: x: 4, y: 4 (y_hi: 2, y_lo: 2; y = y_hi * 2 + y_lo), z: 4, core: 2. Of those that a mesh axis runs over, the one named last changes fastest.
Arguments:
- tokens: bfloat16 [16384, 2048], P(('ulysses', 'blk')), may hold values from -6 to 6
- cotangent: bfloat16 [16384, 2048], P(('ulysses', 'blk')), may hold values from -6 to 6
- doc_ids: int32 [128], replicated, may hold values from 0 to 20, never falling along the last dimension, each value on 1 to 16 neighbouring positions
- ln1_gain: bfloat16 [2048], P('blk'), may hold values from 0.099609375 to 1.8984375
- ln1_shift: bfloat16 [2048], P('blk'), may hold values from -1.75 to 1.75
- w_qkv: bfloat16 [2048, 3, 2048], P('blk', None, 'ulysses'), may hold values from -0.125 to 0.125
- b_qkv: bfloat16 [3, 2048], P(None, ('ulysses', 'blk')), may hold values from -0.625 to 0.625
- w_out: bfloat16 [2048, 2048], P('ulysses', 'blk'), may hold values from -0.5 to 0.5
- ln2_gain: bfloat16 [2048], P('blk'), may hold values from 0.099609375 to 1.8984375
- ln2_shift: bfloat16 [2048], P('blk'), may hold values from -1.75 to 1.75
- w_gate: bfloat16 [2048, 5632], P('blk', 'ulysses'), may hold values from -0.125 to 0.125
- w_up: bfloat16 [2048, 5632], P('blk', 'ulysses'), may hold values from -0.125 to 0.125
- w_down: bfloat16 [5632, 2048], P('ulysses', 'blk'), may hold values from -0.15625 to 0.15625
Outputs:
- mixed: bfloat16 [16384, 2048], P(('ulysses', 'blk'))
- input_grad: float32 [16384, 2048], P(('ulysses', 'blk'))
- ln1_gain_grad: float32 [2048], P(('ulysses', 'blk'))
- ln1_shift_grad: float32 [2048], P(('ulysses', 'blk'))
- w_qkv_grad: float32 [2048, 3, 2048], P('blk', None, 'ulysses')
- b_qkv_grad: float32 [3, 2048], P(None, ('ulysses', 'blk'))
- w_out_grad: float32 [2048, 2048], P('ulysses', 'blk')
- ln2_gain_grad: float32 [2048], P(('ulysses', 'blk'))
- ln2_shift_grad: float32 [2048], P(('ulysses', 'blk'))
- w_gate_grad: float32 [2048, 5632], P('blk', 'ulysses')
- w_up_grad: float32 [2048, 5632], P('blk', 'ulysses')
- w_down_grad: float32 [5632, 2048], P('ulysses', 'blk')
Inputs may be any that keep to these rules, and one draw needn't show every extreme that they name: `doc_ids`: document numbers never fall along the blocks; each of the 21 documents covers 1 to 16 consecutive blocks, one exactly 16.
All inputs are finite; a program needn't handle non-finite values.
Results may differ from a plain program's by a relative error of at most 0.035.
Values may be sent and summed in bfloat16 or wider, within the bound.
No kernel may reach another device: no remote copies, remote signals or barrier semaphores. Data moves between devices by JAX's collectives and lax.ppermute only.
A program may use at most 128 MiB of HBM per device.

v0:
```python
import functools

import jax
import jax.numpy as jnp
from jax import lax
from jax.experimental import pallas as pl
from jax.experimental.pallas import tpu as pltpu
from jax.sharding import Mesh
from jax.sharding import PartitionSpec as P

D = 2048
HEADS = 32
HEAD_DIM = 64
ROT = 16
BLK_TOK = 128
HID = 704
HID_PAD = 768
SHARED = 3 * HID_PAD + 256

eps = 1e-05
rope_base = 10000.0
masked_score = -1e30
score_scale = HEAD_DIM ** (-0.5)

AXES = ("yh", "x", "z", "yl", "k")
PLANE = ("z", "yh", "yl", "k")
BLK = ("z", "yl", "k")
Y = ("yh", "yl")

VMEM_LIMIT = 60 * 1024 * 1024
TINY = pl.CostEstimate(flops=1, bytes_accessed=1, transcendentals=0)


def mm(a, b, ca=1, cb=0):
    return lax.dot_general(a, b, (((ca,), (cb,)), ((), ())), preferred_element_type=jnp.float32)


def swap_core(value):
    return lax.ppermute(value, ("k",), [(0, 1), (1, 0)])


def exchange(parts, axes):
    return lax.all_to_all(parts, axes, 0, 0, tiled=True)


def send(value, axes, step):
    return lax.ppermute(value, axes, [(i, (i + step) % 4) for i in range(4)])


def ring_gather(value):
    return exchange(jnp.broadcast_to(value, (4,) + value.shape), ("x",))


def send(value, axes, step):
    return lax.ppermute(value, axes, [(i, (i + step) % 4) for i in range(4)])


def gather(value, axes, *others):
    me = lax.axis_index(axes)
    pieces = [send(value, axes, step) for step in (1, 3, 2)]
    if others:
        pieces = after(pieces, *others)
    buffer = jnp.zeros((4,) + value.shape, value.dtype)
    for step, piece in zip((0, 1, 3, 2), [value] + pieces):
        buffer = lax.dynamic_update_index_in_dim(buffer, piece, (me - step) % 4, 0)
    return buffer


def ring_gather(value):
    return exchange(jnp.broadcast_to(value, (4,) + value.shape), ("x",))


def after(value, *others):
    return lax.optimization_barrier((value,) + others)[0]


def rotary_tables(positions):
    halfway = ROT // 2
    counter = jnp.arange(halfway, dtype=jnp.float32)
    frequency = rope_base ** (-2.0 * counter / ROT)
    lane = jnp.arange(128) % HEAD_DIM
    frequency = jnp.where(lane < ROT, jnp.tile(frequency, 16), 0.0)
    angles = positions.astype(jnp.float32)[:, None] * frequency[None, :]
    sine = jnp.sin(angles)
    return (
        jnp.cos(angles),
        jnp.where(lane < halfway, -sine, 0.0),
        jnp.where((lane >= halfway) & (lane < ROT), sine, 0.0),
    )


def pack_joint_kernel(qkv_ref, out_ref, vectors_ref, bias_ref, w_ref, small_ref):
    out_t = jnp.transpose(out_ref[...])
    for j in range(2):
        pair = slice(j * 128, (j + 1) * 128)
        for part in range(3):
            column = j * 512 + part * 128
            w_ref[:128, column : column + 128] = qkv_ref[part, :, pair]
        w_ref[:128, j * 512 + 384 : j * 512 + 512] = out_t[:, pair]
    small_ref[...] = jnp.zeros_like(small_ref)
    small_ref[0:4, :128] = vectors_ref[...].astype(jnp.float32)
    small_ref[8:11, :16] = bias_ref[...].astype(jnp.float32)
    w_ref[128:, :] = small_ref[...].astype(jnp.bfloat16)


def pack_joint_call(qkv, out, vectors, bias):
    return whole_call(
        pack_joint_kernel,
        jax.ShapeDtypeStruct((144, 1024), jnp.bfloat16),
        qkv,
        out,
        vectors,
        bias,
        scratch=[pltpu.VMEM((16, 1024), jnp.float32)],
    )


def pack_hidden_kernel(gate_ref, up_ref, down_ref, rest_ref):
    for i, ref in enumerate((gate_ref, up_ref, down_ref)):
        first = i * HID_PAD
        rest_ref[:, first + HID_PAD - 128 : first + HID_PAD] = jnp.zeros((128, 128), jnp.bfloat16)
        rest_ref[:, first : first + HID] = jnp.transpose(ref[...])


def pack_hidden_call(gate, up, down):
    return whole_call(
        pack_hidden_kernel, jax.ShapeDtypeStruct((128, 3 * HID_PAD), jnp.bfloat16), gate, up, down
    )


def core_columns(ref, core, blocks):
    columns = [ref[:blocks, :, pl.ds(pl.multiple_of((2 * i + core) * 128, 128), 128)] for i in range(8)]
    return jnp.concatenate(columns, 2).reshape(blocks * 128, 1024)


def normalise(values):
    centred = values - jnp.mean(values, -1, keepdims=True)
    inverse = lax.rsqrt(jnp.mean(centred * centred, -1, keepdims=True) + eps)
    return centred * inverse, inverse


def qkv_kernel(
    x_ref,
    before_ref,
    gain_ref,
    shift_ref,
    w0_ref,
    w1_ref,
    bias_ref,
    cos_ref,
    up_ref,
    down_ref,
    out_ref,
    normed_ref,
    unit_ref,
    normed_rows,
):
    part = pl.program_id(1)

    @pl.when((pl.program_id(0) == 0) & (part == 0))
    def _():
        for b in range(5):
            block = x_ref[b] if b < 4 else before_ref[...]
            unit, _ = normalise(block.astype(jnp.float32))
            normed = (unit * gain_ref[...] + shift_ref[...]).astype(jnp.bfloat16)
            if b < 4:
                normed_ref[b] = normed
                unit_ref[b] = unit.astype(jnp.bfloat16)
            normed_rows[b * 128 : (b + 1) * 128] = normed

    def joint(rows):
        weights = [ref[:, 0, :, :128, :].reshape(D, 128) for ref in (w0_ref, w1_ref)]
        return mm(normed_rows[:rows], jnp.concatenate(weights, 1)) + bias_ref[0, 0]

    def turned(value):
        rows = value.shape[0]
        return (
            value * cos_ref[:rows]
            + pltpu.roll(value, 120, 1) * up_ref[:rows]
            + pltpu.roll(value, 8, 1) * down_ref[:rows]
        )

    @pl.when(part == 0)
    def _():
        value = joint(512)
        for j in range(2):
            query = turned(value[:, j * 128 : (j + 1) * 128]) * score_scale
            out_ref[:, j, 0, 4] = query.astype(jnp.bfloat16).reshape(4, 128, 128)

    @pl.when(part > 0)
    def _():
        value = joint(640)
        for j in range(2):
            block = value[:, j * 128 : (j + 1) * 128]
            block = jnp.where(part == 1, turned(block), block)
            block = block.astype(jnp.bfloat16).reshape(5, 128, 128)

            @pl.when(part == 1)
            def _():
                out_ref[:, j, 0, 2] = block[:4]
                out_ref[1:, j, 0, 0] = block[:3]
                out_ref[0, j, 0, 0] = block[4]

            @pl.when(part == 2)
            def _():
                out_ref[:, j, 0, 3] = block[:4]
                out_ref[1:, j, 0, 1] = block[:3]
                out_ref[0, j, 0, 1] = block[4]


def qkv_call(tokens, before, gain, shift, weights, bias, tables):
    table = pl.BlockSpec((640, 128), lambda h, p: (0, 0))
    vector = pl.BlockSpec((1, D), lambda h, p: (0, 0))
    return pl.pallas_call(
        qkv_kernel,
        grid=(2, 3),
        in_specs=[
            pl.BlockSpec((4, 128, D), lambda h, p: (0, 0, 0)),
            pl.BlockSpec((128, D), lambda h, p: (0, 0)),
            vector,
            vector,
            pl.BlockSpec((4, 1, 4, 144, 128), lambda h, p: (0, h, 0, 0, p)),
            pl.BlockSpec((4, 1, 4, 144, 128), lambda h, p: (0, h, 0, 0, p + 4)),
            pl.BlockSpec((1, 1, 1, 256), lambda h, p: (h, p, 0, 0)),
            table,
            table,
            table,
        ],
        out_specs=[
            pl.BlockSpec((4, 2, 1, 5, 128, 128), lambda h, p: (0, 0, h, 0, 0, 0)),
            pl.BlockSpec((4, 128, D), lambda h, p: (0, 0, 0)),
            pl.BlockSpec((4, 128, D), lambda h, p: (0, 0, 0)),
        ],
        out_shape=[
            jax.ShapeDtypeStruct((4, 2, 2, 5, 128, 128), jnp.bfloat16),
            jax.ShapeDtypeStruct((4, 128, D), jnp.bfloat16),
            jax.ShapeDtypeStruct((4, 128, D), jnp.bfloat16),
        ],
        scratch_shapes=[pltpu.VMEM((640, D), jnp.bfloat16)],
        compiler_params=pltpu.CompilerParams(vmem_limit_bytes=VMEM_LIMIT),
        cost_estimate=TINY,
    )(tokens, before, gain, shift, weights, weights, bias, *tables)


def whole_call(kernel, out_shape, *operands, scratch=()):
    vmem = pl.BlockSpec(memory_space=pltpu.VMEM)
    return pl.pallas_call(
        kernel,
        in_specs=[vmem] * len(operands),
        out_specs=jax.tree.map(lambda _: vmem, out_shape),
        out_shape=out_shape,
        scratch_shapes=list(scratch),
        compiler_params=pltpu.CompilerParams(vmem_limit_bytes=VMEM_LIMIT),
        cost_estimate=TINY,
    )(*operands)


def back_through(came_ref, values, gain):
    grad = came_ref[0].astype(jnp.float32)
    for i in range(1, 4):
        grad = grad + came_ref[i].astype(jnp.float32)
    unit, inverse = normalise(values)
    grad_unit = grad * gain
    centred_grad = (
        grad_unit
        - jnp.mean(grad_unit, -1, keepdims=True)
        - unit * jnp.mean(grad_unit * unit, -1, keepdims=True)
    )
    gain_grad = jnp.sum(grad * unit, 0, keepdims=True)
    return inverse * centred_grad, gain_grad, jnp.sum(grad, 0, keepdims=True)


def input_back_kernel(came_ref, tokens_ref, grad_ref, gain_ref, out_ref):
    values = tokens_ref[...].astype(jnp.float32)
    out_ref[...] = grad_ref[...] + back_through(came_ref, values, gain_ref[...])[0]


def shared_end_kernel(total_ref, gate_ref, up_ref, down_ref, out_ref):
    total = jnp.transpose(total_ref[...].astype(jnp.float32))
    for c in range(3):
        width = min(HID, c * 256 + 256) - c * 256
        gate_ref[c * 256 : c * 256 + width] = total[c * 512 : c * 512 + width]
        up_ref[c * 256 : c * 256 + width] = total[c * 512 + 256 : c * 512 + 256 + width]
    down_ref[...] = total[2 * HID_PAD : 2 * HID_PAD + HID]
    out_ref[...] = total[3 * HID_PAD :]


def joint_end_kernel(*refs):
    for j in range(2):
        total = sum(ref[...].astype(jnp.float32) for ref in refs[4 * j : 4 * j + 4])
        for part in range(3):
            refs[8][part, :, j * 128 : (j + 1) * 128] = total[:, part * 128 : part * 128 + 128]


def out_rows_kernel(place_ref, w0_ref, w1_ref, out_ref):
    for yl in range(2):
        for h in range(2):
            for j, ref in enumerate((w0_ref, w1_ref)):
                column = h * 256 + j * 128
                out_ref[yl, :, column : column + 128] = ref[0, h, 2 * yl + place_ref[1], :128]


def out_rows_call(place, weights):
    return pl.pallas_call(
        out_rows_kernel,
        grid=(4,),
        in_specs=[
            pl.BlockSpec(memory_space=pltpu.SMEM),
            pl.BlockSpec((1, 2, 4, 144, 128), lambda n: (n, 0, 0, 0, 3)),
            pl.BlockSpec((1, 2, 4, 144, 128), lambda n: (n, 0, 0, 0, 7)),
        ],
        out_specs=pl.BlockSpec((2, 128, 512), lambda n: (n, 0, 0)),
        out_shape=jax.ShapeDtypeStruct((8, 128, 512), jnp.bfloat16),
        compiler_params=pltpu.CompilerParams(vmem_limit_bytes=VMEM_LIMIT),
        cost_estimate=TINY,
    )(place, weights, weights)


def planes_columns(refs, yl):
    return jnp.concatenate([ref[yl] for ref in refs], 1)


def project_kernel(place_ref, att_ref, tokens_ref, gain_ref, shift_ref, *refs):
    own_refs, other_refs, (middle_ref, normed_ref, att_cols, total) = refs[:4], refs[4:8], refs[8:]
    n, me, core = pl.program_id(0), place_ref[0], place_ref[1]

    @pl.when(n == 0)
    def _():
        for t in range(4):
            x = (me + 4 - t) % 4
            for h in range(2):
                for j in range(2):
                    column = t * 512 + h * 256 + j * 128
                    att_cols[:, column : column + 128] = att_ref[x, j, h]

    weights = jnp.concatenate(
        [planes_columns(refs, yl) for refs in (own_refs, other_refs) for yl in range(2)], 0
    )
    values = mm(att_cols[...], weights, 1, 1)
    for i in range(4):
        holder = core if i < 2 else 1 - core
        column = pl.multiple_of((n * 4 + i % 2 * 2 + holder) * 128, 128)
        total[:, pl.ds(column, 128)] = values[:, i * 128 : i * 128 + 128]

    @pl.when(n == 3)
    def _():
        middle = tokens_ref[...].astype(jnp.float32) + total[...]
        middle_ref[...] = middle
        normed = (normalise(middle)[0] * gain_ref[...] + shift_ref[...]).astype(jnp.bfloat16)
        for i in range(4):
            normed_ref[i] = normed


def project_call(place, att, tokens, gain, shift, own, other):
    def whole(*dims):
        return pl.BlockSpec(dims, lambda n: (0,) * len(dims))

    rows = pl.BlockSpec((2, 128, 512), lambda n: (n, 0, 0))
    return pl.pallas_call(
        project_kernel,
        grid=(4,),
        in_specs=[
            pl.BlockSpec(memory_space=pltpu.SMEM),
            whole(4, 2, 2, 128, 128),
            whole(128, D),
            whole(1, D),
            whole(1, D),
        ]
        + [rows] * 8,
        out_specs=[whole(128, D), whole(4, 128, D)],
        out_shape=[
            jax.ShapeDtypeStruct((128, D), jnp.float32),
            jax.ShapeDtypeStruct((4, 128, D), jnp.bfloat16),
        ],
        scratch_shapes=[pltpu.VMEM((128, D), jnp.bfloat16), pltpu.VMEM((128, D), jnp.float32)],
        compiler_params=pltpu.CompilerParams(vmem_limit_bytes=VMEM_LIMIT),
        cost_estimate=TINY,
    )(place, att, tokens, gain, shift, *own, *other)


def project_back_kernel(place_ref, came_ref, middle_ref, cot_ref, gain_ref, *refs):
    own_refs, other_refs = refs[:4], refs[4:8]
    grad_ref, low_ref, gain_grad_ref, shift_grad_ref, out_ref, low, total = refs[8:]
    n, me, core = pl.program_id(0), place_ref[0], place_ref[1]

    @pl.when(n == 0)
    def _():
        grad, gain_grad_ref[...], shift_grad_ref[...] = back_through(came_ref, middle_ref[...], gain_ref[...])
        grad = grad + cot_ref[...].astype(jnp.float32)
        grad_ref[...] = grad
        low[...] = grad.astype(jnp.bfloat16)
        low_ref[...] = low[...]
        total[...] = jnp.zeros_like(total)

    columns = []
    for i in range(4):
        holder = core if i < 2 else 1 - core
        column = pl.multiple_of((n * 4 + i % 2 * 2 + holder) * 128, 128)
        columns.append(low[:, pl.ds(column, 128)])
    weights = jnp.concatenate(
        [planes_columns(refs, yl) for refs in (own_refs, other_refs) for yl in range(2)], 0
    )
    total[...] += mm(jnp.concatenate(columns, 1), weights)

    @pl.when(n == 3)
    def _():
        for t in range(4):
            x = (me + 4 - t) % 4
            for h in range(2):
                for j in range(2):
                    column = t * 512 + h * 256 + j * 128
                    out_ref[x, j, h] = total[:, column : column + 128].astype(jnp.bfloat16)


def project_back_call(place, came, middle, cot, gain, own, other):
    def whole(*dims):
        return pl.BlockSpec(dims, lambda n: (0,) * len(dims))

    rows = pl.BlockSpec((2, 128, 512), lambda n: (n, 0, 0))
    return pl.pallas_call(
        project_back_kernel,
        grid=(4,),
        in_specs=[
            pl.BlockSpec(memory_space=pltpu.SMEM),
            whole(4, 128, D),
            whole(128, D),
            whole(128, D),
            whole(1, D),
        ]
        + [rows] * 8,
        out_specs=[whole(128, D), whole(128, D), whole(1, D), whole(1, D), whole(4, 2, 2, 128, 128)],
        out_shape=[
            jax.ShapeDtypeStruct((128, D), jnp.float32),
            jax.ShapeDtypeStruct((128, D), jnp.bfloat16),
            jax.ShapeDtypeStruct((1, D), jnp.float32),
            jax.ShapeDtypeStruct((1, D), jnp.float32),
            jax.ShapeDtypeStruct((4, 2, 2, 128, 128), jnp.bfloat16),
        ],
        scratch_shapes=[pltpu.VMEM((128, D), jnp.bfloat16), pltpu.VMEM((128, D), jnp.float32)],
        compiler_params=pltpu.CompilerParams(vmem_limit_bytes=VMEM_LIMIT),
        cost_estimate=TINY,
    )(place, came, middle, cot, gain, *own, *other)


def feed_forward_kernel(
    x_ref, cot_ref, gate_ref, up_ref, down_ref, active_ref, grads_ref, back_ref, out_ref, back_sum, out_sum
):
    first_half = pl.program_id(0) == 0
    x = x_ref[...].reshape(512, D)
    cot = cot_ref[...].reshape(512, D)
    for c in range(3):
        columns = slice(c * 256, c * 256 + 256)
        gate = mm(x, gate_ref[:, 0, :, columns].reshape(D, 256))
        up = mm(x, up_ref[:, 0, :, columns].reshape(D, 256))
        grad_active = mm(cot, down_ref[:, 0, :, columns].reshape(D, 256))
        sigmoid = jax.nn.sigmoid(gate)
        silu = gate * sigmoid
        active_ref[0, :, columns] = (silu * up).astype(jnp.bfloat16)
        grad_gate = grad_active * up * (sigmoid + silu * (1.0 - sigmoid))
        grads_ref[0, :, c * 512 : c * 512 + 256] = grad_gate.astype(jnp.bfloat16)
        grads_ref[0, :, c * 512 + 256 : c * 512 + 512] = (grad_active * silu).astype(jnp.bfloat16)
    for n in range(4):
        rows = slice(n * 512, n * 512 + 512)
        weights = jnp.concatenate(
            [ref[n, 0, :, c * 256 : c * 256 + 256] for c in range(3) for ref in (gate_ref, up_ref)], 1
        )
        back = mm(grads_ref[0], weights, 1, 1)
        out = mm(active_ref[0], down_ref[n, 0], 1, 1)

        @pl.when(first_half)
        def _():
            back_sum[:, rows] = back
            out_sum[:, rows] = out

        @pl.when(~first_half)
        def _():
            back_ref[:, :, rows] = (back_sum[:, rows] + back).astype(jnp.bfloat16).reshape(4, 128, 512)
            out_ref[:, :, rows] = (out_sum[:, rows] + out).astype(jnp.bfloat16).reshape(4, 128, 512)


def feed_forward_call(x, ring, rest):
    tokens = pl.BlockSpec((4, 128, D), lambda h: (0, 0, 0))
    tokens_once = pl.BlockSpec((4, 128, D), lambda h: (0, 0, 0), pipeline_mode=pl.Buffered(1))
    weight = [pl.BlockSpec((4, 1, 512, HID_PAD), lambda h, i=i: (0, h, 0, i)) for i in range(3)]
    ring_shape = jax.ShapeDtypeStruct((4, 128, D), jnp.bfloat16)
    return pl.pallas_call(
        feed_forward_kernel,
        grid=(2,),
        in_specs=[tokens_once, tokens_once] + weight,
        out_specs=[
            pl.BlockSpec((1, 512, HID_PAD), lambda h: (h, 0, 0)),
            pl.BlockSpec((1, 512, 2 * HID_PAD), lambda h: (h, 0, 0)),
            tokens,
            tokens,
        ],
        out_shape=[
            jax.ShapeDtypeStruct((2, 512, HID_PAD), jnp.bfloat16),
            jax.ShapeDtypeStruct((2, 512, 2 * HID_PAD), jnp.bfloat16),
            ring_shape,
            ring_shape,
        ],
        scratch_shapes=[pltpu.VMEM((512, D), jnp.float32), pltpu.VMEM((512, D), jnp.float32)],
        compiler_params=pltpu.CompilerParams(vmem_limit_bytes=VMEM_LIMIT),
        cost_estimate=TINY,
    )(x, ring, rest, rest, rest)


def plane_grad_kernel(core_ref, left_ref, left_other_ref, right_ref, right_other_ref, *refs):
    out_ref, left_t = refs[-2:]

    @pl.when((pl.program_id(0) == 0) & (pl.program_id(1) == 0))
    def _():
        left_t[:, :512] = jnp.transpose(core_columns(left_ref, core_ref[0], 4))
        left_t[:, 512:] = jnp.transpose(core_columns(left_other_ref, core_ref[0], 4))

    total = mm(left_t[...], jnp.concatenate([right_ref[0], right_other_ref[0]], 0)).astype(jnp.bfloat16)
    for z in range(4):
        for yl in range(2):
            row = (z * 2 + yl) * 128
            out_ref[0, yl, z] = total[row : row + 128]


def plane_grad_call(core, left, right, columns, first, shared=None):
    left_block = pl.BlockSpec((4, 128, D), lambda n, h: (0, 0, 0))
    right_block = pl.BlockSpec((1, 512, 256), lambda n, h: (h, 0, n))
    extra = [] if shared is None else [shared]
    return pl.pallas_call(
        plane_grad_kernel,
        grid=(columns // 256, 2),
        in_specs=[
            pl.BlockSpec(memory_space=pltpu.SMEM),
            left_block,
            left_block,
            right_block,
            right_block,
        ]
        + [pl.BlockSpec(memory_space=pl.ANY)] * len(extra),
        out_specs=pl.BlockSpec((1, 2, 4, 128, 256), lambda n, h: (h, 0, 0, 0, first // 256 + n)),
        out_shape=jax.ShapeDtypeStruct((2, 2, 4, 128, SHARED), jnp.bfloat16),
        input_output_aliases={5: 0} if extra else {},
        scratch_shapes=[pltpu.VMEM((1024, 1024), jnp.bfloat16)],
        compiler_params=pltpu.CompilerParams(vmem_limit_bytes=VMEM_LIMIT),
        cost_estimate=TINY,
    )(core, *left, *right, *extra)


def weight_grad_kernel(core_ref, place_ref, left_ref, left_other_ref, right_ref, right_other_ref, *refs):
    outs, left_t = refs[:4], refs[4]
    h = pl.program_id(1)

    @pl.when((h == 0) & (pl.program_id(0) == 0))
    def _():
        left_t[:, :512] = jnp.transpose(core_columns(left_ref, core_ref[0], 4))
        left_t[:, 512:] = jnp.transpose(core_columns(left_other_ref, core_ref[0], 4))

    total = mm(left_t[...], jnp.concatenate([right_ref[0], right_other_ref[0]], 0)).astype(jnp.bfloat16)
    for z in range(4):
        for yl in range(2):
            row = (z * 2 + yl) * 128
            chip = (h * 2 + yl) * 4 + z
            step, slot = place_ref[0, chip], place_ref[1, chip]
            for t in range(4):

                @pl.when(step == t)
                def _():
                    outs[t][slot] = total[row : row + 128]


def weight_grad_call(core, place, left, right, columns):
    smem = pl.BlockSpec(memory_space=pltpu.SMEM)
    left_block = pl.BlockSpec((4, 128, D), lambda n, h: (0, 0, 0))
    right_block = pl.BlockSpec((1, 512, 256), lambda n, h: (h, 0, n))
    return pl.pallas_call(
        weight_grad_kernel,
        grid=(columns // 256, 2),
        in_specs=[smem, smem, left_block, left_block, right_block, right_block],
        out_specs=[pl.BlockSpec((4, 128, 256), lambda n, h: (0, 0, n))] * 4,
        out_shape=[jax.ShapeDtypeStruct((4, 128, columns), jnp.bfloat16)] * 4,
        scratch_shapes=[pltpu.VMEM((1024, 1024), jnp.bfloat16)],
        compiler_params=pltpu.CompilerParams(vmem_limit_bytes=VMEM_LIMIT),
        cost_estimate=TINY,
    )(core, place, *left, *right)


def joint_grad_kernel(core_ref, place_ref, left_ref, left_other_ref, right_ref, right_other_ref, *refs):
    outs, left_t = refs[:8], refs[8]
    h = pl.program_id(0)

    @pl.when(h == 0)
    def _():
        left_t[:, :512] = jnp.transpose(core_columns(left_ref, core_ref[0], 4))
        left_t[:, 512:] = jnp.transpose(core_columns(left_other_ref, core_ref[0], 4))

    right = jnp.concatenate([right_ref[0], right_other_ref[0]], 0)
    total = mm(left_t[...], right).astype(jnp.bfloat16)
    for z in range(4):
        for yl in range(2):
            row = (z * 2 + yl) * 128
            chip = (h * 2 + yl) * 4 + z
            for j in range(2):
                step, slot = place_ref[2 * j, chip], place_ref[2 * j + 1, chip]
                for t in range(4):

                    @pl.when(step == t)
                    def _():
                        outs[4 * j + t][slot] = total[row : row + 128, j * 384 : j * 384 + 384]


def joint_grad_call(core, places, left, right):
    smem = pl.BlockSpec(memory_space=pltpu.SMEM)
    left_block = pl.BlockSpec((4, 128, D), lambda h: (0, 0, 0))
    right_block = pl.BlockSpec((1, 512, 768), lambda h: (h, 0, 0))
    return pl.pallas_call(
        joint_grad_kernel,
        grid=(2,),
        in_specs=[smem, smem, left_block, left_block, right_block, right_block],
        out_specs=[pl.BlockSpec((4, 128, 384), lambda h: (0, 0, 0))] * 8,
        out_shape=[jax.ShapeDtypeStruct((4, 128, 384), jnp.bfloat16)] * 8,
        scratch_shapes=[pltpu.VMEM((1024, 1024), jnp.bfloat16)],
        compiler_params=pltpu.CompilerParams(vmem_limit_bytes=VMEM_LIMIT),
        cost_estimate=TINY,
    )(core, jnp.concatenate(places, 0), *left, *right)


def split_sum_kernel(place_ref, a_ref, b_ref, c_ref, d_ref, *out_refs):
    for t in range(4):
        i = (place_ref[0] + t) % 4
        total = sum(ref[i].astype(jnp.float32) for ref in (a_ref, b_ref, c_ref, d_ref))
        out_refs[t][...] = total.astype(jnp.bfloat16)


def split_sum_call(place, parts):
    columns = parts[0].shape[2]
    width = 256 if columns % 256 == 0 else 384
    return pl.pallas_call(
        split_sum_kernel,
        grid=(columns // width,),
        in_specs=[pl.BlockSpec(memory_space=pltpu.SMEM)]
        + [pl.BlockSpec((4, 128, width), lambda n: (0, 0, n))] * 4,
        out_specs=[pl.BlockSpec((128, width), lambda n: (0, n))] * 4,
        out_shape=[jax.ShapeDtypeStruct((128, columns), jnp.bfloat16)] * 4,
        compiler_params=pltpu.CompilerParams(vmem_limit_bytes=VMEM_LIMIT),
        cost_estimate=TINY,
    )(place, *parts)


def chip_places(y_first):
    y, z = jnp.arange(16, dtype=jnp.int32) // 4, jnp.arange(16, dtype=jnp.int32) % 4
    if y_first:
        return jnp.stack([(y - lax.axis_index(Y)) % 4, z])
    return jnp.stack([(z - lax.axis_index("z")) % 4, y])


def plane_sum(parts):
    parts = parts.reshape(2048, parts.shape[-1])
    return lax.psum_scatter(parts, ("yh", "yl", "z"), scatter_dimension=0, tiled=True)


def with_other(value):
    return value, swap_core(value)


def first_send(parts, y_first):
    axes = Y if y_first else ("z",)
    return [parts[0]] + [send(parts[t], axes, t) for t in (1, 3, 2)]


def first_sum(parts, y_first):
    return split_sum_call(lax.axis_index(("z",) if y_first else Y).reshape(1), parts)


def second_send(parts, y_first):
    axes = ("z",) if y_first else Y
    return [parts[0]] + [send(parts[t], axes, t) for t in (1, 3, 2)]


def stack_heads(ref, *index):
    first = (lax.broadcasted_iota(jnp.int32, (128, 128), 1) < HEAD_DIM).astype(jnp.float32).astype(jnp.bfloat16)
    masks = (first, 1 - first)
    return jnp.concatenate([ref[i] * mask for i in index for mask in masks], 0)


def unstack_heads(values, block):
    low = lax.broadcasted_iota(jnp.int32, (128, 128), 1) < HEAD_DIM
    rows = values[block * 256 : block * 256 + 256]
    return jnp.where(low, rows[:128], rows[128:])


def key_blocks(r_ref, block, slot):
    rows = []
    for i in range(4):
        index = jnp.maximum(block + i, 0)
        rows.append(r_ref[index & 15, (index >> 4) * 2 + slot])
    return jnp.concatenate(rows, 0)


def masked(values, a, block, lo_a, lo_b, diagonal, fill):
    key_row = lax.broadcasted_iota(jnp.int32, (128, 256), 0)
    causal = key_row <= lax.broadcasted_iota(jnp.int32, (128, 256), 1) % 128
    rows = []
    for k in range(4):
        parts = []
        for i, lo in enumerate((lo_a, lo_b)):
            mask = block + k >= lo
            if diagonal and k == 2 + i:
                mask = causal
            part = values[k * 128 : k * 128 + 128, i * 256 : i * 256 + 256]
            if diagonal and k == 3 and i == 0:
                parts.append(jnp.full((128, 256), fill, jnp.float32))
            else:
                parts.append(jnp.where(mask, part, fill))
        rows.append(jnp.concatenate(parts, 1))
    return jnp.concatenate(rows, 0)


def attend_kernel(lo_ref, r_ref, o32_ref, o16_ref, lse_ref):
    def one_pair(a, _):
        lo_a, lo_b = lo_ref[2 * a], lo_ref[2 * a + 1]
        queries = stack_heads(r_ref, (2 * a, 4), (2 * a + 1, 4))

        def scores(block, diagonal):
            values = mm(key_blocks(r_ref, block, 0), queries, 1, 1)
            return masked(values, a, block, lo_a, lo_b, diagonal, masked_score)

        def add(scores, block, top):
            weights = jnp.exp(scores - top)
            sums = mm(key_blocks(r_ref, block, 1), weights.astype(jnp.bfloat16), 0, 0)
            return jnp.sum(weights, 0, keepdims=True), sums

        diagonal = scores(2 * a + 14, True)
        top = jnp.max(diagonal, 0, keepdims=True)
        total, sums = add(diagonal, 2 * a + 14, top)

        def earlier(i, carry):
            top, total, sums = carry
            block = 2 * a + 14 - 4 * i
            values = scores(block, False)
            new = jnp.maximum(top, jnp.max(values, 0, keepdims=True))
            scale = jnp.exp(top - new)
            more, more_sums = add(values, block, new)
            return new, total * scale + more, sums * scale + more_sums

        steps = (2 * a + 21 - lo_a) // 4
        top, total, sums = lax.fori_loop(1, steps, earlier, (top, total, sums))
        out = jnp.transpose(sums / total)
        for block in range(2):
            rows = unstack_heads(out, block)
            o32_ref[2 * a + block] = rows
            o16_ref[2 * a + block] = rows.astype(jnp.bfloat16)
        lse_ref[a] = top + jnp.log(total)
        return 0

    lax.fori_loop(0, 8, one_pair, 0)


def attend_call(lo, blocks):
    vmem = pl.BlockSpec(memory_space=pltpu.VMEM)
    return pl.pallas_call(
        attend_kernel,
        in_specs=[pl.BlockSpec(memory_space=pltpu.SMEM), vmem],
        out_specs=[vmem, vmem, vmem],
        out_shape=[
            jax.ShapeDtypeStruct((16, 128, 128), jnp.float32),
            jax.ShapeDtypeStruct((16, 128, 128), jnp.bfloat16),
            jax.ShapeDtypeStruct((8, 1, 512), jnp.float32),
        ],
        compiler_params=pltpu.CompilerParams(vmem_limit_bytes=VMEM_LIMIT),
        cost_estimate=TINY,
    )(lo, blocks)


def attend_back_kernel(lo_ref, r_ref, do_ref, o32_ref, lse_ref, out_ref, dk_ref, dv_ref):
    dk_ref[...] = jnp.zeros_like(dk_ref)
    dv_ref[...] = jnp.zeros_like(dv_ref)

    def one_pair(a, _):
        lo_a, lo_b = lo_ref[2 * a], lo_ref[2 * a + 1]
        queries = stack_heads(r_ref, (2 * a, 4), (2 * a + 1, 4))
        grads = stack_heads(do_ref, 2 * a, 2 * a + 1)
        out = jnp.concatenate([o32_ref[2 * a]] * 2 + [o32_ref[2 * a + 1]] * 2, 0)
        delta = jnp.sum(jnp.transpose(grads.astype(jnp.float32) * out), 0, keepdims=True)
        lse = lse_ref[a]

        def blocks_back(block, diagonal):
            keys, values = key_blocks(r_ref, block, 0), key_blocks(r_ref, block, 1)
            weights = jnp.exp(mm(keys, queries, 1, 1) - lse)
            weights = masked(weights, a, block, lo_a, lo_b, diagonal, 0.0)
            grad_scores = (weights * (mm(values, grads, 1, 1) - delta)).astype(jnp.bfloat16)
            grad_values = mm(weights.astype(jnp.bfloat16), grads)
            grad_keys = mm(grad_scores, queries)
            for k in range(4):
                index, rows = jnp.maximum(block + k, 0), slice(k * 128, k * 128 + 128)
                dv_ref[index] += grad_values[rows]
                dk_ref[index] += grad_keys[rows]
            return mm(grad_scores, keys, 0, 0)

        def earlier(i, grad_query):
            return grad_query + blocks_back(2 * a + 14 - 4 * i, False)

        steps = (2 * a + 21 - lo_a) // 4
        grad_query = blocks_back(2 * a + 14, True)
        grad_query = lax.fori_loop(1, steps, earlier, grad_query)
        for block in range(2):
            rows = unstack_heads(grad_query, block) * score_scale
            out_ref[2 * a + block, 4] = rows.astype(jnp.bfloat16)
        return 0

    lax.fori_loop(0, 8, one_pair, 0)

    def finish(c, _):
        out_ref[c, 0] = dk_ref[c].astype(jnp.bfloat16)
        out_ref[c, 1] = dv_ref[c].astype(jnp.bfloat16)
        out_ref[c, 2] = dk_ref[c + 16].astype(jnp.bfloat16)
        out_ref[c, 3] = dv_ref[c + 16].astype(jnp.bfloat16)
        return 0

    lax.fori_loop(0, 16, finish, 0)


def attend_back_call(lo, blocks, grads, out, lse):
    vmem = pl.BlockSpec(memory_space=pltpu.VMEM)
    return pl.pallas_call(
        attend_back_kernel,
        in_specs=[pl.BlockSpec(memory_space=pltpu.SMEM), vmem, vmem, vmem, vmem],
        out_specs=vmem,
        out_shape=jax.ShapeDtypeStruct((16, 5, 128, 128), jnp.bfloat16),
        scratch_shapes=[
            pltpu.VMEM((32, 128, 128), jnp.float32),
            pltpu.VMEM((32, 128, 128), jnp.float32),
        ],
        compiler_params=pltpu.CompilerParams(vmem_limit_bytes=VMEM_LIMIT),
        cost_estimate=TINY,
    )(lo, blocks, grads, out, lse)


def turn_back_kernel(r_ref, halo_ref, cos_ref, up_ref, down_ref, out_ref, bias_ref):
    for j in range(2):
        sums = [jnp.zeros((1, 128), jnp.float32) for _ in range(3)]
        for x in range(4):
            rows = slice(x * 128, (x + 1) * 128)

            def turned(grad):
                return (
                    grad * cos_ref[rows]
                    - pltpu.roll(grad, 120, 1) * up_ref[rows]
                    - pltpu.roll(grad, 8, 1) * down_ref[rows]
                )

            def read(slot):
                later = r_ref[x + 1, j, 0, slot] if x < 3 else halo_ref[j, 0, slot]
                return r_ref[x, j, 0, slot + 2].astype(jnp.float32) + later.astype(jnp.float32)

            parts = (
                turned(r_ref[x, j, 0, 4].astype(jnp.float32)),
                turned(read(0)),
                read(1),
            )
            for part in range(3):
                grad = parts[part].astype(jnp.bfloat16)
                column = (j * 3 + part) * 128
                out_ref[0, rows, column : column + 128] = grad
                sums[part] = sums[part] + jnp.sum(grad.astype(jnp.float32), 0, keepdims=True)
        for part in range(3):
            column = (j * 3 + part) * 128
            bias_ref[0, :, column : column + 128] = sums[part]


def turn_back_call(blocks, halo, tables):
    table = pl.BlockSpec((512, 128), lambda h: (0, 0))
    return pl.pallas_call(
        turn_back_kernel,
        grid=(2,),
        in_specs=[
            pl.BlockSpec((4, 2, 1, 5, 128, 128), lambda h: (0, 0, h, 0, 0, 0)),
            pl.BlockSpec((2, 1, 2, 128, 128), lambda h: (0, h, 0, 0, 0)),
            table,
            table,
            table,
        ],
        out_specs=[
            pl.BlockSpec((1, 512, 768), lambda h: (h, 0, 0)),
            pl.BlockSpec((1, 1, 768), lambda h: (h, 0, 0)),
        ],
        out_shape=[
            jax.ShapeDtypeStruct((2, 512, 768), jnp.bfloat16),
            jax.ShapeDtypeStruct((2, 1, 768), jnp.float32),
        ],
        compiler_params=pltpu.CompilerParams(vmem_limit_bytes=VMEM_LIMIT),
        cost_estimate=TINY,
    )(blocks, halo, *tables)


def normed_back_kernel(g_ref, unit_ref, w_ref, out_ref, gain_grad_ref, shift_grad_ref):
    grads = jnp.concatenate([g_ref[0], g_ref[1]], 1)
    weights = jnp.concatenate(
        [
            w_ref[0, h, :, :128, j * 512 : j * 512 + 384].reshape(512, 384)
            for h in range(2)
            for j in range(2)
        ],
        1,
    )
    total = mm(grads, weights, 1, 1)
    out_ref[...] = total.astype(jnp.bfloat16).reshape(4, 128, 512)
    unit = unit_ref[...].reshape(512, 512).astype(jnp.float32)
    gain_grad_ref[...] = jnp.sum(total * unit, 0, keepdims=True)
    shift_grad_ref[...] = jnp.sum(total, 0, keepdims=True)


def normed_back_call(grad_joint, unit, weights):
    ring = pl.BlockSpec((4, 128, 512), lambda n: (0, 0, n))
    vector = pl.BlockSpec((1, 512), lambda n: (0, n))
    return pl.pallas_call(
        normed_back_kernel,
        grid=(4,),
        in_specs=[
            pl.BlockSpec((2, 512, 768), lambda n: (0, 0, 0)),
            ring,
            pl.BlockSpec((1, 2, 4, 144, 1024), lambda n: (n, 0, 0, 0, 0)),
        ],
        out_specs=[ring, vector, vector],
        out_shape=[
            jax.ShapeDtypeStruct((4, 128, D), jnp.bfloat16),
            jax.ShapeDtypeStruct((1, D), jnp.float32),
            jax.ShapeDtypeStruct((1, D), jnp.float32),
        ],
        compiler_params=pltpu.CompilerParams(vmem_limit_bytes=VMEM_LIMIT),
        cost_estimate=TINY,
    )(grad_joint, unit, weights)


def local(
    tokens,
    cotangent,
    doc_ids,
    ln1_gain,
    ln1_shift,
    w_qkv,
    b_qkv,
    w_out,
    ln2_gain,
    ln2_shift,
    w_gate,
    w_up,
    w_down,
):
    half = lax.axis_index("yh")
    blk = lax.axis_index(BLK)

    core = lax.axis_index("k").reshape(1)
    vectors = jnp.stack([ln1_gain, ln1_shift, ln2_gain, ln2_shift])
    joint_w = pack_joint_call(w_qkv.transpose(1, 0, 2), w_out, vectors, b_qkv)
    joint_w = lax.all_gather(joint_w, PLANE, axis=0).reshape(4, 2, 4, 144, 1024)
    ring = ring_gather(tokens)
    place = jnp.stack([lax.axis_index("x"), lax.axis_index("k")]).astype(jnp.int32)
    before = lax.ppermute(ring[3], ("yh",), [(0, 1)])
    ring_cot = lax.all_gather(after(cotangent, ring), "x", axis=0)
    rest = pack_hidden_call(w_gate.T, w_up.T, w_down)

    small = joint_w[:, :, :, 128:, :128].astype(jnp.float32)
    bias = small[:, :, :, 8:11, :16].transpose(1, 3, 0, 2, 4).reshape(2, 3, 1, 256)
    vectors = small[:, 0, :, :4].transpose(2, 0, 1, 3).reshape(4, D)
    gain_one, shift_one, gain_two, shift_two = [vectors[i : i + 1] for i in range(4)]

    first_block = jnp.sum((doc_ids[None, :] < doc_ids[:, None]).astype(jnp.int32), axis=1)
    cycles = jnp.arange(4, dtype=jnp.int32) * 16 + half * 64 + blk
    cycles = jnp.concatenate([cycles, 48 + blk.reshape(1)])
    block_position = (cycles - first_block[cycles]) * BLK_TOK
    positions = (block_position[:, None] + jnp.arange(BLK_TOK, dtype=jnp.int32)).reshape(640)
    tables = rotary_tables(positions)
    first_query = half * 64 + (blk // 4) * 16
    lo = lax.dynamic_slice(first_block, (first_query,), (16,)) - (first_query - 16)

    payload, normed_one, unit_one = qkv_call(
        ring, before, gain_one, shift_one, joint_w, bias, tables
    )
    out_w, payload = lax.optimization_barrier((joint_w, payload))
    own_rows = out_rows_call(place, out_w)
    near_rows = [send(own_rows, ("x",), t) for t in (1, 3)]
    blocks = after(exchange(payload.reshape(16, 5, 128, 128), BLK), near_rows)
    rest = lax.all_gather(after(rest, blocks), PLANE, axis=0).reshape(4, 2, 512, 3 * HID_PAD)
    att32, att16, lse = attend_call(lo, blocks)
    far_rows = send(after(own_rows, blocks), ("x",), 2)
    attended = exchange(att16, BLK).reshape(4, 2, 2, 128, 128)
    own_rows = [own_rows, near_rows[0], after(far_rows, attended), near_rows[1]]
    other_rows = [swap_core(rows) for rows in own_rows]
    middle, normed_two = project_call(
        place, exchange(attended, ("x",)), tokens, gain_two, shift_two, own_rows, other_rows
    )

    ring_two = exchange(normed_two, ("x",))
    active, grad_gu, ring_grad, ring_out = feed_forward_call(ring_two, ring_cot, rest)
    shared = plane_grad_call(core, with_other(ring_cot), with_other(active), HID_PAD, 2 * HID_PAD)
    came = after(exchange(ring_grad, ("x",)), shared)
    grad_middle, grad_branch, grad_gain_two, grad_shift_two, grad_att = project_back_call(
        place, came, middle, cotangent, gain_two, own_rows, other_rows
    )
    grad_att = exchange(grad_att, ("x",))
    ring_branch = lax.all_gather(after(grad_branch, grad_att), "x", axis=0)
    shared = plane_grad_call(core, with_other(ring_two), with_other(grad_gu), 2 * HID_PAD, 0, shared)
    grad_att = after(exchange(grad_att.reshape(16, 128, 128), BLK), shared)
    attended_pair = with_other(attended.transpose(2, 0, 3, 1, 4).reshape(2, 512, 256))

    mixed = lax.psum_scatter(
        after(ring_out, grad_att).reshape(512, D), "x", scatter_dimension=0, tiled=True
    )
    back = attend_back_call(lo, blocks, grad_att, att32, lse)
    branch_pair = with_other(after(ring_branch, back))
    shared = plane_grad_call(core, branch_pair, attended_pair, 256, 3 * HID_PAD, shared)
    back = exchange(back, BLK).reshape(4, 2, 2, 5, 128, 128)
    back, shared = lax.optimization_barrier((back, shared))
    shared = plane_sum(shared)
    mixed = (middle + after(mixed, back).astype(jnp.float32)).astype(jnp.bfloat16)
    halo_back = lax.ppermute(back[0, :, :, :2], ("yh",), [(1, 0)])
    back = after(back, mixed)
    grad_joint, grad_bias = turn_back_call(back, halo_back, tables)
    ring_one, grad_gain_one, grad_shift_one = normed_back_call(grad_joint, unit_one, joint_w)
    places = (chip_places(True), chip_places(False))
    parts = joint_grad_call(core, places, with_other(normed_one), with_other(grad_joint))
    pair_came = [first_send(parts[4 * j : 4 * j + 4], j == 0) for j in range(2)]

    norms = jnp.concatenate([grad_gain_one, grad_shift_one, grad_gain_two, grad_shift_two], 0)
    norms = norms.reshape(4, 2, 4, 16, 16).transpose(1, 2, 3, 0, 4).reshape(2, 4, 16, 64)
    biases = grad_bias.reshape(2, 2, 3, 8, 16).transpose(0, 1, 3, 2, 4).reshape(2, 1, 16, 48)
    plane = jnp.arange(4).reshape(1, 4, 1, 1) == lax.axis_index("x")
    biases = jnp.where(plane, biases, 0.0)
    sums = jnp.concatenate([norms, biases, jnp.zeros((2, 4, 16, 16), jnp.float32)], 3)
    sums = jnp.sum(exchange(sums.reshape(128, 128), AXES), 0)
    norms = sums[:64].reshape(4, 16)

    came = exchange(after(ring_one, norms, parts[0]), ("x",))
    input_grad = whole_call(
        input_back_kernel,
        jax.ShapeDtypeStruct((128, D), jnp.float32),
        came,
        tokens,
        grad_middle,
        gain_one,
    )
    pair_came[1] = after(pair_came[1], input_grad)
    pair_came = [second_send(first_sum(part, j == 0), j == 0) for j, part in enumerate(pair_came)]

    def shape(*dims):
        return jax.ShapeDtypeStruct(dims, jnp.float32)

    grad_gate, grad_up, grad_down, grad_out = whole_call(
        shared_end_kernel, [shape(HID, 128)] * 3 + [shape(256, 128)], after(shared, input_grad)
    )
    grad_qkv = whole_call(joint_end_kernel, shape(3, 128, 256), *pair_came[0], *pair_came[1])

    return (
        mixed,
        input_grad,
        norms[0],
        norms[1],
        grad_qkv.transpose(1, 0, 2),
        sums[64:112].reshape(3, 16),
        grad_out,
        norms[2],
        norms[3],
        grad_gate.T,
        grad_up.T,
        grad_down,
    )


def solution(mesh):
    whole = Mesh(mesh.devices.reshape(2, 4, 4, 2, 2), AXES)
    ulysses, blk = ("yh", "x"), BLK
    both = ulysses + blk
    placed = (
        P(both, None),
        P(both, None),
        P(),
        P(blk),
        P(blk),
        P(blk, None, ulysses),
        P(None, both),
        P(ulysses, blk),
        P(blk),
        P(blk),
        P(blk, ulysses),
        P(blk, ulysses),
        P(ulysses, blk),
    )
    return jax.shard_map(
        local,
        mesh=whole,
        in_specs=placed,
        out_specs=(
            P(both, None),
            P(both, None),
            P(both),
            P(both),
            P(blk, None, ulysses),
            P(None, both),
            P(ulysses, blk),
            P(both),
            P(both),
            P(blk, ulysses),
            P(blk, ulysses),
            P(ulysses, blk),
        ),
        check_vma=False,
    )
```

profile of v0, /device:TPU:4, one launch (start us, length us, event | category | flops | bytes accessed | tf_op | source)
XLA Modules:
  0.0 513.5 jit_solution(13243143102819995016)
XLA Ops:
  10.3 2.6 broadcast_in_dim.57
  12.9 4.9 all-to-all-start
  21.2 20.0 %all-to-all-done.x_ref = bf16[4,128,2048]{2,1,0:T(8,128)(2,1)S(1)} async-done(((bf16[4,128,2048]{2,1,0:T(8,128)(2,1)}), bf16[4,128,2048]{2,1,0:T(8,128)(2,1)S(1)}, u32[]{:S(2)}, u32[]{:S(2)}) %all-to-all-start) | async-done | bytes 2097184 | tf_op jit(solution)/shard_map/all_to_all | solution.py:43
  41.2 5.1 collective-permute-start
  46.4 31.7 %all-gather.9.cloned.1.call-done = bf16[4608,1024]{1,0:T(8,128)(2,1)} async-done(((bf16[144,1024]{1,0:T(8,128)(2,1)}), bf16[4608,1024]{1,0:T(8,128)(2,1)}) %all-gather.9.cloned.1.call-update) | async-done | bytes 9437200 | tf_op jit(solution)/shard_map/all_gather | solution.py:953
  81.2 14.7 %shard_map.221 = (bf16[4,2,2,5,128,128]{5,4,3,2,1,0:T(8,128)(2,1)}, bf16[4,128,2048]{2,1,0:T(8,128)(2,1)}, bf16[4,128,2048]{2,1,0:T(8,128)(2,1)}) custom-call(bf16[4,128,2048]{2,1,0:T(8,128)(2,1)} %copy-done.4, bf16[128,2048]{1,0:T(8,128)(2,1)} %copy-done.13, f32[1,2048]{1,0:T(1,128)} %bitcast.83, f32[1,2048]{1,0:T(1,128)} %bitcast.88, ...), custom_call_target="tpu_custom_call" | custom-call | flops 1 | bytes 1 | tf_op jit(solution)/shard_map/pallas_call | solution.py:214
  95.9 4.7 all-to-all-start.1
  101.2 3.7 shard_map.222.refs_0_
  107.0 2.2 shard_map.225
  109.1 22.0 %collective-permute-done.1.refs_1_ = bf16[8,128,512]{2,1,0:T(8,128)(2,1)} collective-permute-done((bf16[8,128,512]{2,1,0:T(8,128)(2,1)}, bf16[8,128,512]{2,1,0:T(8,128)(2,1)}, u32[]{:S(2)}, u32[]{:S(2)}) %collective-permute-start.1) | collective-permute-done | bytes 1048608 | tf_op jit(solution)/shard_map/ppermute | solution.py:55
  135.6 10.5 %shard_map.223 = (f32[16,128,128]{2,1,0:T(8,128)}, bf16[16,128,128]{2,1,0:T(8,128)(2,1)}, f32[8,1,512]{2,1,0:T(1,128)}) custom-call(s32[16]{0:T(128)} %dynamic-slice_subtract_fusion.lo_ref, bf16[16,5,128,128]{3,2,1,0:T(8,128)(2,1)} %copy-done), custom_call_target="tpu_custom_call" | custom-call | flops 1 | bytes 1 | tf_op jit(solution)/shard_map/pallas_call | solution.py:758
  146.1 9.3 %all-to-all-start.2 = ((bf16[16,128,128]{2,1,0:T(8,128)(2,1)}), bf16[16,128,128]{2,1,0:T(8,128)(2,1)}, u32[]{:S(2)}, u32[]{:S(2)}) async-start(bf16[16,128,128]{2,1,0:T(8,128)(2,1)} %get-tuple-element.80), calls=%async_computation.2 | async-start | bytes 1048576 | tf_op jit(solution)/shard_map/all_to_all | solution.py:43
  156.3 10.0 %all-to-all-done.2 = bf16[16,128,128]{2,1,0:T(8,128)(2,1)} async-done(((bf16[16,128,128]{2,1,0:T(8,128)(2,1)}), bf16[16,128,128]{2,1,0:T(8,128)(2,1)}, u32[]{:S(2)}, u32[]{:S(2)}) %all-to-all-start.2) | async-done | bytes 524320 | tf_op jit(solution)/shard_map/all_to_all | solution.py:43
  166.4 5.9 %all-to-all-start.3 = ((bf16[4,2,2,128,128]{4,3,2,1,0:T(8,128)(2,1)}), bf16[4,2,2,128,128]{4,3,2,1,0:T(8,128)(2,1)}, u32[]{:S(2)}, u32[]{:S(2)}) async-start(bf16[4,2,2,128,128]{4,3,2,1,0:T(8,128)(2,1)} %bitcast.21), calls=%async_computation.3 | async-start | bytes 1048576 | tf_op jit(solution)/shard_map/all_to_all | solution.py:43
  172.3 7.5 %all-to-all-done.3.att_ref = bf16[4,2,2,128,128]{4,3,2,1,0:T(8,128)(2,1)} async-done(((bf16[4,2,2,128,128]{4,3,2,1,0:T(8,128)(2,1)}), bf16[4,2,2,128,128]{4,3,2,1,0:T(8,128)(2,1)}, u32[]{:S(2)}, u32[]{:S(2)}) %all-to-all-start.3) | async-done | bytes 524320 | tf_op jit(solution)/shard_map/all_to_all | solution.py:43
  179.9 8.6 %shard_map.224 = (f32[128,2048]{1,0:T(8,128)}, bf16[4,128,2048]{2,1,0:T(8,128)(2,1)}) custom-call(s32[2]{0:T(128)} %pad_add_fusion.1.place_ref, bf16[4,2,2,128,128]{4,3,2,1,0:T(8,128)(2,1)} %all-to-all-done.3.att_ref, bf16[128,2048]{1,0:T(8,128)(2,1)} %tokens_ref.3, f32[1,2048]{1,0:T(1,128)} %bitcast.85, f32[1,2048]{1,0:T(1,128)} %bitcast.87, ...), custom_call_target="tpu_custom_call" | custom-call | flops 1 | bytes 1 | tf_op jit(solution)/shard_map/pallas_call | solution.py:359
  188.4 6.6 %all-to-all-start.4 = ((bf16[4,128,2048]{2,1,0:T(8,128)(2,1)}), bf16[4,128,2048]{2,1,0:T(8,128)(2,1)S(1)}, u32[]{:S(2)}, u32[]{:S(2)}) async-start(bf16[4,128,2048]{2,1,0:T(8,128)(2,1)} %get-tuple-element.84), calls=%async_computation.4 | async-start | bytes 4194304 | tf_op jit(solution)/shard_map/all_to_all | solution.py:43
  195.2 23.4 %all-to-all-done.4.x_ref.left_ref = bf16[4,128,2048]{2,1,0:T(8,128)(2,1)S(1)} async-done(((bf16[4,128,2048]{2,1,0:T(8,128)(2,1)}), bf16[4,128,2048]{2,1,0:T(8,128)(2,1)S(1)}, u32[]{:S(2)}, u32[]{:S(2)}) %all-to-all-start.4) | async-done | bytes 2097184 | tf_op jit(solution)/shard_map/all_to_all | solution.py:43
  219.9 30.4 %shard_map.226 = (bf16[2,512,768]{2,1,0:T(8,128)(2,1)}, bf16[2,512,1536]{2,1,0:T(8,128)(2,1)}, bf16[4,128,2048]{2,1,0:T(8,128)(2,1)}, bf16[4,128,2048]{2,1,0:T(8,128)(2,1)}) custom-call(bf16[4,128,2048]{2,1,0:T(8,128)(2,1)} %copy-done.1, bf16[4,128,2048]{2,1,0:T(8,128)(2,1)} %bitcast.70, bf16[4,2,512,2304]{3,2,1,0:T(8,128)(2,1)} %bitcast.63, ...), custom_call_target="tpu_custom_call" | custom-call | flops 1 | bytes 1 | tf_op jit(solution)/shard_map/pallas_call | solution.py:486
  250.3 6.6 %all-to-all-start.5 = ((bf16[4,128,2048]{2,1,0:T(8,128)(2,1)}), bf16[4,128,2048]{2,1,0:T(8,128)(2,1)S(1)}, u32[]{:S(2)}, u32[]{:S(2)}) async-start(bf16[4,128,2048]{2,1,0:T(8,128)(2,1)} %get-tuple-element.88), calls=%async_computation.5 | async-start | bytes 4194304 | tf_op jit(solution)/shard_map/all_to_all | solution.py:43
  256.9 9.4 %shard_map.227.refs_0_ = bf16[2,2,4,128,2560]{4,3,2,1,0:T(8,128)(2,1)} custom-call(s32[1]{0:T(128)} %bitcast.1.core_ref, bf16[4,128,2048]{2,1,0:T(8,128)(2,1)} %bitcast.71, bf16[4,128,2048]{2,1,0:T(8,128)(2,1)} %collective-permute-done.8.left_other_ref, bf16[2,512,768]{2,1,0:T(8,128)(2,1)} %get-tuple-element.89.right_ref, ...), custom_call_target="tpu_custom_call" | custom-call | flops 1 | bytes 1 | tf_op jit(solution)/shard_map/pallas_call | solution.py:527
  266.3 14.9 %all-to-all-done.5.came_ref = bf16[4,128,2048]{2,1,0:T(8,128)(2,1)S(1)} async-done(((bf16[4,128,2048]{2,1,0:T(8,128)(2,1)}), bf16[4,128,2048]{2,1,0:T(8,128)(2,1)S(1)}, u32[]{:S(2)}, u32[]{:S(2)}) %all-to-all-start.5) | async-done | bytes 2097184 | tf_op jit(solution)/shard_map/all_to_all | solution.py:43
  282.5 9.1 %shard_map.228 = (f32[128,2048]{1,0:T(8,128)}, bf16[128,2048]{1,0:T(8,128)(2,1)}, f32[1,2048]{1,0:T(1,128)}, f32[1,2048]{1,0:T(1,128)}, bf16[4,2,2,128,128]{4,3,2,1,0:T(8,128)(2,1)}) custom-call(s32[2]{0:T(128)} %pad_add_fusion.1.place_ref, bf16[4,128,2048]{2,1,0:T(8,128)(2,1)} %copy-done.6, f32[128,2048]{1,0:T(8,128)} %get-tuple-element.83.middle_ref, ...), custom_call_target="tpu_custom_call" | custom-call | flops 1 | bytes 1 | tf_op jit(solution)/shard_map/pallas_call | solution.py:420
  291.7 7.1 %all-to-all-start.6 = ((bf16[4,2,2,128,128]{4,3,2,1,0:T(8,128)(2,1)}), bf16[4,2,2,128,128]{4,3,2,1,0:T(8,128)(2,1)}, u32[]{:S(2)}, u32[]{:S(2)}) async-start(bf16[4,2,2,128,128]{4,3,2,1,0:T(8,128)(2,1)} %get-tuple-element.91), calls=%async_computation.6 | async-start | bytes 1048576 | tf_op jit(solution)/shard_map/all_to_all | solution.py:43
  299.1 6.5 %all-to-all-done.6 = bf16[4,2,2,128,128]{4,3,2,1,0:T(8,128)(2,1)} async-done(((bf16[4,2,2,128,128]{4,3,2,1,0:T(8,128)(2,1)}), bf16[4,2,2,128,128]{4,3,2,1,0:T(8,128)(2,1)}, u32[]{:S(2)}, u32[]{:S(2)}) %all-to-all-start.6) | async-done | bytes 524320 | tf_op jit(solution)/shard_map/all_to_all | solution.py:43
  305.6 3.6 all-to-all-start.7
  309.9 15.3 %shard_map.229.refs_0_ = bf16[2,2,4,128,2560]{4,3,2,1,0:T(8,128)(2,1)} custom-call(s32[1]{0:T(128)} %bitcast.1.core_ref, bf16[4,128,2048]{2,1,0:T(8,128)(2,1)} %copy-done.1, bf16[4,128,2048]{2,1,0:T(8,128)(2,1)} %collective-permute-done.10.left_other_ref, bf16[2,512,1536]{2,1,0:T(8,128)(2,1)} %get-tuple-element.92.right_ref, ...), custom_call_target="tpu_custom_call", output_to_operand_aliasing={{}: (5, {})} | custom-call | flops 1 | bytes 1 | tf_op jit(solution)/shard_map/pallas_call | solution.py:527
  326.1 13.5 %shard_map.230 = bf16[16,5,128,128]{3,2,1,0:T(8,128)(2,1)} custom-call(s32[16]{0:T(128)} %dynamic-slice_subtract_fusion.lo_ref, bf16[16,5,128,128]{3,2,1,0:T(8,128)(2,1)} %copy-done, bf16[16,128,128]{2,1,0:T(8,128)(2,1)} %copy-done.11, f32[16,128,128]{2,1,0:T(8,128)} %get-tuple-element.95.o32_ref, f32[8,1,512]{2,1,0:T(1,128)} %get-tuple-element.96.lse_ref), custom_call_target="tpu_custom_call" | custom-call | flops 1 | bytes 1 | tf_op jit(solution)/shard_map/pallas_call | solution.py:822
  339.5 11.3 %all-to-all-start.8 = ((bf16[16,5,128,128]{3,2,1,0:T(8,128)(2,1)}), bf16[16,5,128,128]{3,2,1,0:T(8,128)(2,1)S(1)}, u32[]{:S(2)}, u32[]{:S(2)}) async-start(bf16[16,5,128,128]{3,2,1,0:T(8,128)(2,1)} %shard_map.230), calls=%async_computation.9 | async-start | bytes 5242880 | tf_op jit(solution)/shard_map/all_to_all | solution.py:43
  351.4 2.4 copy.49
  357.9 5.4 %shard_map.231 = bf16[2,2,4,128,2560]{4,3,2,1,0:T(8,128)(2,1)} custom-call(s32[1]{0:T(128)} %bitcast.1.core_ref, bf16[4,128,2048]{2,1,0:T(8,128)(2,1)} %bitcast.74, bf16[4,128,2048]{2,1,0:T(8,128)(2,1)} %collective-permute-done.12.left_other_ref, bf16[2,512,256]{2,1,0:T(8,128)(2,1)} %copy-done.10, ...), custom_call_target="tpu_custom_call", output_to_operand_aliasing={{}: (5, {})} | custom-call | flops 1 | bytes 1 | tf_op jit(solution)/shard_map/pallas_call | solution.py:527
  363.3 21.0 %all-to-all-done.8 = bf16[16,5,128,128]{3,2,1,0:T(8,128)(2,1)S(1)} async-done(((bf16[16,5,128,128]{3,2,1,0:T(8,128)(2,1)}), bf16[16,5,128,128]{3,2,1,0:T(8,128)(2,1)S(1)}, u32[]{:S(2)}, u32[]{:S(2)}) %all-to-all-start.8) | async-done | bytes 2621472 | tf_op jit(solution)/shard_map/all_to_all | solution.py:43
  387.2 2.3 add_convert_fusion
  389.5 13.6 %collective-permute-done.14.halo_ref = bf16[2,2,2,128,128]{4,3,2,1,0:T(8,128)(2,1)S(1)} collective-permute-done((bf16[2,2,2,128,128]{4,3,2,1,0:T(8,128)(2,1)S(1)}, bf16[2,2,2,128,128]{4,3,2,1,0:T(8,128)(2,1)S(1)}, u32[]{:S(2)}, u32[]{:S(2)}) %collective-permute-start.14) | collective-permute-done | bytes 262176 | tf_op jit(solution)/shard_map/ppermute | solution.py:1014
  403.8 3.7 shard_map.232
  407.8 8.7 %shard_map.233 = (bf16[4,128,2048]{2,1,0:T(8,128)(2,1)}, f32[1,2048]{1,0:T(1,128)}, f32[1,2048]{1,0:T(1,128)}) custom-call(bf16[2,512,768]{2,1,0:T(8,128)(2,1)} %get-tuple-element.103.g_ref.right_ref, bf16[4,128,2048]{2,1,0:T(8,128)(2,1)} %get-tuple-element.104.unit_ref, bf16[4,2,4,144,1024]{4,3,2,1,0:T(8,128)(2,1)} %bitcast.62), custom_call_target="tpu_custom_call" | custom-call | flops 1 | bytes 1 | tf_op jit(solution)/shard_map/pallas_call | solution.py:913
  419.0 9.4 %all-to-all-start.10 = ((f32[128,1,128]{2,1,0:T(1,128)}), f32[128,1,128]{2,1,0:T(1,128)S(1)}, u32[]{:S(2)}, u32[]{:S(2)}) async-start(f32[128,1,128]{2,1,0:T(1,128)} %copy.53), calls=%async_computation.11 | async-start | bytes 131072 | tf_op jit(solution)/shard_map/all_to_all | solution.py:43
  430.2 10.1 %shard_map.234 = (bf16[4,128,384]{2,1,0:T(8,128)(2,1)}, bf16[4,128,384]{2,1,0:T(8,128)(2,1)}, bf16[4,128,384]{2,1,0:T(8,128)(2,1)}, bf16[4,128,384]{2,1,0:T(8,12...) custom-call(s32[1]{0:T(128)} %bitcast.1.core_ref, ...), custom_call_target="tpu_custom_call" | custom-call | flops 1 | bytes 1 | tf_op jit(solution)/shard_map/pallas_call | solution.py:613
  440.3 4.9 all-to-all-start.9
  453.6 16.8 %collective-permute-done.17.b_ref = bf16[4,128,384]{2,1,0:T(8,128)(2,1)S(1)} collective-permute-done((bf16[4,128,384]{2,1,0:T(8,128)(2,1)S(1)}, bf16[4,128,384]{2,1,0:T(8,128)(2,1)S(1)}, u32[]{:S(2)}, u32[]{:S(2)}) %collective-permute-start.17) | collective-permute-done | bytes 393248 | tf_op jit(solution)/shard_map/ppermute | solution.py:55
  471.1 2.2 shard_map.236
  473.5 3.3 collective-permute-start.21
  478.2 4.0 shard_map.235
  483.7 5.0 collective-permute-done.25.d_ref
  489.4 2.2 shard_map.237
  491.7 3.2 collective-permute-start.27
  498.5 2.8 collective-permute-done.28.refs_7_
  503.9 2.3 shard_map.239
  (186 shorter events, 54.2 us)
Async XLA Ops:
  7.2 70.9 %all-gather.9.cloned.1.call-start = ((), (), s32[]{:S(2)}) async-start(), calls=%async_computation.15 | async-start | bytes 9732096 | tf_op jit(solution)/shard_map/all_gather | solution.py:953
  12.9 28.3 %all-to-all-start = ((bf16[4,128,2048]{2,1,0:T(8,128)(2,1)}), bf16[4,128,2048]{2,1,0:T(8,128)(2,1)S(1)}, u32[]{:S(2)}, u32[]{:S(2)}) async-start(bf16[4,128,2048]{2,1,0:T(8,128)(2,1)} %broadcast_in_dim.57), calls=%async_computation | async-start | bytes 4194304 | tf_op jit(solution)/shard_map/all_to_all | solution.py:43
  17.8 177.2 %all-gather.11.cloned.1.call-start = ((), (), s32[]{:S(2)}) async-start(), calls=%async_computation.16 | async-start | bytes 2621440 | tf_op jit(solution)/shard_map/all_gather | solution.py:957
  41.2 39.2 %copy-start.4 = (bf16[4,128,2048]{2,1,0:T(8,128)(2,1)}, bf16[4,128,2048]{2,1,0:T(8,128)(2,1)S(1)}, u32[]{:S(2)}) copy-start(bf16[4,128,2048]{2,1,0:T(8,128)(2,1)S(1)} %all-to-all-done.x_ref) | copy-start | bytes 6291460
  41.2 39.2 %collective-permute-start = (bf16[128,2048]{1,0:T(8,128)(2,1)S(1)}, bf16[128,2048]{1,0:T(8,128)(2,1)S(1)}, u32[]{:S(2)}, u32[]{:S(2)}) collective-permute-start(bf16[128,2048]{1,0:T(8,128)(2,1)S(1)} %slice_bitcast_fusion), channel_id=1, source_target_pairs={{0,64},{1,65},{2,66},{3,67},{4,68},{5,69},{6,70},{7,71},{8,72},{9,... | collective-permute-start | bytes 1572872 | tf_op jit(solution)/shard_map/ppermute | solution.py:956
  95.9 38.2 %all-to-all-start.1 = ((bf16[16,5,128,128]{3,2,1,0:T(8,128)(2,1)}), bf16[16,5,128,128]{3,2,1,0:T(8,128)(2,1)S(1)}, u32[]{:S(2)}, u32[]{:S(2)}) async-start(bf16[16,5,128,128]{3,2,1,0:T(8,128)(2,1)} %bitcast.72), calls=%async_computation.1 | async-start | bytes 5242880 | tf_op jit(solution)/shard_map/all_to_all | solution.py:43
  100.6 118.0 %all-gather.13.cloned.1.call-start = ((), (), s32[]{:S(2)}) async-start(), calls=%async_computation.17 | async-start | bytes 19464192 | tf_op jit(solution)/shard_map/all_gather | solution.py:981
  104.9 26.2 %collective-permute-start.1 = (bf16[8,128,512]{2,1,0:T(8,128)(2,1)}, bf16[8,128,512]{2,1,0:T(8,128)(2,1)}, u32[]{:S(2)}, u32[]{:S(2)}) collective-permute-start(bf16[8,128,512]{2,1,0:T(8,128)(2,1)} %shard_map.222.refs_0_), channel_id=1, source_target_pairs={{0,16},{16,32},{32,48},{48,0},{1,17},{17,33},{33,49},{49,1},{2,18}... | collective-permute-start | bytes 3145736 | tf_op jit(solution)/shard_map/ppermute | solution.py:55
  106.1 26.0 %collective-permute-start.2 = (bf16[8,128,512]{2,1,0:T(8,128)(2,1)}, bf16[8,128,512]{2,1,0:T(8,128)(2,1)}, u32[]{:S(2)}, u32[]{:S(2)}) collective-permute-start(bf16[8,128,512]{2,1,0:T(8,128)(2,1)} %shard_map.222.refs_0_), channel_id=1, source_target_pairs={{0,48},{16,0},{32,16},{48,32},{1,49},{17,1},{33,17},{49,33},{2,50}... | collective-permute-start | bytes 3145736 | tf_op jit(solution)/shard_map/ppermute | solution.py:55
  134.1 32.3 %collective-permute-start.3 = (bf16[8,128,512]{2,1,0:T(8,128)(2,1)}, bf16[8,128,512]{2,1,0:T(8,128)(2,1)}, u32[]{:S(2)}, u32[]{:S(2)}) collective-permute-start(bf16[8,128,512]{2,1,0:T(8,128)(2,1)} %shard_map.222.refs_0_), channel_id=1, source_target_pairs={{0,32},{16,48},{32,0},{48,16},{1,33},{17,49},{33,1},{49,17},{2,34}... | collective-permute-start | bytes 3145736 | tf_op jit(solution)/shard_map/ppermute | solution.py:55
  146.1 20.3 %all-to-all-start.2 = ((bf16[16,128,128]{2,1,0:T(8,128)(2,1)}), bf16[16,128,128]{2,1,0:T(8,128)(2,1)}, u32[]{:S(2)}, u32[]{:S(2)}) async-start(bf16[16,128,128]{2,1,0:T(8,128)(2,1)} %get-tuple-element.80), calls=%async_computation.2 | async-start | bytes 1048576 | tf_op jit(solution)/shard_map/all_to_all | solution.py:43
  155.5 16.8 %collective-permute-start.4 = (bf16[8,128,512]{2,1,0:T(8,128)(2,1)}, bf16[8,128,512]{2,1,0:T(8,128)(2,1)S(1)}, u32[]{:S(2)}, u32[]{:S(2)}) collective-permute-start(bf16[8,128,512]{2,1,0:T(8,128)(2,1)} %shard_map.222.refs_0_), channel_id=1, source_target_pairs={{0,1},{1,0},{2,3},{3,2},{4,5},{5,4},{6,7},{7,6},{8,9},{9,8},{10,11... | collective-permute-start | bytes 3145736 | tf_op jit(solution)/shard_map/ppermute | solution.py:39
  155.8 16.5 %collective-permute-start.5 = (bf16[8,128,512]{2,1,0:T(8,128)(2,1)}, bf16[8,128,512]{2,1,0:T(8,128)(2,1)S(1)}, u32[]{:S(2)}, u32[]{:S(2)}) collective-permute-start(bf16[8,128,512]{2,1,0:T(8,128)(2,1)} %collective-permute-done.1.refs_1_), channel_id=1, source_target_pairs={{0,1},{1,0},{2,3},{3,2},{4,5},{5,4},{6,7},{7,6},{8,9},{9,8},{10,11... | collective-permute-start | bytes 3145736 | tf_op jit(solution)/shard_map/ppermute | solution.py:39
  156.1 16.2 %collective-permute-start.7 = (bf16[8,128,512]{2,1,0:T(8,128)(2,1)}, bf16[8,128,512]{2,1,0:T(8,128)(2,1)S(1)}, u32[]{:S(2)}, u32[]{:S(2)}) collective-permute-start(bf16[8,128,512]{2,1,0:T(8,128)(2,1)} %collective-permute-done.2.refs_3_), channel_id=1, source_target_pairs={{0,1},{1,0},{2,3},{3,2},{4,5},{5,4},{6,7},{7,6},{8,9},{9,8},{10,11... | collective-permute-start | bytes 3145736 | tf_op jit(solution)/shard_map/ppermute | solution.py:39
  166.4 13.5 %collective-permute-start.6 = (bf16[8,128,512]{2,1,0:T(8,128)(2,1)}, bf16[8,128,512]{2,1,0:T(8,128)(2,1)}, u32[]{:S(2)}, u32[]{:S(2)}) collective-permute-start(bf16[8,128,512]{2,1,0:T(8,128)(2,1)} %collective-permute-done.3.refs_2_), channel_id=1, source_target_pairs={{0,1},{1,0},{2,3},{3,2},{4,5},{5,4},{6,7},{7,6},{8,9},{9,8},{10,11... | collective-permute-start | bytes 3145736 | tf_op jit(solution)/shard_map/ppermute | solution.py:39
  166.4 13.4 %all-to-all-start.3 = ((bf16[4,2,2,128,128]{4,3,2,1,0:T(8,128)(2,1)}), bf16[4,2,2,128,128]{4,3,2,1,0:T(8,128)(2,1)}, u32[]{:S(2)}, u32[]{:S(2)}) async-start(bf16[4,2,2,128,128]{4,3,2,1,0:T(8,128)(2,1)} %bitcast.21), calls=%async_computation.3 | async-start | bytes 1048576 | tf_op jit(solution)/shard_map/all_to_all | solution.py:43
  188.4 30.1 %all-to-all-start.4 = ((bf16[4,128,2048]{2,1,0:T(8,128)(2,1)}), bf16[4,128,2048]{2,1,0:T(8,128)(2,1)S(1)}, u32[]{:S(2)}, u32[]{:S(2)}) async-start(bf16[4,128,2048]{2,1,0:T(8,128)(2,1)} %get-tuple-element.84), calls=%async_computation.4 | async-start | bytes 4194304 | tf_op jit(solution)/shard_map/all_to_all | solution.py:43
  195.0 61.9 %collective-permute-start.8 = (bf16[4,128,2048]{2,1,0:T(8,128)(2,1)}, bf16[4,128,2048]{2,1,0:T(8,128)(2,1)}, u32[]{:S(2)}, u32[]{:S(2)}) collective-permute-start(bf16[4,128,2048]{2,1,0:T(8,128)(2,1)} %bitcast.69), channel_id=1, source_target_pairs={{0,1},{1,0},{2,3},{3,2},{4,5},{5,4},{6,7},{7,6},{8,9},{9,8},{10,11... | collective-permute-start | bytes 6291464 | tf_op jit(solution)/shard_map/ppermute | solution.py:39
  250.2 6.7 %collective-permute-start.9 = (bf16[2,512,768]{2,1,0:T(8,128)(2,1)}, bf16[2,512,768]{2,1,0:T(8,128)(2,1)}, u32[]{:S(2)}, u32[]{:S(2)}) collective-permute-start(bf16[2,512,768]{2,1,0:T(8,128)(2,1)} %get-tuple-element.89.right_ref), channel_id=1, source_target_pairs={{0,1},{1,0},{2,3},{3,2},{4,5},{5,4},{6,7},{7,6},{8,9},{9,8},{10,11... | collective-permute-start | bytes 4718600 | tf_op jit(solution)/shard_map/ppermute | solution.py:39
  250.3 30.8 %all-to-all-start.5 = ((bf16[4,128,2048]{2,1,0:T(8,128)(2,1)}), bf16[4,128,2048]{2,1,0:T(8,128)(2,1)S(1)}, u32[]{:S(2)}, u32[]{:S(2)}) async-start(bf16[4,128,2048]{2,1,0:T(8,128)(2,1)} %get-tuple-element.88), calls=%async_computation.5 | async-start | bytes 4194304 | tf_op jit(solution)/shard_map/all_to_all | solution.py:43
  282.5 23.0 %copy-start.2 = (bf16[4,128,2048]{2,1,0:T(8,128)(2,1)S(1)}, bf16[4,128,2048]{2,1,0:T(8,128)(2,1)}, u32[]{:S(2)}) copy-start(bf16[4,128,2048]{2,1,0:T(8,128)(2,1)} %copy-done.1) | copy-start | bytes 6291460
  291.7 13.8 %all-to-all-start.6 = ((bf16[4,2,2,128,128]{4,3,2,1,0:T(8,128)(2,1)}), bf16[4,2,2,128,128]{4,3,2,1,0:T(8,128)(2,1)}, u32[]{:S(2)}, u32[]{:S(2)}) async-start(bf16[4,2,2,128,128]{4,3,2,1,0:T(8,128)(2,1)} %get-tuple-element.91), calls=%async_computation.6 | async-start | bytes 1048576 | tf_op jit(solution)/shard_map/all_to_all | solution.py:43
  298.7 52.1 %all-gather.15.cloned.1.call-start = ((), (), s32[]{:S(2)}) async-start(), calls=%async_computation.18 | async-start | bytes 2621440 | tf_op jit(solution)/shard_map/all_gather | solution.py:999
  299.0 11.0 %collective-permute-start.11 = (bf16[2,512,1536]{2,1,0:T(8,128)(2,1)}, bf16[2,512,1536]{2,1,0:T(8,128)(2,1)}, u32[]{:S(2)}, u32[]{:S(2)}) collective-permute-start(bf16[2,512,1536]{2,1,0:T(8,128)(2,1)} %get-tuple-element.92.right_ref), channel_id=1, source_target_pairs={{0,1},{1,0},{2,3},{3,2},{4,5},{5,4},{6,7},{7,6},{8,9},{9,8},{10,11... | collective-permute-start | bytes 9437192 | tf_op jit(solution)/shard_map/ppermute | solution.py:39
  305.5 4.4 collective-permute-start.10
  305.6 19.6 %all-to-all-start.7 = ((bf16[16,128,128]{2,1,0:T(8,128)(2,1)}), bf16[16,128,128]{2,1,0:T(8,128)(2,1)S(1)}, u32[]{:S(2)}, u32[]{:S(2)}) async-start(bf16[16,128,128]{2,1,0:T(8,128)(2,1)} %bitcast.28), calls=%async_computation.7 | async-start | bytes 1048576 | tf_op jit(solution)/shard_map/all_to_all | solution.py:43
  309.2 78.0 %reduce-scatter.3.cloned.1.call-start = ((), (), s32[]{:S(2)}) async-start(), calls=%async_computation.13 | async-start | bytes 2621440 | tf_op jit(solution)/shard_map/reduce_scatter | solution.py:1004
  339.5 44.8 %all-to-all-start.8 = ((bf16[16,5,128,128]{3,2,1,0:T(8,128)(2,1)}), bf16[16,5,128,128]{3,2,1,0:T(8,128)(2,1)S(1)}, u32[]{:S(2)}, u32[]{:S(2)}) async-start(bf16[16,5,128,128]{3,2,1,0:T(8,128)(2,1)} %shard_map.230), calls=%async_computation.9 | async-start | bytes 5242880 | tf_op jit(solution)/shard_map/all_to_all | solution.py:43
  350.8 153.1 %reduce-scatter.5.cloned.1.call-start = ((), (), s32[]{:S(2)}) async-start(), calls=%async_computation.14 | async-start | bytes 11141120 | tf_op jit(solution)/shard_map/reduce_scatter | solution.py:656
  350.9 6.3 %collective-permute-start.12 = (bf16[4,128,2048]{2,1,0:T(8,128)(2,1)}, bf16[4,128,2048]{2,1,0:T(8,128)(2,1)}, u32[]{:S(2)}, u32[]{:S(2)}) collective-permute-start(bf16[4,128,2048]{2,1,0:T(8,128)(2,1)} %bitcast.73), channel_id=1, source_target_pairs={{0,1},{1,0},{2,3},{3,2},{4,5},{5,4},{6,7},{7,6},{8,9},{9,8},{10,11... | collective-permute-start | bytes 6291464 | tf_op jit(solution)/shard_map/ppermute | solution.py:39
  355.2 2.0 collective-permute-start.13
  384.4 44.6 %collective-permute-start.15 = (bf16[4,128,2048]{2,1,0:T(8,128)(2,1)}, bf16[4,128,2048]{2,1,0:T(8,128)(2,1)}, u32[]{:S(2)}, u32[]{:S(2)}) collective-permute-start(bf16[4,128,2048]{2,1,0:T(8,128)(2,1)} %get-tuple-element.106.left_ref), channel_id=1, source_target_pairs={{0,1},{1,0},{2,3},{3,2},{4,5},{5,4},{6,7},{7,6},{8,9},{9,8},{10,11... | collective-permute-start | bytes 6291464 | tf_op jit(solution)/shard_map/ppermute | solution.py:39
  385.9 17.2 %collective-permute-start.14 = (bf16[2,2,2,128,128]{4,3,2,1,0:T(8,128)(2,1)S(1)}, bf16[2,2,2,128,128]{4,3,2,1,0:T(8,128)(2,1)S(1)}, u32[]{:S(2)}, u32[]{:S(2)}) collective-permute-start(bf16[2,2,2,128,128]{4,3,2,1,0:T(8,128)(2,1)S(1)} %slice_bitcast_fusion.1), channel_id=1, source_target_pairs={{64,0},{65,1},{66,2},{67,3},{68,4},{69,5},{70,6},{71,7},{72,8},{73... | collective-permute-start | bytes 786440 | tf_op jit(solution)/shard_map/ppermute | solution.py:1014
  407.5 21.5 %collective-permute-start.16 = (bf16[2,512,768]{2,1,0:T(8,128)(2,1)}, bf16[2,512,768]{2,1,0:T(8,128)(2,1)S(1)}, u32[]{:S(2)}, u32[]{:S(2)}) collective-permute-start(bf16[2,512,768]{2,1,0:T(8,128)(2,1)} %get-tuple-element.103.g_ref.right_ref), channel_id=1, source_target_pairs={{0,1},{1,0},{2,3},{3,2},{4,5},{5,4},{6,7},{7,6},{8,9},{9,8},{10,11... | collective-permute-start | bytes 4718600 | tf_op jit(solution)/shard_map/ppermute | solution.py:39
  419.0 21.3 %all-to-all-start.10 = ((f32[128,1,128]{2,1,0:T(1,128)}), f32[128,1,128]{2,1,0:T(1,128)S(1)}, u32[]{:S(2)}, u32[]{:S(2)}) async-start(f32[128,1,128]{2,1,0:T(1,128)} %copy.53), calls=%async_computation.11 | async-start | bytes 131072 | tf_op jit(solution)/shard_map/all_to_all | solution.py:43
  440.3 36.5 %all-to-all-start.9 = ((bf16[4,128,2048]{2,1,0:T(8,128)(2,1)}), bf16[4,128,2048]{2,1,0:T(8,128)(2,1)S(1)}, u32[]{:S(2)}, u32[]{:S(2)}) async-start(bf16[4,128,2048]{2,1,0:T(8,128)(2,1)} %get-tuple-element.108), calls=%async_computation.10 | async-start | bytes 4194304 | tf_op jit(solution)/shard_map/all_to_all | solution.py:43
  445.3 25.1 %collective-permute-start.17 = (bf16[4,128,384]{2,1,0:T(8,128)(2,1)S(1)}, bf16[4,128,384]{2,1,0:T(8,128)(2,1)S(1)}, u32[]{:S(2)}, u32[]{:S(2)}) collective-permute-start(bf16[4,128,384]{2,1,0:T(8,128)(2,1)S(1)} %copy-done.29), channel_id=1, source_target_pairs={{0,2},{2,64},{64,66},{66,0},{1,3},{3,65},{65,67},{67,1},{4,6},{6,6... | collective-permute-start | bytes 1179656 | tf_op jit(solution)/shard_map/ppermute | solution.py:55
  446.7 23.7 %collective-permute-start.18 = (bf16[4,128,384]{2,1,0:T(8,128)(2,1)}, bf16[4,128,384]{2,1,0:T(8,128)(2,1)}, u32[]{:S(2)}, u32[]{:S(2)}) collective-permute-start(bf16[4,128,384]{2,1,0:T(8,128)(2,1)} %get-tuple-element.116), channel_id=1, source_target_pairs={{0,66},{2,0},{64,2},{66,64},{1,67},{3,1},{65,3},{67,65},{4,70},{6,... | collective-permute-start | bytes 1179656 | tf_op jit(solution)/shard_map/ppermute | solution.py:55
  448.5 21.9 %collective-permute-start.19 = (bf16[4,128,384]{2,1,0:T(8,128)(2,1)}, bf16[4,128,384]{2,1,0:T(8,128)(2,1)}, u32[]{:S(2)}, u32[]{:S(2)}) collective-permute-start(bf16[4,128,384]{2,1,0:T(8,128)(2,1)} %get-tuple-element.117), channel_id=1, source_target_pairs={{0,64},{2,66},{64,0},{66,2},{1,65},{3,67},{65,1},{67,3},{4,68},{6,... | collective-permute-start | bytes 1179656 | tf_op jit(solution)/shard_map/ppermute | solution.py:55
  450.2 31.9 %collective-permute-start.23 = (bf16[4,128,384]{2,1,0:T(8,128)(2,1)}, bf16[4,128,384]{2,1,0:T(8,128)(2,1)S(1)}, u32[]{:S(2)}, u32[]{:S(2)}) collective-permute-start(bf16[4,128,384]{2,1,0:T(8,128)(2,1)} %get-tuple-element.123), channel_id=1, source_target_pairs={{0,4},{4,8},{8,12},{12,0},{1,5},{5,9},{9,13},{13,1},{2,6},{6,10},{... | collective-permute-start | bytes 1179656 | tf_op jit(solution)/shard_map/ppermute | solution.py:55
  451.8 31.9 %collective-permute-start.24 = (bf16[4,128,384]{2,1,0:T(8,128)(2,1)}, bf16[4,128,384]{2,1,0:T(8,128)(2,1)S(1)}, u32[]{:S(2)}, u32[]{:S(2)}) collective-permute-start(bf16[4,128,384]{2,1,0:T(8,128)(2,1)} %get-tuple-element.124), channel_id=1, source_target_pairs={{0,12},{4,0},{8,4},{12,8},{1,13},{5,1},{9,5},{13,9},{2,14},{6,2},{... | collective-permute-start | bytes 1179656 | tf_op jit(solution)/shard_map/ppermute | solution.py:55
  470.4 18.3 %collective-permute-start.25 = (bf16[4,128,384]{2,1,0:T(8,128)(2,1)}, bf16[4,128,384]{2,1,0:T(8,128)(2,1)S(1)}, u32[]{:S(2)}, u32[]{:S(2)}) collective-permute-start(bf16[4,128,384]{2,1,0:T(8,128)(2,1)} %get-tuple-element.125), channel_id=1, source_target_pairs={{0,8},{4,12},{8,0},{12,4},{1,9},{5,13},{9,1},{13,5},{2,10},{6,14},... | collective-permute-start | bytes 1179656 | tf_op jit(solution)/shard_map/ppermute | solution.py:55
  473.3 21.6 %collective-permute-start.20 = (bf16[128,384]{1,0:T(8,128)(2,1)}, bf16[128,384]{1,0:T(8,128)(2,1)S(1)}, u32[]{:S(2)}, u32[]{:S(2)}) collective-permute-start(bf16[128,384]{1,0:T(8,128)(2,1)} %get-tuple-element.119), channel_id=1, source_target_pairs={{0,4},{4,8},{8,12},{12,0},{1,5},{5,9},{9,13},{13,1},{2,6},{6,10},{... | collective-permute-start | bytes 294920 | tf_op jit(solution)/shard_map/ppermute | solution.py:55
  473.5 22.8 %collective-permute-start.21 = (bf16[128,384]{1,0:T(8,128)(2,1)}, bf16[128,384]{1,0:T(8,128)(2,1)S(1)}, u32[]{:S(2)}, u32[]{:S(2)}) collective-permute-start(bf16[128,384]{1,0:T(8,128)(2,1)} %get-tuple-element.120), channel_id=1, source_target_pairs={{0,12},{4,0},{8,4},{12,8},{1,13},{5,1},{9,5},{13,9},{2,14},{6,2},{... | collective-permute-start | bytes 294920 | tf_op jit(solution)/shard_map/ppermute | solution.py:55
  482.1 14.1 %collective-permute-start.22 = (bf16[128,384]{1,0:T(8,128)(2,1)}, bf16[128,384]{1,0:T(8,128)(2,1)S(1)}, u32[]{:S(2)}, u32[]{:S(2)}) collective-permute-start(bf16[128,384]{1,0:T(8,128)(2,1)} %get-tuple-element.121), channel_id=1, source_target_pairs={{0,8},{4,12},{8,0},{12,4},{1,9},{5,13},{9,1},{13,5},{2,10},{6,14},... | collective-permute-start | bytes 294920 | tf_op jit(solution)/shard_map/ppermute | solution.py:55
  491.7 6.0 %collective-permute-start.26 = (bf16[128,384]{1,0:T(8,128)(2,1)}, bf16[128,384]{1,0:T(8,128)(2,1)S(1)}, u32[]{:S(2)}, u32[]{:S(2)}) collective-permute-start(bf16[128,384]{1,0:T(8,128)(2,1)} %get-tuple-element.131), channel_id=1, source_target_pairs={{0,2},{2,64},{64,66},{66,0},{1,3},{3,65},{65,67},{67,1},{4,6},{6,6... | collective-permute-start | bytes 294920 | tf_op jit(solution)/shard_map/ppermute | solution.py:55
  491.7 6.8 %collective-permute-start.27 = (bf16[128,384]{1,0:T(8,128)(2,1)}, bf16[128,384]{1,0:T(8,128)(2,1)S(1)}, u32[]{:S(2)}, u32[]{:S(2)}) collective-permute-start(bf16[128,384]{1,0:T(8,128)(2,1)} %get-tuple-element.132), channel_id=1, source_target_pairs={{0,66},{2,0},{64,2},{66,64},{1,67},{3,1},{65,3},{67,65},{4,70},{6,... | collective-permute-start | bytes 294920 | tf_op jit(solution)/shard_map/ppermute | solution.py:55
  494.9 6.3 %collective-permute-start.28 = (bf16[128,384]{1,0:T(8,128)(2,1)}, bf16[128,384]{1,0:T(8,128)(2,1)S(1)}, u32[]{:S(2)}, u32[]{:S(2)}) collective-permute-start(bf16[128,384]{1,0:T(8,128)(2,1)} %get-tuple-element.133), channel_id=1, source_target_pairs={{0,64},{2,66},{64,0},{66,2},{1,65},{3,67},{65,1},{67,3},{4,68},{6,... | collective-permute-start | bytes 294920 | tf_op jit(solution)/shard_map/ppermute | solution.py:55
  (29 other events, 109.4 us)
Sparse Core Ops, SparseCore 0:
  10.8 67.2 all-gather.8
  79.8 30.3 all-gather.10
  134.2 80.3 all-gather.12
  305.7 32.9 all-gather.14
  340.9 29.3 reduce-scatter.2
  384.5 106.4 reduce-scatter.4
where the time goes:
time: 523 us; the launch traced here: 513 us
  waiting for transfers between devices  203 us (39%)
  Pallas kernels  160 us (31%)
  starting transfers between devices  102 us (20%)
  local copies, waits for them, and re-layouts  23.6 us (5%)
  between operations  15.1 us (3%)
  other arithmetic  10 us (2%)
    all_to_all x11, waiting for transfers between devices, exchange(): return lax.all_to_all(parts, axes, 0, 0, tiled=True)  105 us
    all_to_all x11, starting transfers between devices, exchange(): return lax.all_to_all(parts, axes, 0, 0, tiled=True)  74.3 us
    ppermute x15, waiting for transfers between devices, send(): return lax.ppermute(value, axes, [(i, (i + step) % 4) for i in range(4)])  49.7 us
    all_gather x1, waiting for transfers between devices, local(): joint_w = lax.all_gather(joint_w, PLANE, axis=0).reshape(4, 2, 4, 144, 1024)  31.7 us
    pallas_call x1, Pallas kernels, feed_forward_call(): pl.pallas_call(feed_forward_kernel, grid=(2,), in_specs=[tokens_once, tok...  30.4 us
    pallas_call x3, Pallas kernels, plane_grad_call(): pl.pallas_call(plane_grad_kernel, grid=(columns // 256, 2), in_specs=[pl....  30.2 us
    ppermute x15, starting transfers between devices, send(): return lax.ppermute(value, axes, [(i, (i + step) % 4) for i in range(4)])  19.1 us
    pallas_call x1, Pallas kernels, qkv_call(): pl.pallas_call(qkv_kernel, grid=(2, 3), in_specs=[pl.BlockSpec((4, 128, D...  14.7 us
  transfers between devices with their start and end apart: 46, of which 19 were waited for; matrix products, arithmetic and copies ran while one was open for 4% of the time, Pallas kernels for 29%

commit v1 on v0

--- a/solution.py
+++ b/solution.py
@@ -139,9 +139,28 @@
     return centred * inverse, inverse
 
 
+def unit_kernel(x_ref, before_ref, out_ref):
+    block = jnp.where(pl.program_id(0) < 4, x_ref[0], before_ref[...])
+    out_ref[0] = normalise(block.astype(jnp.float32))[0].astype(jnp.bfloat16)
+
+
+def unit_call(ring, before):
+    return pl.pallas_call(
+        unit_kernel,
+        grid=(5,),
+        in_specs=[
+            pl.BlockSpec((1, 128, D), lambda b: (jnp.minimum(b, 3), 0, 0)),
+            pl.BlockSpec((128, D), lambda b: (0, 0)),
+        ],
+        out_specs=pl.BlockSpec((1, 128, D), lambda b: (b, 0, 0)),
+        out_shape=jax.ShapeDtypeStruct((5, 128, D), jnp.bfloat16),
+        compiler_params=pltpu.CompilerParams(vmem_limit_bytes=VMEM_LIMIT),
+        cost_estimate=TINY,
+    )(ring, before)
+
+
 def qkv_kernel(
-    x_ref,
-    before_ref,
+    unit_ref,
     gain_ref,
     shift_ref,
     w0_ref,
@@ -152,7 +171,6 @@
     down_ref,
     out_ref,
     normed_ref,
-    unit_ref,
     normed_rows,
 ):
     part = pl.program_id(1)
@@ -160,12 +178,10 @@
     @pl.when((pl.program_id(0) == 0) & (part == 0))
     def _():
         for b in range(5):
-            block = x_ref[b] if b < 4 else before_ref[...]
-            unit, _ = normalise(block.astype(jnp.float32))
-            normed = (unit * gain_ref[...] + shift_ref[...]).astype(jnp.bfloat16)
+            normed = unit_ref[b].astype(jnp.float32) * gain_ref[...] + shift_ref[...]
+            normed = normed.astype(jnp.bfloat16)
             if b < 4:
                 normed_ref[b] = normed
-                unit_ref[b] = unit.astype(jnp.bfloat16)
             normed_rows[b * 128 : (b + 1) * 128] = normed
 
     def joint(rows):
@@ -208,15 +224,14 @@
                 out_ref[0, j, 0, 1] = block[4]
 
 
-def qkv_call(tokens, before, gain, shift, weights, bias, tables):
+def qkv_call(unit, gain, shift, weights, bias, tables):
     table = pl.BlockSpec((640, 128), lambda h, p: (0, 0))
     vector = pl.BlockSpec((1, D), lambda h, p: (0, 0))
     return pl.pallas_call(
         qkv_kernel,
         grid=(2, 3),
         in_specs=[
-            pl.BlockSpec((4, 128, D), lambda h, p: (0, 0, 0)),
-            pl.BlockSpec((128, D), lambda h, p: (0, 0)),
+            pl.BlockSpec((5, 128, D), lambda h, p: (0, 0, 0)),
             vector,
             vector,
             pl.BlockSpec((4, 1, 4, 144, 128), lambda h, p: (0, h, 0, 0, p)),
@@ -229,17 +244,15 @@
         out_specs=[
             pl.BlockSpec((4, 2, 1, 5, 128, 128), lambda h, p: (0, 0, h, 0, 0, 0)),
             pl.BlockSpec((4, 128, D), lambda h, p: (0, 0, 0)),
-            pl.BlockSpec((4, 128, D), lambda h, p: (0, 0, 0)),
         ],
         out_shape=[
             jax.ShapeDtypeStruct((4, 2, 2, 5, 128, 128), jnp.bfloat16),
             jax.ShapeDtypeStruct((4, 128, D), jnp.bfloat16),
-            jax.ShapeDtypeStruct((4, 128, D), jnp.bfloat16),
         ],
         scratch_shapes=[pltpu.VMEM((640, D), jnp.bfloat16)],
         compiler_params=pltpu.CompilerParams(vmem_limit_bytes=VMEM_LIMIT),
         cost_estimate=TINY,
-    )(tokens, before, gain, shift, weights, weights, bias, *tables)
+    )(unit, gain, shift, weights, weights, bias, *tables)
 
 
 def whole_call(kernel, out_shape, *operands, scratch=()):
@@ -544,55 +557,27 @@
     )(core, *left, *right, *extra)
 
 
-def weight_grad_kernel(core_ref, place_ref, left_ref, left_other_ref, right_ref, right_other_ref, *refs):
-    outs, left_t = refs[:4], refs[4]
-    h = pl.program_id(1)
-
-    @pl.when((h == 0) & (pl.program_id(0) == 0))
-    def _():
-        left_t[:, :512] = jnp.transpose(core_columns(left_ref, core_ref[0], 4))
-        left_t[:, 512:] = jnp.transpose(core_columns(left_other_ref, core_ref[0], 4))
-
-    total = mm(left_t[...], jnp.concatenate([right_ref[0], right_other_ref[0]], 0)).astype(jnp.bfloat16)
-    for z in range(4):
-        for yl in range(2):
-            row = (z * 2 + yl) * 128
-            chip = (h * 2 + yl) * 4 + z
-            step, slot = place_ref[0, chip], place_ref[1, chip]
-            for t in range(4):
-
-                @pl.when(step == t)
-                def _():
-                    outs[t][slot] = total[row : row + 128]
-
-
-def weight_grad_call(core, place, left, right, columns):
-    smem = pl.BlockSpec(memory_space=pltpu.SMEM)
-    left_block = pl.BlockSpec((4, 128, D), lambda n, h: (0, 0, 0))
-    right_block = pl.BlockSpec((1, 512, 256), lambda n, h: (h, 0, n))
-    return pl.pallas_call(
-        weight_grad_kernel,
-        grid=(columns // 256, 2),
-        in_specs=[smem, smem, left_block, left_block, right_block, right_block],
-        out_specs=[pl.BlockSpec((4, 128, 256), lambda n, h: (0, 0, n))] * 4,
-        out_shape=[jax.ShapeDtypeStruct((4, 128, columns), jnp.bfloat16)] * 4,
-        scratch_shapes=[pltpu.VMEM((1024, 1024), jnp.bfloat16)],
-        compiler_params=pltpu.CompilerParams(vmem_limit_bytes=VMEM_LIMIT),
-        cost_estimate=TINY,
-    )(core, place, *left, *right)
-
-
-def joint_grad_kernel(core_ref, place_ref, left_ref, left_other_ref, right_ref, right_other_ref, *refs):
-    outs, left_t = refs[:8], refs[8]
+def own_rows_kernel(place_ref, left_ref, left_other_ref, out_ref):
+    out_ref[:, :512] = jnp.transpose(core_columns(left_ref, place_ref[1], 4))
+    out_ref[:, 512:] = jnp.transpose(core_columns(left_other_ref, place_ref[1], 4))
+
+
+def own_rows_call(place, left):
+    vmem = pl.BlockSpec(memory_space=pltpu.VMEM)
+    return pl.pallas_call(
+        own_rows_kernel,
+        in_specs=[pl.BlockSpec(memory_space=pltpu.SMEM), vmem, vmem],
+        out_specs=vmem,
+        out_shape=jax.ShapeDtypeStruct((1024, 1024), jnp.bfloat16),
+        compiler_params=pltpu.CompilerParams(vmem_limit_bytes=VMEM_LIMIT),
+        cost_estimate=TINY,
+    )(place, *left)
+
+
+def joint_grad_kernel(place_ref, left_ref, right_ref, right_other_ref, *outs):
     h = pl.program_id(0)
-
-    @pl.when(h == 0)
-    def _():
-        left_t[:, :512] = jnp.transpose(core_columns(left_ref, core_ref[0], 4))
-        left_t[:, 512:] = jnp.transpose(core_columns(left_other_ref, core_ref[0], 4))
-
     right = jnp.concatenate([right_ref[0], right_other_ref[0]], 0)
-    total = mm(left_t[...], right).astype(jnp.bfloat16)
+    total = mm(left_ref[...], right).astype(jnp.bfloat16)
     for z in range(4):
         for yl in range(2):
             row = (z * 2 + yl) * 128
@@ -606,20 +591,22 @@
                         outs[4 * j + t][slot] = total[row : row + 128, j * 384 : j * 384 + 384]
 
 
-def joint_grad_call(core, places, left, right):
-    smem = pl.BlockSpec(memory_space=pltpu.SMEM)
-    left_block = pl.BlockSpec((4, 128, D), lambda h: (0, 0, 0))
+def joint_grad_call(places, left, right):
     right_block = pl.BlockSpec((1, 512, 768), lambda h: (h, 0, 0))
     return pl.pallas_call(
         joint_grad_kernel,
         grid=(2,),
-        in_specs=[smem, smem, left_block, left_block, right_block, right_block],
+        in_specs=[
+            pl.BlockSpec(memory_space=pltpu.SMEM),
+            pl.BlockSpec((1024, 1024), lambda h: (0, 0)),
+            right_block,
+            right_block,
+        ],
         out_specs=[pl.BlockSpec((4, 128, 384), lambda h: (0, 0, 0))] * 8,
         out_shape=[jax.ShapeDtypeStruct((4, 128, 384), jnp.bfloat16)] * 8,
-        scratch_shapes=[pltpu.VMEM((1024, 1024), jnp.bfloat16)],
-        compiler_params=pltpu.CompilerParams(vmem_limit_bytes=VMEM_LIMIT),
-        cost_estimate=TINY,
-    )(core, jnp.concatenate(places, 0), *left, *right)
+        compiler_params=pltpu.CompilerParams(vmem_limit_bytes=VMEM_LIMIT),
+        cost_estimate=TINY,
+    )(jnp.concatenate(places, 0), left, *right)
 
 
 def split_sum_kernel(place_ref, a_ref, b_ref, c_ref, d_ref, *out_refs):
@@ -971,9 +958,8 @@
     first_query = half * 64 + (blk // 4) * 16
     lo = lax.dynamic_slice(first_block, (first_query,), (16,)) - (first_query - 16)
 
-    payload, normed_one, unit_one = qkv_call(
-        ring, before, gain_one, shift_one, joint_w, bias, tables
-    )
+    unit_one = unit_call(ring, before)
+    payload, normed_one = qkv_call(unit_one, gain_one, shift_one, joint_w, bias, tables)
     out_w, payload = lax.optimization_barrier((joint_w, payload))
     own_rows = out_rows_call(place, out_w)
     near_rows = [send(own_rows, ("x",), t) for t in (1, 3)]
@@ -997,14 +983,16 @@
     )
     grad_att = exchange(grad_att, ("x",))
     ring_branch = lax.all_gather(after(grad_branch, grad_att), "x", axis=0)
-    shared = plane_grad_call(core, with_other(ring_two), with_other(grad_gu), 2 * HID_PAD, 0, shared)
-    grad_att = after(exchange(grad_att.reshape(16, 128, 128), BLK), shared)
+    joint_left = own_rows_call(place, with_other(normed_one))
+    grad_att = after(exchange(grad_att.reshape(16, 128, 128), BLK), joint_left)
     attended_pair = with_other(attended.transpose(2, 0, 3, 1, 4).reshape(2, 512, 256))
 
     mixed = lax.psum_scatter(
         after(ring_out, grad_att).reshape(512, D), "x", scatter_dimension=0, tiled=True
     )
     back = attend_back_call(lo, blocks, grad_att, att32, lse)
+    hidden_pair = with_other(ring_two), with_other(grad_gu)
+    shared = plane_grad_call(core, *after(hidden_pair, back), 2 * HID_PAD, 0, shared)
     branch_pair = with_other(after(ring_branch, back))
     shared = plane_grad_call(core, branch_pair, attended_pair, 256, 3 * HID_PAD, shared)
     back = exchange(back, BLK).reshape(4, 2, 2, 5, 128, 128)
@@ -1014,9 +1002,9 @@
     halo_back = lax.ppermute(back[0, :, :, :2], ("yh",), [(1, 0)])
     back = after(back, mixed)
     grad_joint, grad_bias = turn_back_call(back, halo_back, tables)
+    places = (chip_places(True), chip_places(False))
+    parts = joint_grad_call(places, joint_left, with_other(grad_joint))
     ring_one, grad_gain_one, grad_shift_one = normed_back_call(grad_joint, unit_one, joint_w)
-    places = (chip_places(True), chip_places(False))
-    parts = joint_grad_call(core, places, with_other(normed_one), with_other(grad_joint))
     pair_came = [first_send(parts[4 * j : 4 * j + 4], j == 0) for j in range(2)]
 
     norms = jnp.concatenate([grad_gain_one, grad_shift_one, grad_gain_two, grad_shift_two], 0)

time: 523 us -> 516 us (0.987)
  the two profiles are of different devices: /device:TPU:4 before, /device:TPU:0 now
where the time goes in v1:
time: 516 us; the launch traced here: 506 us
  waiting for transfers between devices  195 us (38%)
  Pallas kernels  167 us (32%)
  starting transfers between devices  83.1 us (16%)
  local copies, waits for them, and re-layouts  22.1 us (4%)
  between operations  15.1 us (3%)
  blocking collectives  14 us (3%)
  other arithmetic  9.53 us (2%)
    all_to_all x10, waiting for transfers between devices, exchange(): return lax.all_to_all(parts, axes, 0, 0, tiled=True)  100 us
    all_to_all x10, starting transfers between devices, exchange(): return lax.all_to_all(parts, axes, 0, 0, tiled=True)  50.4 us
    ppermute x15, waiting for transfers between devices, send(): return lax.ppermute(value, axes, [(i, (i + step) % 4) for i in range(4)])  49.1 us
    pallas_call x1, Pallas kernels, feed_forward_call(): pl.pallas_call(feed_forward_kernel, grid=(2,), in_specs=[tokens_once, tok...  30.4 us
    pallas_call x3, Pallas kernels, plane_grad_call(): pl.pallas_call(plane_grad_kernel, grid=(columns // 256, 2), in_specs=[pl....  30 us
    ppermute x15, starting transfers between devices, send(): return lax.ppermute(value, axes, [(i, (i + step) % 4) for i in range(4)])  23.7 us
    ppermute x1, waiting for transfers between devices, local(): halo_back = lax.ppermute(back[0, :, :, :2], ('yh',), [(1, 0)])  20.6 us
    ppermute x1, waiting for transfers between devices, local(): before = lax.ppermute(ring[3], ('yh',), [(0, 1)])  20.5 us
  transfers between devices with their start and end apart: 45, of which 19 were waited for; matrix products, arithmetic and copies ran while one was open for 4% of the time, Pallas kernels for 30%

profile of v1, /device:TPU:0, one launch (start us, length us, event | category | flops | bytes accessed | tf_op | source)
XLA Modules:
  0.0 506.0 jit_solution(3627443102960092518)
XLA Ops:
  10.3 2.6 broadcast_in_dim.57
  12.9 4.5 all-to-all-start
  18.6 25.2 %all-to-all-done.x_ref = bf16[4,128,2048]{2,1,0:T(8,128)(2,1)S(1)} async-done(((bf16[4,128,2048]{2,1,0:T(8,128)(2,1)}), bf16[4,128,2048]{2,1,0:T(8,128)(2,1)S(1)}, u32[]{:S(2)}, u32[]{:S(2)}) %all-to-all-start) | async-done | bytes 2097184 | tf_op jit(solution)/shard_map/all_to_all | solution.py:43
  43.8 5.1 %collective-permute-start = (bf16[128,2048]{1,0:T(8,128)(2,1)S(1)}, bf16[128,2048]{1,0:T(8,128)(2,1)S(1)}, u32[]{:S(2)}, u32[]{:S(2)}) collective-permute-start(bf16[128,2048]{1,0:T(8,128)(2,1)S(1)} %slice_bitcast_fusion), channel_id=1, source_target_pairs={{0,64},{1,65},{2,66},{3,67},{4,68},{5,69},{6,70},{7,71},{8,72},{9,... | collective-permute-start | bytes 1572872 | tf_op jit(solution)/shard_map/ppermute | solution.py:943
  51.2 20.5 %collective-permute-done.before_ref = bf16[128,2048]{1,0:T(8,128)(2,1)S(1)} collective-permute-done((bf16[128,2048]{1,0:T(8,128)(2,1)S(1)}, bf16[128,2048]{1,0:T(8,128)(2,1)S(1)}, u32[]{:S(2)}, u32[]{:S(2)}) %collective-permute-start) | collective-permute-done | bytes 524320 | tf_op jit(solution)/shard_map/ppermute | solution.py:943
  72.4 5.3 %shard_map.221.unit_ref = bf16[5,128,2048]{2,1,0:T(8,128)(2,1)} custom-call(bf16[4,128,2048]{2,1,0:T(8,128)(2,1)} %copy-done.3, bf16[128,2048]{1,0:T(8,128)(2,1)} %copy-done.14), custom_call_target="tpu_custom_call" | custom-call | flops 1 | bytes 1 | tf_op jit(solution)/shard_map/pallas_call | solution.py:148
  80.7 12.6 %shard_map.222 = (bf16[4,2,2,5,128,128]{5,4,3,2,1,0:T(8,128)(2,1)}, bf16[4,128,2048]{2,1,0:T(8,128)(2,1)}) custom-call(bf16[5,128,2048]{2,1,0:T(8,128)(2,1)} %shard_map.221.unit_ref, f32[1,2048]{1,0:T(1,128)} %bitcast.81, f32[1,2048]{1,0:T(1,128)} %bitcast.86, bf16[4,2,4,144,1024]{4,3,2,1,0:T(8,128)(2,1)} %bitcast.58, ...), custom_call_target="tpu_custom_call" | custom-call | flops 1 | bytes 1 | tf_op jit(solution)/shard_map/pallas_call | solution.py:230
  93.2 4.8 all-to-all-start.1
  98.6 3.7 shard_map.223.refs_0_
  107.7 25.7 %collective-permute-done.1.refs_1_ = bf16[8,128,512]{2,1,0:T(8,128)(2,1)} collective-permute-done((bf16[8,128,512]{2,1,0:T(8,128)(2,1)}, bf16[8,128,512]{2,1,0:T(8,128)(2,1)}, u32[]{:S(2)}, u32[]{:S(2)}) %collective-permute-start.1) | collective-permute-done | bytes 1048608 | tf_op jit(solution)/shard_map/ppermute | solution.py:55
  135.9 11.3 %shard_map.224 = (f32[16,128,128]{2,1,0:T(8,128)}, bf16[16,128,128]{2,1,0:T(8,128)(2,1)}, f32[8,1,512]{2,1,0:T(1,128)}) custom-call(s32[16]{0:T(128)} %dynamic-slice_subtract_fusion.lo_ref, bf16[16,5,128,128]{3,2,1,0:T(8,128)(2,1)} %copy-done), custom_call_target="tpu_custom_call" | custom-call | flops 1 | bytes 1 | tf_op jit(solution)/shard_map/pallas_call | solution.py:745
  147.1 9.6 %all-to-all-start.2 = ((bf16[16,128,128]{2,1,0:T(8,128)(2,1)}), bf16[16,128,128]{2,1,0:T(8,128)(2,1)}, u32[]{:S(2)}, u32[]{:S(2)}) async-start(bf16[16,128,128]{2,1,0:T(8,128)(2,1)} %get-tuple-element.83), calls=%async_computation.2 | async-start | bytes 1048576 | tf_op jit(solution)/shard_map/all_to_all | solution.py:43
  157.6 10.0 %all-to-all-done.2 = bf16[16,128,128]{2,1,0:T(8,128)(2,1)} async-done(((bf16[16,128,128]{2,1,0:T(8,128)(2,1)}), bf16[16,128,128]{2,1,0:T(8,128)(2,1)}, u32[]{:S(2)}, u32[]{:S(2)}) %all-to-all-start.2) | async-done | bytes 524320 | tf_op jit(solution)/shard_map/all_to_all | solution.py:43
  167.7 4.1 all-to-all-start.3
  171.9 10.4 %all-to-all-done.3.att_ref = bf16[4,2,2,128,128]{4,3,2,1,0:T(8,128)(2,1)} async-done(((bf16[4,2,2,128,128]{4,3,2,1,0:T(8,128)(2,1)}), bf16[4,2,2,128,128]{4,3,2,1,0:T(8,128)(2,1)}, u32[]{:S(2)}, u32[]{:S(2)}) %all-to-all-start.3) | async-done | bytes 524320 | tf_op jit(solution)/shard_map/all_to_all | solution.py:43
  182.3 8.7 %shard_map.225 = (f32[128,2048]{1,0:T(8,128)}, bf16[4,128,2048]{2,1,0:T(8,128)(2,1)}) custom-call(s32[2]{0:T(128)} %pad_add_fusion.1.place_ref, bf16[4,2,2,128,128]{4,3,2,1,0:T(8,128)(2,1)} %all-to-all-done.3.att_ref, bf16[128,2048]{1,0:T(8,128)(2,1)} %tokens_ref.3, f32[1,2048]{1,0:T(1,128)} %bitcast.83, f32[1,2048]{1,0:T(1,128)} %bitcast.85, ...), custom_call_target="tpu_custom_call" | custom-call | flops 1 | bytes 1 | tf_op jit(solution)/shard_map/pallas_call | solution.py:372
  191.0 3.6 all-to-all-start.4
  194.9 26.1 %all-to-all-done.4.x_ref.left_ref = bf16[4,128,2048]{2,1,0:T(8,128)(2,1)S(1)} async-done(((bf16[4,128,2048]{2,1,0:T(8,128)(2,1)}), bf16[4,128,2048]{2,1,0:T(8,128)(2,1)S(1)}, u32[]{:S(2)}, u32[]{:S(2)}) %all-to-all-start.4) | async-done | bytes 2097184 | tf_op jit(solution)/shard_map/all_to_all | solution.py:43
  222.4 30.4 %shard_map.227 = (bf16[2,512,768]{2,1,0:T(8,128)(2,1)}, bf16[2,512,1536]{2,1,0:T(8,128)(2,1)}, bf16[4,128,2048]{2,1,0:T(8,128)(2,1)}, bf16[4,128,2048]{2,1,0:T(8,128)(2,1)}) custom-call(bf16[4,128,2048]{2,1,0:T(8,128)(2,1)} %copy-done.1, bf16[4,128,2048]{2,1,0:T(8,128)(2,1)} %bitcast.68, bf16[4,2,512,2304]{3,2,1,0:T(8,128)(2,1)} %bitcast.63, ...), custom_call_target="tpu_custom_call" | custom-call | flops 1 | bytes 1 | tf_op jit(solution)/shard_map/pallas_call | solution.py:499
  253.0 3.6 all-to-all-start.5
  256.7 9.3 %shard_map.228.refs_0_ = bf16[2,2,4,128,2560]{4,3,2,1,0:T(8,128)(2,1)} custom-call(s32[1]{0:T(128)} %bitcast.1.core_ref, bf16[4,128,2048]{2,1,0:T(8,128)(2,1)} %bitcast.69, bf16[4,128,2048]{2,1,0:T(8,128)(2,1)} %collective-permute-done.8.left_other_ref, bf16[2,512,768]{2,1,0:T(8,128)(2,1)} %get-tuple-element.92.right_ref, ...), custom_call_target="tpu_custom_call" | custom-call | flops 1 | bytes 1 | tf_op jit(solution)/shard_map/pallas_call | solution.py:540
  266.0 17.8 %all-to-all-done.5.came_ref = bf16[4,128,2048]{2,1,0:T(8,128)(2,1)S(1)} async-done(((bf16[4,128,2048]{2,1,0:T(8,128)(2,1)}), bf16[4,128,2048]{2,1,0:T(8,128)(2,1)S(1)}, u32[]{:S(2)}, u32[]{:S(2)}) %all-to-all-start.5) | async-done | bytes 2097184 | tf_op jit(solution)/shard_map/all_to_all | solution.py:43
  285.2 9.0 %shard_map.229 = (f32[128,2048]{1,0:T(8,128)}, bf16[128,2048]{1,0:T(8,128)(2,1)}, f32[1,2048]{1,0:T(1,128)}, f32[1,2048]{1,0:T(1,128)}, bf16[4,2,2,128,128]{4,3,2,1,0:T(8,128)(2,1)}) custom-call(s32[2]{0:T(128)} %pad_add_fusion.1.place_ref, bf16[4,128,2048]{2,1,0:T(8,128)(2,1)} %copy-done.5, f32[128,2048]{1,0:T(8,128)} %get-tuple-element.86.middle_ref, ...), custom_call_target="tpu_custom_call" | custom-call | flops 1 | bytes 1 | tf_op jit(solution)/shard_map/pallas_call | solution.py:433
  294.2 14.0 %all_to_all.59 = bf16[4,2,2,128,128]{4,3,2,1,0:T(8,128)(2,1)} all-to-all(bf16[4,2,2,128,128]{4,3,2,1,0:T(8,128)(2,1)} %get-tuple-element.94), channel_id=1, replica_groups=mesh['yh'=2,'x'=4,'z'=4,'yl'=2,'k'=2] {'x'}, dimensions={0} | all-to-all | bytes 1048576 | tf_op jit(solution)/shard_map/all_to_all | solution.py:43
  308.3 3.6 all-to-all-start.7
  314.1 4.2 shard_map.230.left_ref
  318.3 4.5 all-to-all-done.7.do_ref
  323.6 14.3 %shard_map.231 = bf16[16,5,128,128]{3,2,1,0:T(8,128)(2,1)} custom-call(s32[16]{0:T(128)} %dynamic-slice_subtract_fusion.lo_ref, bf16[16,5,128,128]{3,2,1,0:T(8,128)(2,1)} %copy-done, bf16[16,128,128]{2,1,0:T(8,128)(2,1)} %copy-done.12, f32[16,128,128]{2,1,0:T(8,128)} %get-tuple-element.98.o32_ref, f32[8,1,512]{2,1,0:T(1,128)} %get-tuple-element.99.lse_ref), custom_call_target="tpu_custom_call" | custom-call | flops 1 | bytes 1 | tf_op jit(solution)/shard_map/pallas_call | solution.py:809
  337.9 7.8 %all-to-all-start.8 = ((bf16[16,5,128,128]{3,2,1,0:T(8,128)(2,1)}), bf16[16,5,128,128]{3,2,1,0:T(8,128)(2,1)}, u32[]{:S(2)}, u32[]{:S(2)}) async-start(bf16[16,5,128,128]{3,2,1,0:T(8,128)(2,1)} %shard_map.231), calls=%async_computation.9 | async-start | bytes 5242880 | tf_op jit(solution)/shard_map/all_to_all | solution.py:43
  348.8 2.9 collective-permute-done.13.left_other_ref
  351.6 15.3 %shard_map.232.refs_0_ = bf16[2,2,4,128,2560]{4,3,2,1,0:T(8,128)(2,1)} custom-call(s32[1]{0:T(128)} %bitcast.1.core_ref, bf16[4,128,2048]{2,1,0:T(8,128)(2,1)} %copy-done.1, bf16[4,128,2048]{2,1,0:T(8,128)(2,1)} %collective-permute-done.13.left_other_ref, bf16[2,512,1536]{2,1,0:T(8,128)(2,1)} %get-tuple-element.106.right_ref, ...), custom_call_target="tpu_custom_call", output_to_operand_aliasing={{}: (5, {})} | custom-call | flops 1 | bytes 1 | tf_op jit(solution)/shard_map/pallas_call | solution.py:540
  367.8 5.4 %shard_map.233 = bf16[2,2,4,128,2560]{4,3,2,1,0:T(8,128)(2,1)} custom-call(s32[1]{0:T(128)} %bitcast.1.core_ref, bf16[4,128,2048]{2,1,0:T(8,128)(2,1)} %bitcast.72, bf16[4,128,2048]{2,1,0:T(8,128)(2,1)} %collective-permute-done.11.left_other_ref, bf16[2,512,256]{2,1,0:T(8,128)(2,1)} %copy-done.11, ...), custom_call_target="tpu_custom_call", output_to_operand_aliasing={{}: (5, {})} | custom-call | flops 1 | bytes 1 | tf_op jit(solution)/shard_map/pallas_call | solution.py:540
  373.1 6.1 %all-to-all-done.8 = bf16[16,5,128,128]{3,2,1,0:T(8,128)(2,1)} async-done(((bf16[16,5,128,128]{3,2,1,0:T(8,128)(2,1)}), bf16[16,5,128,128]{3,2,1,0:T(8,128)(2,1)}, u32[]{:S(2)}, u32[]{:S(2)}) %all-to-all-start.8) | async-done | bytes 2621472 | tf_op jit(solution)/shard_map/all_to_all | solution.py:43
  383.6 20.6 %collective-permute-done.15.halo_ref = bf16[2,2,2,128,128]{4,3,2,1,0:T(8,128)(2,1)S(1)} collective-permute-done((bf16[2,2,2,128,128]{4,3,2,1,0:T(8,128)(2,1)S(1)}, bf16[2,2,2,128,128]{4,3,2,1,0:T(8,128)(2,1)S(1)}, u32[]{:S(2)}, u32[]{:S(2)}) %collective-permute-start.15) | collective-permute-done | bytes 262176 | tf_op jit(solution)/shard_map/ppermute | solution.py:1002
  405.0 3.7 shard_map.234
  409.0 8.9 %shard_map.235 = (bf16[4,128,2048]{2,1,0:T(8,128)(2,1)}, f32[1,2048]{1,0:T(1,128)}, f32[1,2048]{1,0:T(1,128)}) custom-call(bf16[2,512,768]{2,1,0:T(8,128)(2,1)} %get-tuple-element.111.g_ref.right_ref, bf16[5,128,2048]{2,1,0:T(8,128)(2,1)} %shard_map.221.unit_ref, bf16[4,2,4,144,1024]{4,3,2,1,0:T(8,128)(2,1)} %bitcast.62), custom_call_target="tpu_custom_call" | custom-call | flops 1 | bytes 1 | tf_op jit(solution)/shard_map/pallas_call | solution.py:900
  420.3 4.8 all-to-all-start.10
  427.0 8.7 %shard_map.236 = (bf16[4,128,384]{2,1,0:T(8,128)(2,1)}, bf16[4,128,384]{2,1,0:T(8,128)(2,1)}, bf16[4,128,384]{2,1,0:T(8,128)(2,1)}, bf16[4,128,384]{2,1,0:T(8,12...) custom-call(s32[4,16]{1,0:T(4,128)} %pad_add_fusion.place_ref, ...), custom_call_target="tpu_custom_call" | custom-call | flops 1 | bytes 1 | tf_op jit(solution)/shard_map/pallas_call | solution.py:596
  435.7 3.8 all-to-all-start.9
  448.2 9.9 %collective-permute-done.17.b_ref = bf16[4,128,384]{2,1,0:T(8,128)(2,1)S(1)} collective-permute-done((bf16[4,128,384]{2,1,0:T(8,128)(2,1)S(1)}, bf16[4,128,384]{2,1,0:T(8,128)(2,1)S(1)}, u32[]{:S(2)}, u32[]{:S(2)}) %collective-permute-start.17) | collective-permute-done | bytes 393248 | tf_op jit(solution)/shard_map/ppermute | solution.py:55
  458.1 2.3 collective-permute-start.25
  460.4 5.0 collective-permute-done.18.c_ref
  470.1 2.9 collective-permute-start.21
  474.4 3.9 shard_map.237
  482.9 2.5 collective-permute-start.27
  487.2 4.1 collective-permute-done.26.refs_5_
  491.3 2.5 collective-permute-done.28.refs_7_
  496.4 2.3 shard_map.241
  (189 shorter events, 62.9 us)
Async XLA Ops:
  7.2 71.2 %all-gather.9.cloned.1.call-start = ((), (), s32[]{:S(2)}) async-start(), calls=%async_computation.15 | async-start | bytes 9732096 | tf_op jit(solution)/shard_map/all_gather | solution.py:940
  12.9 30.8 %all-to-all-start = ((bf16[4,128,2048]{2,1,0:T(8,128)(2,1)}), bf16[4,128,2048]{2,1,0:T(8,128)(2,1)S(1)}, u32[]{:S(2)}, u32[]{:S(2)}) async-start(bf16[4,128,2048]{2,1,0:T(8,128)(2,1)} %broadcast_in_dim.57), calls=%async_computation | async-start | bytes 4194304 | tf_op jit(solution)/shard_map/all_to_all | solution.py:43
  17.4 177.2 %all-gather.11.cloned.1.call-start = ((), (), s32[]{:S(2)}) async-start(), calls=%async_computation.16 | async-start | bytes 2621440 | tf_op jit(solution)/shard_map/all_gather | solution.py:944
  43.7 27.9 %copy-start.3 = (bf16[4,128,2048]{2,1,0:T(8,128)(2,1)}, bf16[4,128,2048]{2,1,0:T(8,128)(2,1)S(1)}, u32[]{:S(2)}) copy-start(bf16[4,128,2048]{2,1,0:T(8,128)(2,1)S(1)} %all-to-all-done.x_ref) | copy-start | bytes 6291460
  43.8 27.8 %collective-permute-start = (bf16[128,2048]{1,0:T(8,128)(2,1)S(1)}, bf16[128,2048]{1,0:T(8,128)(2,1)S(1)}, u32[]{:S(2)}, u32[]{:S(2)}) collective-permute-start(bf16[128,2048]{1,0:T(8,128)(2,1)S(1)} %slice_bitcast_fusion), channel_id=1, source_target_pairs={{0,64},{1,65},{2,66},{3,67},{4,68},{5,69},{6,70},{7,71},{8,72},{9,... | collective-permute-start | bytes 1572872 | tf_op jit(solution)/shard_map/ppermute | solution.py:943
  93.2 40.2 %all-to-all-start.1 = ((bf16[16,5,128,128]{3,2,1,0:T(8,128)(2,1)}), bf16[16,5,128,128]{3,2,1,0:T(8,128)(2,1)S(1)}, u32[]{:S(2)}, u32[]{:S(2)}) async-start(bf16[16,5,128,128]{3,2,1,0:T(8,128)(2,1)} %bitcast.70), calls=%async_computation.1 | async-start | bytes 5242880 | tf_op jit(solution)/shard_map/all_to_all | solution.py:43
  98.0 123.1 %all-gather.13.cloned.1.call-start = ((), (), s32[]{:S(2)}) async-start(), calls=%async_computation.17 | async-start | bytes 19464192 | tf_op jit(solution)/shard_map/all_gather | solution.py:967
  102.4 31.0 %collective-permute-start.1 = (bf16[8,128,512]{2,1,0:T(8,128)(2,1)}, bf16[8,128,512]{2,1,0:T(8,128)(2,1)}, u32[]{:S(2)}, u32[]{:S(2)}) collective-permute-start(bf16[8,128,512]{2,1,0:T(8,128)(2,1)} %shard_map.223.refs_0_), channel_id=1, source_target_pairs={{0,16},{16,32},{32,48},{48,0},{1,17},{17,33},{33,49},{49,1},{2,18}... | collective-permute-start | bytes 3145736 | tf_op jit(solution)/shard_map/ppermute | solution.py:55
  103.6 29.8 %collective-permute-start.2 = (bf16[8,128,512]{2,1,0:T(8,128)(2,1)}, bf16[8,128,512]{2,1,0:T(8,128)(2,1)}, u32[]{:S(2)}, u32[]{:S(2)}) collective-permute-start(bf16[8,128,512]{2,1,0:T(8,128)(2,1)} %shard_map.223.refs_0_), channel_id=1, source_target_pairs={{0,48},{16,0},{32,16},{48,32},{1,49},{17,1},{33,17},{49,33},{2,50}... | collective-permute-start | bytes 3145736 | tf_op jit(solution)/shard_map/ppermute | solution.py:55
  133.4 34.2 %collective-permute-start.3 = (bf16[8,128,512]{2,1,0:T(8,128)(2,1)}, bf16[8,128,512]{2,1,0:T(8,128)(2,1)}, u32[]{:S(2)}, u32[]{:S(2)}) collective-permute-start(bf16[8,128,512]{2,1,0:T(8,128)(2,1)} %shard_map.223.refs_0_), channel_id=1, source_target_pairs={{0,32},{16,48},{32,0},{48,16},{1,33},{17,49},{33,1},{49,17},{2,34}... | collective-permute-start | bytes 3145736 | tf_op jit(solution)/shard_map/ppermute | solution.py:55
  147.1 20.6 %all-to-all-start.2 = ((bf16[16,128,128]{2,1,0:T(8,128)(2,1)}), bf16[16,128,128]{2,1,0:T(8,128)(2,1)}, u32[]{:S(2)}, u32[]{:S(2)}) async-start(bf16[16,128,128]{2,1,0:T(8,128)(2,1)} %get-tuple-element.83), calls=%async_computation.2 | async-start | bytes 1048576 | tf_op jit(solution)/shard_map/all_to_all | solution.py:43
  156.8 15.1 %collective-permute-start.4 = (bf16[8,128,512]{2,1,0:T(8,128)(2,1)}, bf16[8,128,512]{2,1,0:T(8,128)(2,1)S(1)}, u32[]{:S(2)}, u32[]{:S(2)}) collective-permute-start(bf16[8,128,512]{2,1,0:T(8,128)(2,1)} %shard_map.223.refs_0_), channel_id=1, source_target_pairs={{0,1},{1,0},{2,3},{3,2},{4,5},{5,4},{6,7},{7,6},{8,9},{9,8},{10,11... | collective-permute-start | bytes 3145736 | tf_op jit(solution)/shard_map/ppermute | solution.py:39
  157.1 14.7 %collective-permute-start.5 = (bf16[8,128,512]{2,1,0:T(8,128)(2,1)}, bf16[8,128,512]{2,1,0:T(8,128)(2,1)S(1)}, u32[]{:S(2)}, u32[]{:S(2)}) collective-permute-start(bf16[8,128,512]{2,1,0:T(8,128)(2,1)} %collective-permute-done.1.refs_1_), channel_id=1, source_target_pairs={{0,1},{1,0},{2,3},{3,2},{4,5},{5,4},{6,7},{7,6},{8,9},{9,8},{10,11... | collective-permute-start | bytes 3145736 | tf_op jit(solution)/shard_map/ppermute | solution.py:39
  157.4 14.5 %collective-permute-start.7 = (bf16[8,128,512]{2,1,0:T(8,128)(2,1)}, bf16[8,128,512]{2,1,0:T(8,128)(2,1)S(1)}, u32[]{:S(2)}, u32[]{:S(2)}) collective-permute-start(bf16[8,128,512]{2,1,0:T(8,128)(2,1)} %collective-permute-done.2.refs_3_), channel_id=1, source_target_pairs={{0,1},{1,0},{2,3},{3,2},{4,5},{5,4},{6,7},{7,6},{8,9},{9,8},{10,11... | collective-permute-start | bytes 3145736 | tf_op jit(solution)/shard_map/ppermute | solution.py:39
  167.7 14.6 %collective-permute-start.6 = (bf16[8,128,512]{2,1,0:T(8,128)(2,1)}, bf16[8,128,512]{2,1,0:T(8,128)(2,1)}, u32[]{:S(2)}, u32[]{:S(2)}) collective-permute-start(bf16[8,128,512]{2,1,0:T(8,128)(2,1)} %collective-permute-done.3.refs_2_), channel_id=1, source_target_pairs={{0,1},{1,0},{2,3},{3,2},{4,5},{5,4},{6,7},{7,6},{8,9},{9,8},{10,11... | collective-permute-start | bytes 3145736 | tf_op jit(solution)/shard_map/ppermute | solution.py:39
  167.7 14.6 %all-to-all-start.3 = ((bf16[4,2,2,128,128]{4,3,2,1,0:T(8,128)(2,1)}), bf16[4,2,2,128,128]{4,3,2,1,0:T(8,128)(2,1)}, u32[]{:S(2)}, u32[]{:S(2)}) async-start(bf16[4,2,2,128,128]{4,3,2,1,0:T(8,128)(2,1)} %bitcast.21), calls=%async_computation.3 | async-start | bytes 1048576 | tf_op jit(solution)/shard_map/all_to_all | solution.py:43
  171.9 10.5 %copy-start.6 = (bf16[8,128,512]{2,1,0:T(8,128)(2,1)}, bf16[8,128,512]{2,1,0:T(8,128)(2,1)S(1)}, u32[]{:S(2)}) copy-start(bf16[8,128,512]{2,1,0:T(8,128)(2,1)S(1)} %collective-permute-done.4.refs_4_) | copy-start | bytes 3145732
  191.0 30.1 %all-to-all-start.4 = ((bf16[4,128,2048]{2,1,0:T(8,128)(2,1)}), bf16[4,128,2048]{2,1,0:T(8,128)(2,1)S(1)}, u32[]{:S(2)}, u32[]{:S(2)}) async-start(bf16[4,128,2048]{2,1,0:T(8,128)(2,1)} %get-tuple-element.87), calls=%async_computation.4 | async-start | bytes 4194304 | tf_op jit(solution)/shard_map/all_to_all | solution.py:43
  194.7 62.0 %collective-permute-start.8 = (bf16[4,128,2048]{2,1,0:T(8,128)(2,1)}, bf16[4,128,2048]{2,1,0:T(8,128)(2,1)}, u32[]{:S(2)}, u32[]{:S(2)}) collective-permute-start(bf16[4,128,2048]{2,1,0:T(8,128)(2,1)} %bitcast.67), channel_id=1, source_target_pairs={{0,1},{1,0},{2,3},{3,2},{4,5},{5,4},{6,7},{7,6},{8,9},{9,8},{10,11... | collective-permute-start | bytes 6291464 | tf_op jit(solution)/shard_map/ppermute | solution.py:39
  252.9 3.8 collective-permute-start.9
  253.0 30.8 %all-to-all-start.5 = ((bf16[4,128,2048]{2,1,0:T(8,128)(2,1)}), bf16[4,128,2048]{2,1,0:T(8,128)(2,1)S(1)}, u32[]{:S(2)}, u32[]{:S(2)}) async-start(bf16[4,128,2048]{2,1,0:T(8,128)(2,1)} %get-tuple-element.91), calls=%async_computation.5 | async-start | bytes 4194304 | tf_op jit(solution)/shard_map/all_to_all | solution.py:43
  256.6 89.6 %all-gather.15.cloned.1.call-start = ((), (), s32[]{:S(2)}) async-start(), calls=%async_computation.18 | async-start | bytes 2621440 | tf_op jit(solution)/shard_map/all_gather | solution.py:985
  308.2 4.5 collective-permute-start.10
  308.3 14.4 %all-to-all-start.7 = ((bf16[16,128,128]{2,1,0:T(8,128)(2,1)}), bf16[16,128,128]{2,1,0:T(8,128)(2,1)S(1)}, u32[]{:S(2)}, u32[]{:S(2)}) async-start(bf16[16,128,128]{2,1,0:T(8,128)(2,1)} %bitcast.28), calls=%async_computation.7 | async-start | bytes 1048576 | tf_op jit(solution)/shard_map/all_to_all | solution.py:43
  311.9 67.4 %reduce-scatter.3.cloned.1.call-start = ((), (), s32[]{:S(2)}) async-start(), calls=%async_computation.13 | async-start | bytes 2621440 | tf_op jit(solution)/shard_map/reduce_scatter | solution.py:990
  322.8 28.9 %collective-permute-start.14 = (bf16[2,512,1536]{2,1,0:T(8,128)(2,1)}, bf16[2,512,1536]{2,1,0:T(8,128)(2,1)}, u32[]{:S(2)}, u32[]{:S(2)}) collective-permute-start(bf16[2,512,1536]{2,1,0:T(8,128)(2,1)} %get-tuple-element.106.right_ref), channel_id=1, source_target_pairs={{0,1},{1,0},{2,3},{3,2},{4,5},{5,4},{6,7},{7,6},{8,9},{9,8},{10,11... | collective-permute-start | bytes 9437192 | tf_op jit(solution)/shard_map/ppermute | solution.py:39
  337.9 41.4 %all-to-all-start.8 = ((bf16[16,5,128,128]{3,2,1,0:T(8,128)(2,1)}), bf16[16,5,128,128]{3,2,1,0:T(8,128)(2,1)}, u32[]{:S(2)}, u32[]{:S(2)}) async-start(bf16[16,5,128,128]{3,2,1,0:T(8,128)(2,1)} %shard_map.231), calls=%async_computation.9 | async-start | bytes 5242880 | tf_op jit(solution)/shard_map/all_to_all | solution.py:43
  345.7 150.7 %reduce-scatter.5.cloned.1.call-start = ((), (), s32[]{:S(2)}) async-start(), calls=%async_computation.14 | async-start | bytes 11141120 | tf_op jit(solution)/shard_map/reduce_scatter | solution.py:643
  345.8 5.8 %collective-permute-start.13 = (bf16[4,128,2048]{2,1,0:T(8,128)(2,1)S(1)}, bf16[4,128,2048]{2,1,0:T(8,128)(2,1)}, u32[]{:S(2)}, u32[]{:S(2)}) collective-permute-start(bf16[4,128,2048]{2,1,0:T(8,128)(2,1)S(1)} %copy-done.2), channel_id=1, source_target_pairs={{0,1},{1,0},{2,3},{3,2},{4,5},{5,4},{6,7},{7,6},{8,9},{9,8},{10,11... | collective-permute-start | bytes 6291464 | tf_op jit(solution)/shard_map/ppermute | solution.py:39
  346.2 20.7 %collective-permute-start.11 = (bf16[4,128,2048]{2,1,0:T(8,128)(2,1)}, bf16[4,128,2048]{2,1,0:T(8,128)(2,1)}, u32[]{:S(2)}, u32[]{:S(2)}) collective-permute-start(bf16[4,128,2048]{2,1,0:T(8,128)(2,1)} %bitcast.71), channel_id=1, source_target_pairs={{0,1},{1,0},{2,3},{3,2},{4,5},{5,4},{6,7},{7,6},{8,9},{9,8},{10,11... | collective-permute-start | bytes 6291464 | tf_op jit(solution)/shard_map/ppermute | solution.py:39
  348.3 18.6 %copy-start.11 = (bf16[2,512,256]{2,1,0:T(8,128)(2,1)}, bf16[2,512,256]{2,1,0:T(8,128)(2,1)S(1)}, u32[]{:S(2)}) copy-start(bf16[2,512,256]{2,1,0:T(8,128)(2,1)S(1)} %reshape.369.right_ref) | copy-start | bytes 1572868
  348.3 18.6 %collective-permute-start.12 = (bf16[2,512,256]{2,1,0:T(8,128)(2,1)S(1)}, bf16[2,512,256]{2,1,0:T(8,128)(2,1)S(1)}, u32[]{:S(2)}, u32[]{:S(2)}) collective-permute-start(bf16[2,512,256]{2,1,0:T(8,128)(2,1)S(1)} %reshape.369.right_ref), channel_id=1, source_target_pairs={{0,1},{1,0},{2,3},{3,2},{4,5},{5,4},{6,7},{7,6},{8,9},{9,8},{10,11... | collective-permute-start | bytes 1572872 | tf_op jit(solution)/shard_map/ppermute | solution.py:39
  380.4 23.9 %collective-permute-start.15 = (bf16[2,2,2,128,128]{4,3,2,1,0:T(8,128)(2,1)S(1)}, bf16[2,2,2,128,128]{4,3,2,1,0:T(8,128)(2,1)S(1)}, u32[]{:S(2)}, u32[]{:S(2)}) collective-permute-start(bf16[2,2,2,128,128]{4,3,2,1,0:T(8,128)(2,1)S(1)} %slice_bitcast_fusion.1), channel_id=1, source_target_pairs={{64,0},{65,1},{66,2},{67,3},{68,4},{69,5},{70,6},{71,7},{72,8},{73... | collective-permute-start | bytes 786440 | tf_op jit(solution)/shard_map/ppermute | solution.py:1002
  408.7 17.1 %collective-permute-start.16 = (bf16[2,512,768]{2,1,0:T(8,128)(2,1)}, bf16[2,512,768]{2,1,0:T(8,128)(2,1)S(1)}, u32[]{:S(2)}, u32[]{:S(2)}) collective-permute-start(bf16[2,512,768]{2,1,0:T(8,128)(2,1)} %get-tuple-element.111.g_ref.right_ref), channel_id=1, source_target_pairs={{0,1},{1,0},{2,3},{3,2},{4,5},{5,4},{6,7},{7,6},{8,9},{9,8},{10,11... | collective-permute-start | bytes 4718600 | tf_op jit(solution)/shard_map/ppermute | solution.py:39
  420.3 15.3 %all-to-all-start.10 = ((f32[128,1,128]{2,1,0:T(1,128)}), f32[128,1,128]{2,1,0:T(1,128)S(1)}, u32[]{:S(2)}, u32[]{:S(2)}) async-start(f32[128,1,128]{2,1,0:T(1,128)} %copy.53), calls=%async_computation.11 | async-start | bytes 131072 | tf_op jit(solution)/shard_map/all_to_all | solution.py:43
  435.7 37.3 %all-to-all-start.9 = ((bf16[4,128,2048]{2,1,0:T(8,128)(2,1)}), bf16[4,128,2048]{2,1,0:T(8,128)(2,1)S(1)}, u32[]{:S(2)}, u32[]{:S(2)}) async-start(bf16[4,128,2048]{2,1,0:T(8,128)(2,1)} %get-tuple-element.114), calls=%async_computation.10 | async-start | bytes 4194304 | tf_op jit(solution)/shard_map/all_to_all | solution.py:43
  439.5 18.5 %collective-permute-start.17 = (bf16[4,128,384]{2,1,0:T(8,128)(2,1)S(1)}, bf16[4,128,384]{2,1,0:T(8,128)(2,1)S(1)}, u32[]{:S(2)}, u32[]{:S(2)}) collective-permute-start(bf16[4,128,384]{2,1,0:T(8,128)(2,1)S(1)} %copy-done.30), channel_id=1, source_target_pairs={{0,2},{2,64},{64,66},{66,0},{1,3},{3,65},{65,67},{67,1},{4,6},{6,6... | collective-permute-start | bytes 1179656 | tf_op jit(solution)/shard_map/ppermute | solution.py:55
  441.1 24.4 %collective-permute-start.18 = (bf16[4,128,384]{2,1,0:T(8,128)(2,1)}, bf16[4,128,384]{2,1,0:T(8,128)(2,1)}, u32[]{:S(2)}, u32[]{:S(2)}) collective-permute-start(bf16[4,128,384]{2,1,0:T(8,128)(2,1)} %get-tuple-element.122), channel_id=1, source_target_pairs={{0,66},{2,0},{64,2},{66,64},{1,67},{3,1},{65,3},{67,65},{4,70},{6,... | collective-permute-start | bytes 1179656 | tf_op jit(solution)/shard_map/ppermute | solution.py:55
  442.8 24.6 %collective-permute-start.19 = (bf16[4,128,384]{2,1,0:T(8,128)(2,1)}, bf16[4,128,384]{2,1,0:T(8,128)(2,1)}, u32[]{:S(2)}, u32[]{:S(2)}) collective-permute-start(bf16[4,128,384]{2,1,0:T(8,128)(2,1)} %get-tuple-element.123), channel_id=1, source_target_pairs={{0,64},{2,66},{64,0},{66,2},{1,65},{3,67},{65,1},{67,3},{4,68},{6,... | collective-permute-start | bytes 1179656 | tf_op jit(solution)/shard_map/ppermute | solution.py:55
  444.7 33.6 %collective-permute-start.23 = (bf16[4,128,384]{2,1,0:T(8,128)(2,1)}, bf16[4,128,384]{2,1,0:T(8,128)(2,1)S(1)}, u32[]{:S(2)}, u32[]{:S(2)}) collective-permute-start(bf16[4,128,384]{2,1,0:T(8,128)(2,1)} %get-tuple-element.129), channel_id=1, source_target_pairs={{0,4},{4,8},{8,12},{12,0},{1,5},{5,9},{9,13},{13,1},{2,6},{6,10},{... | collective-permute-start | bytes 1179656 | tf_op jit(solution)/shard_map/ppermute | solution.py:55
  446.4 32.6 %collective-permute-start.24 = (bf16[4,128,384]{2,1,0:T(8,128)(2,1)}, bf16[4,128,384]{2,1,0:T(8,128)(2,1)S(1)}, u32[]{:S(2)}, u32[]{:S(2)}) collective-permute-start(bf16[4,128,384]{2,1,0:T(8,128)(2,1)} %get-tuple-element.130), channel_id=1, source_target_pairs={{0,12},{4,0},{8,4},{12,8},{1,13},{5,1},{9,5},{13,9},{2,14},{6,2},{... | collective-permute-start | bytes 1179656 | tf_op jit(solution)/shard_map/ppermute | solution.py:55
  458.1 20.9 %collective-permute-start.25 = (bf16[4,128,384]{2,1,0:T(8,128)(2,1)}, bf16[4,128,384]{2,1,0:T(8,128)(2,1)S(1)}, u32[]{:S(2)}, u32[]{:S(2)}) collective-permute-start(bf16[4,128,384]{2,1,0:T(8,128)(2,1)} %get-tuple-element.131), channel_id=1, source_target_pairs={{0,8},{4,12},{8,0},{12,4},{1,9},{5,13},{9,1},{13,5},{2,10},{6,14},... | collective-permute-start | bytes 1179656 | tf_op jit(solution)/shard_map/ppermute | solution.py:55
  469.6 15.8 %collective-permute-start.20 = (bf16[128,384]{1,0:T(8,128)(2,1)}, bf16[128,384]{1,0:T(8,128)(2,1)S(1)}, u32[]{:S(2)}, u32[]{:S(2)}) collective-permute-start(bf16[128,384]{1,0:T(8,128)(2,1)} %get-tuple-element.125), channel_id=1, source_target_pairs={{0,4},{4,8},{8,12},{12,0},{1,5},{5,9},{9,13},{13,1},{2,6},{6,10},{... | collective-permute-start | bytes 294920 | tf_op jit(solution)/shard_map/ppermute | solution.py:55
  470.1 17.0 %collective-permute-start.21 = (bf16[128,384]{1,0:T(8,128)(2,1)}, bf16[128,384]{1,0:T(8,128)(2,1)S(1)}, u32[]{:S(2)}, u32[]{:S(2)}) collective-permute-start(bf16[128,384]{1,0:T(8,128)(2,1)} %get-tuple-element.126), channel_id=1, source_target_pairs={{0,12},{4,0},{8,4},{12,8},{1,13},{5,1},{9,5},{13,9},{2,14},{6,2},{... | collective-permute-start | bytes 294920 | tf_op jit(solution)/shard_map/ppermute | solution.py:55
  478.3 8.9 %collective-permute-start.22 = (bf16[128,384]{1,0:T(8,128)(2,1)}, bf16[128,384]{1,0:T(8,128)(2,1)S(1)}, u32[]{:S(2)}, u32[]{:S(2)}) collective-permute-start(bf16[128,384]{1,0:T(8,128)(2,1)} %get-tuple-element.127), channel_id=1, source_target_pairs={{0,8},{4,12},{8,0},{12,4},{1,9},{5,13},{9,1},{13,5},{2,10},{6,14},... | collective-permute-start | bytes 294920 | tf_op jit(solution)/shard_map/ppermute | solution.py:55
  482.2 9.1 %collective-permute-start.26 = (bf16[128,384]{1,0:T(8,128)(2,1)}, bf16[128,384]{1,0:T(8,128)(2,1)S(1)}, u32[]{:S(2)}, u32[]{:S(2)}) collective-permute-start(bf16[128,384]{1,0:T(8,128)(2,1)} %get-tuple-element.137), channel_id=1, source_target_pairs={{0,2},{2,64},{64,66},{66,0},{1,3},{3,65},{65,67},{67,1},{4,6},{6,6... | collective-permute-start | bytes 294920 | tf_op jit(solution)/shard_map/ppermute | solution.py:55
  482.9 8.4 %collective-permute-start.27 = (bf16[128,384]{1,0:T(8,128)(2,1)}, bf16[128,384]{1,0:T(8,128)(2,1)S(1)}, u32[]{:S(2)}, u32[]{:S(2)}) collective-permute-start(bf16[128,384]{1,0:T(8,128)(2,1)} %get-tuple-element.138), channel_id=1, source_target_pairs={{0,66},{2,0},{64,2},{66,64},{1,67},{3,1},{65,3},{67,65},{4,70},{6,... | collective-permute-start | bytes 294920 | tf_op jit(solution)/shard_map/ppermute | solution.py:55
  485.4 8.4 %collective-permute-start.28 = (bf16[128,384]{1,0:T(8,128)(2,1)}, bf16[128,384]{1,0:T(8,128)(2,1)S(1)}, u32[]{:S(2)}, u32[]{:S(2)}) collective-permute-start(bf16[128,384]{1,0:T(8,128)(2,1)} %get-tuple-element.139), channel_id=1, source_target_pairs={{0,64},{2,66},{64,0},{66,2},{1,65},{3,67},{65,1},{67,3},{4,68},{6,... | collective-permute-start | bytes 294920 | tf_op jit(solution)/shard_map/ppermute | solution.py:55
  (29 other events, 118.4 us)
Sparse Core Ops, SparseCore 0:
  10.8 67.4 all-gather.8
  80.0 35.2 all-gather.10
  133.6 81.1 all-gather.12
  308.3 31.5 all-gather.14
  342.2 29.6 reduce-scatter.2
  379.4 114.7 reduce-scatter.4

commit v2 on v1

--- a/solution.py
+++ b/solution.py
@@ -99,7 +99,9 @@
         w_ref[:128, j * 512 + 384 : j * 512 + 512] = out_t[:, pair]
     small_ref[...] = jnp.zeros_like(small_ref)
     small_ref[0:4, :128] = vectors_ref[...].astype(jnp.float32)
-    small_ref[8:11, :16] = bias_ref[...].astype(jnp.float32)
+    bias = bias_ref[...].astype(jnp.float32)
+    for part in range(3):
+        small_ref[8:9, part * 128 : part * 128 + 16] = bias[part : part + 1]
     w_ref[128:, :] = small_ref[...].astype(jnp.bfloat16)
 
 
@@ -161,11 +163,8 @@
 
 def qkv_kernel(
     unit_ref,
-    gain_ref,
-    shift_ref,
     w0_ref,
     w1_ref,
-    bias_ref,
     cos_ref,
     up_ref,
     down_ref,
@@ -174,11 +173,22 @@
     normed_rows,
 ):
     part = pl.program_id(1)
+    chips = [(z, i) for z in range(4) for i in range(4)]
+    extras = [w0_ref[z, 0, i, 128:144, :].astype(jnp.float32) for z, i in chips]
+
+    held = jnp.concatenate([rows[8:9] for rows in extras], 0).astype(jnp.bfloat16)
+    lane = lax.broadcasted_iota(jnp.int32, (128, 256), 1)
+    spread = lax.broadcasted_iota(jnp.int32, (128, 256), 0) == lane % 16
+    spread = mm(held, spread.astype(jnp.float32).astype(jnp.bfloat16))
+    owner = lax.broadcasted_iota(jnp.int32, (16, 256), 0) == lane[:16] // 16
+    bias = jnp.sum(jnp.where(owner, spread, 0.0), 0, keepdims=True)
 
     @pl.when((pl.program_id(0) == 0) & (part == 0))
     def _():
+        gain = jnp.concatenate([rows[0:1] for rows in extras], 1)
+        shift = jnp.concatenate([rows[1:2] for rows in extras], 1)
         for b in range(5):
-            normed = unit_ref[b].astype(jnp.float32) * gain_ref[...] + shift_ref[...]
+            normed = unit_ref[b].astype(jnp.float32) * gain + shift
             normed = normed.astype(jnp.bfloat16)
             if b < 4:
                 normed_ref[b] = normed
@@ -186,7 +196,7 @@
 
     def joint(rows):
         weights = [ref[:, 0, :, :128, :].reshape(D, 128) for ref in (w0_ref, w1_ref)]
-        return mm(normed_rows[:rows], jnp.concatenate(weights, 1)) + bias_ref[0, 0]
+        return mm(normed_rows[:rows], jnp.concatenate(weights, 1)) + bias
 
     def turned(value):
         rows = value.shape[0]
@@ -224,19 +234,15 @@
                 out_ref[0, j, 0, 1] = block[4]
 
 
-def qkv_call(unit, gain, shift, weights, bias, tables):
+def qkv_call(unit, weights, tables):
     table = pl.BlockSpec((640, 128), lambda h, p: (0, 0))
-    vector = pl.BlockSpec((1, D), lambda h, p: (0, 0))
     return pl.pallas_call(
         qkv_kernel,
         grid=(2, 3),
         in_specs=[
             pl.BlockSpec((5, 128, D), lambda h, p: (0, 0, 0)),
-            vector,
-            vector,
             pl.BlockSpec((4, 1, 4, 144, 128), lambda h, p: (0, h, 0, 0, p)),
             pl.BlockSpec((4, 1, 4, 144, 128), lambda h, p: (0, h, 0, 0, p + 4)),
-            pl.BlockSpec((1, 1, 1, 256), lambda h, p: (h, p, 0, 0)),
             table,
             table,
             table,
@@ -252,7 +258,7 @@
         scratch_shapes=[pltpu.VMEM((640, D), jnp.bfloat16)],
         compiler_params=pltpu.CompilerParams(vmem_limit_bytes=VMEM_LIMIT),
         cost_estimate=TINY,
-    )(unit, gain, shift, weights, weights, bias, *tables)
+    )(unit, weights, weights, *tables)
 
 
 def whole_call(kernel, out_shape, *operands, scratch=()):
@@ -944,10 +950,6 @@
     ring_cot = lax.all_gather(after(cotangent, ring), "x", axis=0)
     rest = pack_hidden_call(w_gate.T, w_up.T, w_down)
 
-    small = joint_w[:, :, :, 128:, :128].astype(jnp.float32)
-    bias = small[:, :, :, 8:11, :16].transpose(1, 3, 0, 2, 4).reshape(2, 3, 1, 256)
-    vectors = small[:, 0, :, :4].transpose(2, 0, 1, 3).reshape(4, D)
-    gain_one, shift_one, gain_two, shift_two = [vectors[i : i + 1] for i in range(4)]
 
     first_block = jnp.sum((doc_ids[None, :] < doc_ids[:, None]).astype(jnp.int32), axis=1)
     cycles = jnp.arange(4, dtype=jnp.int32) * 16 + half * 64 + blk
@@ -959,8 +961,10 @@
     lo = lax.dynamic_slice(first_block, (first_query,), (16,)) - (first_query - 16)
 
     unit_one = unit_call(ring, before)
-    payload, normed_one = qkv_call(unit_one, gain_one, shift_one, joint_w, bias, tables)
+    payload, normed_one = qkv_call(unit_one, joint_w, tables)
     out_w, payload = lax.optimization_barrier((joint_w, payload))
+    vectors = out_w[:, 0, :, 128:132, :128].astype(jnp.float32).transpose(2, 0, 1, 3).reshape(4, D)
+    gain_one, _, gain_two, shift_two = [vectors[i : i + 1] for i in range(4)]
     own_rows = out_rows_call(place, out_w)
     near_rows = [send(own_rows, ("x",), t) for t in (1, 3)]
     blocks = after(exchange(payload.reshape(16, 5, 128, 128), BLK), near_rows)

time: 516 us -> 514 us (level)
  Pallas kernels: 167 us -> 182 us
  starting transfers between devices: 83.1 us -> 73.3 us
    pallas_call x1, Pallas kernels: 14.3 us -> 22.4 us  [attend_back_call(): pl.pallas_call(attend_back_kernel, in_specs=[pl.BlockSpec(memory_space=pl...]
    all_to_all x10, starting transfers between devices: 50.4 us -> 42.9 us  [exchange(): return lax.all_to_all(parts, axes, 0, 0, tiled=True)]
    ppermute x1, waiting for transfers between devices: 20.6 us -> 13.2 us  [local(): halo_back = lax.ppermute(back[0, :, :, :2], ('yh',), [(1, 0)])]
    pallas_call x1, Pallas kernels: 11.3 us -> 17.5 us  [attend_call(): pl.pallas_call(attend_kernel, in_specs=[pl.BlockSpec(memory_space=pltpu.S...]
  transfers between devices with their start and end apart: 45 -> 45, of which waited for: 19 -> 20; matrix products, arithmetic and copies ran while one was open for 4% -> 4% of each run, Pallas kernels for 30% -> 33%
where the time goes in v2:
time: 514 us; the launch traced here: 504 us
  waiting for transfers between devices  190 us (37%)
  Pallas kernels  182 us (35%)
  starting transfers between devices  73.3 us (14%)
  local copies, waits for them, and re-layouts  21.2 us (4%)
  between operations  15.1 us (3%)
  blocking collectives  14 us (3%)
  other arithmetic  9.37 us (2%)
    all_to_all x10, waiting for transfers between devices, exchange(): return lax.all_to_all(parts, axes, 0, 0, tiled=True)  99.8 us
    ppermute x15, waiting for transfers between devices, send(): return lax.ppermute(value, axes, [(i, (i + step) % 4) for i in range(4)])  52.3 us
    all_to_all x10, starting transfers between devices, exchange(): return lax.all_to_all(parts, axes, 0, 0, tiled=True)  42.9 us
    pallas_call x1, Pallas kernels, feed_forward_call(): pl.pallas_call(feed_forward_kernel, grid=(2,), in_specs=[tokens_once, tok...  30.4 us
    pallas_call x3, Pallas kernels, plane_grad_call(): pl.pallas_call(plane_grad_kernel, grid=(columns // 256, 2), in_specs=[pl....  30 us
    pallas_call x1, Pallas kernels, attend_back_call(): pl.pallas_call(attend_back_kernel, in_specs=[pl.BlockSpec(memory_space=pl...  22.4 us
    ppermute x15, starting transfers between devices, send(): return lax.ppermute(value, axes, [(i, (i + step) % 4) for i in range(4)])  21.4 us
    ppermute x1, waiting for transfers between devices, local(): before = lax.ppermute(ring[3], ('yh',), [(0, 1)])  20.5 us
  transfers between devices with their start and end apart: 45, of which 20 were waited for; matrix products, arithmetic and copies ran while one was open for 4% of the time, Pallas kernels for 33%

profile of v2, /device:TPU:0, one launch (start us, length us, event | category | flops | bytes accessed | tf_op | source)
XLA Modules:
  0.0 504.5 jit_solution(4486778915817924977)
XLA Ops:
  10.3 2.6 broadcast_in_dim.57
  12.9 4.5 all-to-all-start
  18.6 25.2 %all-to-all-done.x_ref = bf16[4,128,2048]{2,1,0:T(8,128)(2,1)S(1)} async-done(((bf16[4,128,2048]{2,1,0:T(8,128)(2,1)}), bf16[4,128,2048]{2,1,0:T(8,128)(2,1)S(1)}, u32[]{:S(2)}, u32[]{:S(2)}) %all-to-all-start) | async-done | bytes 2097184 | tf_op jit(solution)/shard_map/all_to_all | solution.py:43
  43.8 5.1 %collective-permute-start = (bf16[128,2048]{1,0:T(8,128)(2,1)S(1)}, bf16[128,2048]{1,0:T(8,128)(2,1)S(1)}, u32[]{:S(2)}, u32[]{:S(2)}) collective-permute-start(bf16[128,2048]{1,0:T(8,128)(2,1)S(1)} %slice_bitcast_fusion), channel_id=1, source_target_pairs={{0,64},{1,65},{2,66},{3,67},{4,68},{5,69},{6,70},{7,71},{8,72},{9,... | collective-permute-start | bytes 1572872 | tf_op jit(solution)/shard_map/ppermute | solution.py:949
  51.2 20.5 %collective-permute-done.before_ref = bf16[128,2048]{1,0:T(8,128)(2,1)S(1)} collective-permute-done((bf16[128,2048]{1,0:T(8,128)(2,1)S(1)}, bf16[128,2048]{1,0:T(8,128)(2,1)S(1)}, u32[]{:S(2)}, u32[]{:S(2)}) %collective-permute-start) | collective-permute-done | bytes 524320 | tf_op jit(solution)/shard_map/ppermute | solution.py:949
  72.4 5.3 %shard_map.221.unit_ref = bf16[5,128,2048]{2,1,0:T(8,128)(2,1)} custom-call(bf16[4,128,2048]{2,1,0:T(8,128)(2,1)} %copy-done.3, bf16[128,2048]{1,0:T(8,128)(2,1)} %copy-done.15), custom_call_target="tpu_custom_call" | custom-call | flops 1 | bytes 1 | tf_op jit(solution)/shard_map/pallas_call | solution.py:150
  78.4 13.0 %shard_map.222 = (bf16[4,2,2,5,128,128]{5,4,3,2,1,0:T(8,128)(2,1)}, bf16[4,128,2048]{2,1,0:T(8,128)(2,1)}) custom-call(bf16[5,128,2048]{2,1,0:T(8,128)(2,1)} %shard_map.221.unit_ref, bf16[4,2,4,144,1024]{4,3,2,1,0:T(8,128)(2,1)} %bitcast.55, bf16[4,2,4,144,1024]{4,3,2,1,0:T(8,128)(2,1)} %bitcast.56, f32[640,128]{1,0:T(8,128)} %get-tuple-element.151.cos_ref, ...), custom_call_target="tpu_custom_call" | custom-call | flops 1 | bytes 1 | tf_op jit(solution)/shard_map/pallas_call | solution.py:239
  91.4 4.8 all-to-all-start.1
  96.9 3.7 shard_map.223.refs_0_
  105.9 27.6 %collective-permute-done.1.refs_1_ = bf16[8,128,512]{2,1,0:T(8,128)(2,1)} collective-permute-done((bf16[8,128,512]{2,1,0:T(8,128)(2,1)}, bf16[8,128,512]{2,1,0:T(8,128)(2,1)}, u32[]{:S(2)}, u32[]{:S(2)}) %collective-permute-start.1) | collective-permute-done | bytes 1048608 | tf_op jit(solution)/shard_map/ppermute | solution.py:55
  136.0 17.5 %shard_map.224 = (f32[16,128,128]{2,1,0:T(8,128)}, bf16[16,128,128]{2,1,0:T(8,128)(2,1)}, f32[8,1,512]{2,1,0:T(1,128)}) custom-call(s32[16]{0:T(128)} %dynamic-slice_subtract_fusion.lo_ref, bf16[16,5,128,128]{3,2,1,0:T(8,128)(2,1)} %copy-done), custom_call_target="tpu_custom_call" | custom-call | flops 1 | bytes 1 | tf_op jit(solution)/shard_map/pallas_call | solution.py:751
  153.5 5.3 %all-to-all-start.2 = ((bf16[16,128,128]{2,1,0:T(8,128)(2,1)}), bf16[16,128,128]{2,1,0:T(8,128)(2,1)}, u32[]{:S(2)}, u32[]{:S(2)}) async-start(bf16[16,128,128]{2,1,0:T(8,128)(2,1)} %get-tuple-element.83), calls=%async_computation.2 | async-start | bytes 1048576 | tf_op jit(solution)/shard_map/all_to_all | solution.py:43
  159.6 10.0 %all-to-all-done.2 = bf16[16,128,128]{2,1,0:T(8,128)(2,1)} async-done(((bf16[16,128,128]{2,1,0:T(8,128)(2,1)}), bf16[16,128,128]{2,1,0:T(8,128)(2,1)}, u32[]{:S(2)}, u32[]{:S(2)}) %all-to-all-start.2) | async-done | bytes 524320 | tf_op jit(solution)/shard_map/all_to_all | solution.py:43
  169.7 4.1 all-to-all-start.3
  175.3 9.1 %all-to-all-done.3.att_ref = bf16[4,2,2,128,128]{4,3,2,1,0:T(8,128)(2,1)} async-done(((bf16[4,2,2,128,128]{4,3,2,1,0:T(8,128)(2,1)}), bf16[4,2,2,128,128]{4,3,2,1,0:T(8,128)(2,1)}, u32[]{:S(2)}, u32[]{:S(2)}) %all-to-all-start.3) | async-done | bytes 524320 | tf_op jit(solution)/shard_map/all_to_all | solution.py:43
  184.4 8.6 %shard_map.225 = (f32[128,2048]{1,0:T(8,128)}, bf16[4,128,2048]{2,1,0:T(8,128)(2,1)}) custom-call(s32[2]{0:T(128)} %pad_add_fusion.1.place_ref, bf16[4,2,2,128,128]{4,3,2,1,0:T(8,128)(2,1)} %all-to-all-done.3.att_ref, bf16[128,2048]{1,0:T(8,128)(2,1)} %tokens_ref.3, f32[1,2048]{1,0:T(1,128)} %bitcast.79, f32[1,2048]{1,0:T(1,128)} %bitcast.82, ...), custom_call_target="tpu_custom_call" | custom-call | flops 1 | bytes 1 | tf_op jit(solution)/shard_map/pallas_call | solution.py:378
  193.0 3.6 all-to-all-start.4
  196.9 26.3 %all-to-all-done.4.x_ref.left_ref = bf16[4,128,2048]{2,1,0:T(8,128)(2,1)S(1)} async-done(((bf16[4,128,2048]{2,1,0:T(8,128)(2,1)}), bf16[4,128,2048]{2,1,0:T(8,128)(2,1)S(1)}, u32[]{:S(2)}, u32[]{:S(2)}) %all-to-all-start.4) | async-done | bytes 2097184 | tf_op jit(solution)/shard_map/all_to_all | solution.py:43
  224.6 30.4 %shard_map.227 = (bf16[2,512,768]{2,1,0:T(8,128)(2,1)}, bf16[2,512,1536]{2,1,0:T(8,128)(2,1)}, bf16[4,128,2048]{2,1,0:T(8,128)(2,1)}, bf16[4,128,2048]{2,1,0:T(8,128)(2,1)}) custom-call(bf16[4,128,2048]{2,1,0:T(8,128)(2,1)} %copy-done.1, bf16[4,128,2048]{2,1,0:T(8,128)(2,1)} %bitcast.66, bf16[4,2,512,2304]{3,2,1,0:T(8,128)(2,1)} %bitcast.61, ...), custom_call_target="tpu_custom_call" | custom-call | flops 1 | bytes 1 | tf_op jit(solution)/shard_map/pallas_call | solution.py:505
  255.1 3.6 all-to-all-start.5
  258.8 9.3 %shard_map.228.refs_0_ = bf16[2,2,4,128,2560]{4,3,2,1,0:T(8,128)(2,1)} custom-call(s32[1]{0:T(128)} %bitcast.1.core_ref, bf16[4,128,2048]{2,1,0:T(8,128)(2,1)} %bitcast.67, bf16[4,128,2048]{2,1,0:T(8,128)(2,1)} %collective-permute-done.8.left_other_ref, bf16[2,512,768]{2,1,0:T(8,128)(2,1)} %get-tuple-element.92.right_ref, ...), custom_call_target="tpu_custom_call" | custom-call | flops 1 | bytes 1 | tf_op jit(solution)/shard_map/pallas_call | solution.py:546
  268.2 17.8 %all-to-all-done.5.came_ref = bf16[4,128,2048]{2,1,0:T(8,128)(2,1)S(1)} async-done(((bf16[4,128,2048]{2,1,0:T(8,128)(2,1)}), bf16[4,128,2048]{2,1,0:T(8,128)(2,1)S(1)}, u32[]{:S(2)}, u32[]{:S(2)}) %all-to-all-start.5) | async-done | bytes 2097184 | tf_op jit(solution)/shard_map/all_to_all | solution.py:43
  287.3 9.0 %shard_map.229 = (f32[128,2048]{1,0:T(8,128)}, bf16[128,2048]{1,0:T(8,128)(2,1)}, f32[1,2048]{1,0:T(1,128)}, f32[1,2048]{1,0:T(1,128)}, bf16[4,2,2,128,128]{4,3,2,1,0:T(8,128)(2,1)}) custom-call(s32[2]{0:T(128)} %pad_add_fusion.1.place_ref, bf16[4,128,2048]{2,1,0:T(8,128)(2,1)} %copy-done.5, f32[128,2048]{1,0:T(8,128)} %get-tuple-element.86.middle_ref, ...), custom_call_target="tpu_custom_call" | custom-call | flops 1 | bytes 1 | tf_op jit(solution)/shard_map/pallas_call | solution.py:439
  296.3 14.0 %all_to_all.59 = bf16[4,2,2,128,128]{4,3,2,1,0:T(8,128)(2,1)} all-to-all(bf16[4,2,2,128,128]{4,3,2,1,0:T(8,128)(2,1)} %get-tuple-element.94), channel_id=1, replica_groups=mesh['yh'=2,'x'=4,'z'=4,'yl'=2,'k'=2] {'x'}, dimensions={0} | all-to-all | bytes 1048576 | tf_op jit(solution)/shard_map/all_to_all | solution.py:43
  310.5 3.6 all-to-all-start.7
  316.2 4.2 shard_map.230.left_ref
  320.4 4.5 all-to-all-done.7.do_ref
  325.7 22.4 %shard_map.231 = bf16[16,5,128,128]{3,2,1,0:T(8,128)(2,1)} custom-call(s32[16]{0:T(128)} %dynamic-slice_subtract_fusion.lo_ref, bf16[16,5,128,128]{3,2,1,0:T(8,128)(2,1)} %copy-done, bf16[16,128,128]{2,1,0:T(8,128)(2,1)} %copy-done.12, f32[16,128,128]{2,1,0:T(8,128)} %get-tuple-element.98.o32_ref, f32[8,1,512]{2,1,0:T(1,128)} %get-tuple-element.99.lse_ref), custom_call_target="tpu_custom_call" | custom-call | flops 1 | bytes 1 | tf_op jit(solution)/shard_map/pallas_call | solution.py:815
  348.1 4.6 all-to-all-start.8
  355.6 2.2 collective-permute-done.13.left_other_ref
  357.8 15.4 %shard_map.232.refs_0_ = bf16[2,2,4,128,2560]{4,3,2,1,0:T(8,128)(2,1)} custom-call(s32[1]{0:T(128)} %bitcast.1.core_ref, bf16[4,128,2048]{2,1,0:T(8,128)(2,1)} %copy-done.1, bf16[4,128,2048]{2,1,0:T(8,128)(2,1)} %collective-permute-done.13.left_other_ref, bf16[2,512,1536]{2,1,0:T(8,128)(2,1)} %get-tuple-element.106.right_ref, ...), custom_call_target="tpu_custom_call", output_to_operand_aliasing={{}: (5, {})} | custom-call | flops 1 | bytes 1 | tf_op jit(solution)/shard_map/pallas_call | solution.py:546
  374.0 5.3 %shard_map.233 = bf16[2,2,4,128,2560]{4,3,2,1,0:T(8,128)(2,1)} custom-call(s32[1]{0:T(128)} %bitcast.1.core_ref, bf16[4,128,2048]{2,1,0:T(8,128)(2,1)} %bitcast.70, bf16[4,128,2048]{2,1,0:T(8,128)(2,1)} %collective-permute-done.11.left_other_ref, bf16[2,512,256]{2,1,0:T(8,128)(2,1)} %copy-done.11, ...), custom_call_target="tpu_custom_call", output_to_operand_aliasing={{}: (5, {})} | custom-call | flops 1 | bytes 1 | tf_op jit(solution)/shard_map/pallas_call | solution.py:546
  379.3 6.9 %all-to-all-done.8 = bf16[16,5,128,128]{3,2,1,0:T(8,128)(2,1)} async-done(((bf16[16,5,128,128]{3,2,1,0:T(8,128)(2,1)}), bf16[16,5,128,128]{3,2,1,0:T(8,128)(2,1)}, u32[]{:S(2)}, u32[]{:S(2)}) %all-to-all-start.8) | async-done | bytes 2621472 | tf_op jit(solution)/shard_map/all_to_all | solution.py:43
  390.6 13.2 %collective-permute-done.15.halo_ref = bf16[2,2,2,128,128]{4,3,2,1,0:T(8,128)(2,1)S(1)} collective-permute-done((bf16[2,2,2,128,128]{4,3,2,1,0:T(8,128)(2,1)S(1)}, bf16[2,2,2,128,128]{4,3,2,1,0:T(8,128)(2,1)S(1)}, u32[]{:S(2)}, u32[]{:S(2)}) %collective-permute-start.15) | collective-permute-done | bytes 262176 | tf_op jit(solution)/shard_map/ppermute | solution.py:1006
  404.5 3.7 shard_map.234
  408.6 9.1 %shard_map.235 = (bf16[4,128,2048]{2,1,0:T(8,128)(2,1)}, f32[1,2048]{1,0:T(1,128)}, f32[1,2048]{1,0:T(1,128)}) custom-call(bf16[2,512,768]{2,1,0:T(8,128)(2,1)} %get-tuple-element.111.g_ref.right_ref, bf16[5,128,2048]{2,1,0:T(8,128)(2,1)} %shard_map.221.unit_ref, bf16[4,2,4,144,1024]{4,3,2,1,0:T(8,128)(2,1)} %bitcast.60), custom_call_target="tpu_custom_call" | custom-call | flops 1 | bytes 1 | tf_op jit(solution)/shard_map/pallas_call | solution.py:906
  420.1 4.8 all-to-all-start.10
  426.7 8.5 %shard_map.236 = (bf16[4,128,384]{2,1,0:T(8,128)(2,1)}, bf16[4,128,384]{2,1,0:T(8,128)(2,1)}, bf16[4,128,384]{2,1,0:T(8,128)(2,1)}, bf16[4,128,384]{2,1,0:T(8,12...) custom-call(s32[4,16]{1,0:T(4,128)} %pad_add_fusion.place_ref, ...), custom_call_target="tpu_custom_call" | custom-call | flops 1 | bytes 1 | tf_op jit(solution)/shard_map/pallas_call | solution.py:602
  435.3 3.9 all-to-all-start.9
  447.8 13.5 %collective-permute-done.17.b_ref = bf16[4,128,384]{2,1,0:T(8,128)(2,1)S(1)} collective-permute-done((bf16[4,128,384]{2,1,0:T(8,128)(2,1)S(1)}, bf16[4,128,384]{2,1,0:T(8,128)(2,1)S(1)}, u32[]{:S(2)}, u32[]{:S(2)}) %collective-permute-start.17) | collective-permute-done | bytes 393248 | tf_op jit(solution)/shard_map/ppermute | solution.py:55
  461.3 5.1 %collective-permute-done.19.d_ref = bf16[4,128,384]{2,1,0:T(8,128)(2,1)} collective-permute-done((bf16[4,128,384]{2,1,0:T(8,128)(2,1)}, bf16[4,128,384]{2,1,0:T(8,128)(2,1)}, u32[]{:S(2)}, u32[]{:S(2)}) %collective-permute-start.19) | collective-permute-done | bytes 393248 | tf_op jit(solution)/shard_map/ppermute | solution.py:55
  466.4 2.2 shard_map.238
  469.6 2.5 collective-permute-start.21
  473.5 3.9 shard_map.237
  480.4 2.2 shard_map.239
  483.6 2.3 collective-permute-start.27
  489.4 2.8 collective-permute-done.28.refs_7_
  494.9 2.3 shard_map.241
  (185 shorter events, 59.2 us)
Async XLA Ops:
  7.2 71.2 %all-gather.9.cloned.1.call-start = ((), (), s32[]{:S(2)}) async-start(), calls=%async_computation.15 | async-start | bytes 9732096 | tf_op jit(solution)/shard_map/all_gather | solution.py:946
  12.9 30.8 %all-to-all-start = ((bf16[4,128,2048]{2,1,0:T(8,128)(2,1)}), bf16[4,128,2048]{2,1,0:T(8,128)(2,1)S(1)}, u32[]{:S(2)}, u32[]{:S(2)}) async-start(bf16[4,128,2048]{2,1,0:T(8,128)(2,1)} %broadcast_in_dim.57), calls=%async_computation | async-start | bytes 4194304 | tf_op jit(solution)/shard_map/all_to_all | solution.py:43
  17.4 179.2 %all-gather.11.cloned.1.call-start = ((), (), s32[]{:S(2)}) async-start(), calls=%async_computation.16 | async-start | bytes 2621440 | tf_op jit(solution)/shard_map/all_gather | solution.py:950
  43.7 27.9 %copy-start.3 = (bf16[4,128,2048]{2,1,0:T(8,128)(2,1)}, bf16[4,128,2048]{2,1,0:T(8,128)(2,1)S(1)}, u32[]{:S(2)}) copy-start(bf16[4,128,2048]{2,1,0:T(8,128)(2,1)S(1)} %all-to-all-done.x_ref) | copy-start | bytes 6291460
  43.8 27.8 %collective-permute-start = (bf16[128,2048]{1,0:T(8,128)(2,1)S(1)}, bf16[128,2048]{1,0:T(8,128)(2,1)S(1)}, u32[]{:S(2)}, u32[]{:S(2)}) collective-permute-start(bf16[128,2048]{1,0:T(8,128)(2,1)S(1)} %slice_bitcast_fusion), channel_id=1, source_target_pairs={{0,64},{1,65},{2,66},{3,67},{4,68},{5,69},{6,70},{7,71},{8,72},{9,... | collective-permute-start | bytes 1572872 | tf_op jit(solution)/shard_map/ppermute | solution.py:949
  91.4 42.1 %all-to-all-start.1 = ((bf16[16,5,128,128]{3,2,1,0:T(8,128)(2,1)}), bf16[16,5,128,128]{3,2,1,0:T(8,128)(2,1)S(1)}, u32[]{:S(2)}, u32[]{:S(2)}) async-start(bf16[16,5,128,128]{3,2,1,0:T(8,128)(2,1)} %bitcast.68), calls=%async_computation.1 | async-start | bytes 5242880 | tf_op jit(solution)/shard_map/all_to_all | solution.py:43
  96.2 127.0 %all-gather.13.cloned.1.call-start = ((), (), s32[]{:S(2)}) async-start(), calls=%async_computation.17 | async-start | bytes 19464192 | tf_op jit(solution)/shard_map/all_gather | solution.py:971
  100.6 32.9 %collective-permute-start.1 = (bf16[8,128,512]{2,1,0:T(8,128)(2,1)}, bf16[8,128,512]{2,1,0:T(8,128)(2,1)}, u32[]{:S(2)}, u32[]{:S(2)}) collective-permute-start(bf16[8,128,512]{2,1,0:T(8,128)(2,1)} %shard_map.223.refs_0_), channel_id=1, source_target_pairs={{0,16},{16,32},{32,48},{48,0},{1,17},{17,33},{33,49},{49,1},{2,18}... | collective-permute-start | bytes 3145736 | tf_op jit(solution)/shard_map/ppermute | solution.py:55
  101.9 31.7 %collective-permute-start.2 = (bf16[8,128,512]{2,1,0:T(8,128)(2,1)}, bf16[8,128,512]{2,1,0:T(8,128)(2,1)}, u32[]{:S(2)}, u32[]{:S(2)}) collective-permute-start(bf16[8,128,512]{2,1,0:T(8,128)(2,1)} %shard_map.223.refs_0_), channel_id=1, source_target_pairs={{0,48},{16,0},{32,16},{48,32},{1,49},{17,1},{33,17},{49,33},{2,50}... | collective-permute-start | bytes 3145736 | tf_op jit(solution)/shard_map/ppermute | solution.py:55
  133.5 36.1 %collective-permute-start.3 = (bf16[8,128,512]{2,1,0:T(8,128)(2,1)}, bf16[8,128,512]{2,1,0:T(8,128)(2,1)}, u32[]{:S(2)}, u32[]{:S(2)}) collective-permute-start(bf16[8,128,512]{2,1,0:T(8,128)(2,1)} %shard_map.223.refs_0_), channel_id=1, source_target_pairs={{0,32},{16,48},{32,0},{48,16},{1,33},{17,49},{33,1},{49,17},{2,34}... | collective-permute-start | bytes 3145736 | tf_op jit(solution)/shard_map/ppermute | solution.py:55
  153.5 16.2 %all-to-all-start.2 = ((bf16[16,128,128]{2,1,0:T(8,128)(2,1)}), bf16[16,128,128]{2,1,0:T(8,128)(2,1)}, u32[]{:S(2)}, u32[]{:S(2)}) async-start(bf16[16,128,128]{2,1,0:T(8,128)(2,1)} %get-tuple-element.83), calls=%async_computation.2 | async-start | bytes 1048576 | tf_op jit(solution)/shard_map/all_to_all | solution.py:43
  158.8 16.5 %collective-permute-start.4 = (bf16[8,128,512]{2,1,0:T(8,128)(2,1)}, bf16[8,128,512]{2,1,0:T(8,128)(2,1)S(1)}, u32[]{:S(2)}, u32[]{:S(2)}) collective-permute-start(bf16[8,128,512]{2,1,0:T(8,128)(2,1)} %shard_map.223.refs_0_), channel_id=1, source_target_pairs={{0,1},{1,0},{2,3},{3,2},{4,5},{5,4},{6,7},{7,6},{8,9},{9,8},{10,11... | collective-permute-start | bytes 3145736 | tf_op jit(solution)/shard_map/ppermute | solution.py:39
  159.1 16.1 %collective-permute-start.5 = (bf16[8,128,512]{2,1,0:T(8,128)(2,1)}, bf16[8,128,512]{2,1,0:T(8,128)(2,1)S(1)}, u32[]{:S(2)}, u32[]{:S(2)}) collective-permute-start(bf16[8,128,512]{2,1,0:T(8,128)(2,1)} %collective-permute-done.1.refs_1_), channel_id=1, source_target_pairs={{0,1},{1,0},{2,3},{3,2},{4,5},{5,4},{6,7},{7,6},{8,9},{9,8},{10,11... | collective-permute-start | bytes 3145736 | tf_op jit(solution)/shard_map/ppermute | solution.py:39
  159.4 15.9 %collective-permute-start.7 = (bf16[8,128,512]{2,1,0:T(8,128)(2,1)}, bf16[8,128,512]{2,1,0:T(8,128)(2,1)S(1)}, u32[]{:S(2)}, u32[]{:S(2)}) collective-permute-start(bf16[8,128,512]{2,1,0:T(8,128)(2,1)} %collective-permute-done.2.refs_3_), channel_id=1, source_target_pairs={{0,1},{1,0},{2,3},{3,2},{4,5},{5,4},{6,7},{7,6},{8,9},{9,8},{10,11... | collective-permute-start | bytes 3145736 | tf_op jit(solution)/shard_map/ppermute | solution.py:39
  169.7 14.7 %collective-permute-start.6 = (bf16[8,128,512]{2,1,0:T(8,128)(2,1)}, bf16[8,128,512]{2,1,0:T(8,128)(2,1)}, u32[]{:S(2)}, u32[]{:S(2)}) collective-permute-start(bf16[8,128,512]{2,1,0:T(8,128)(2,1)} %collective-permute-done.3.refs_2_), channel_id=1, source_target_pairs={{0,1},{1,0},{2,3},{3,2},{4,5},{5,4},{6,7},{7,6},{8,9},{9,8},{10,11... | collective-permute-start | bytes 3145736 | tf_op jit(solution)/shard_map/ppermute | solution.py:39
  169.7 14.7 %all-to-all-start.3 = ((bf16[4,2,2,128,128]{4,3,2,1,0:T(8,128)(2,1)}), bf16[4,2,2,128,128]{4,3,2,1,0:T(8,128)(2,1)}, u32[]{:S(2)}, u32[]{:S(2)}) async-start(bf16[4,2,2,128,128]{4,3,2,1,0:T(8,128)(2,1)} %bitcast.15), calls=%async_computation.3 | async-start | bytes 1048576 | tf_op jit(solution)/shard_map/all_to_all | solution.py:43
  193.0 30.2 %all-to-all-start.4 = ((bf16[4,128,2048]{2,1,0:T(8,128)(2,1)}), bf16[4,128,2048]{2,1,0:T(8,128)(2,1)S(1)}, u32[]{:S(2)}, u32[]{:S(2)}) async-start(bf16[4,128,2048]{2,1,0:T(8,128)(2,1)} %get-tuple-element.87), calls=%async_computation.4 | async-start | bytes 4194304 | tf_op jit(solution)/shard_map/all_to_all | solution.py:43
  196.6 62.1 %collective-permute-start.8 = (bf16[4,128,2048]{2,1,0:T(8,128)(2,1)}, bf16[4,128,2048]{2,1,0:T(8,128)(2,1)}, u32[]{:S(2)}, u32[]{:S(2)}) collective-permute-start(bf16[4,128,2048]{2,1,0:T(8,128)(2,1)} %bitcast.65), channel_id=1, source_target_pairs={{0,1},{1,0},{2,3},{3,2},{4,5},{5,4},{6,7},{7,6},{8,9},{9,8},{10,11... | collective-permute-start | bytes 6291464 | tf_op jit(solution)/shard_map/ppermute | solution.py:39
  255.0 3.8 collective-permute-start.9
  255.1 30.8 %all-to-all-start.5 = ((bf16[4,128,2048]{2,1,0:T(8,128)(2,1)}), bf16[4,128,2048]{2,1,0:T(8,128)(2,1)S(1)}, u32[]{:S(2)}, u32[]{:S(2)}) async-start(bf16[4,128,2048]{2,1,0:T(8,128)(2,1)} %get-tuple-element.91), calls=%async_computation.5 | async-start | bytes 4194304 | tf_op jit(solution)/shard_map/all_to_all | solution.py:43
  258.7 94.4 %all-gather.15.cloned.1.call-start = ((), (), s32[]{:S(2)}) async-start(), calls=%async_computation.18 | async-start | bytes 2621440 | tf_op jit(solution)/shard_map/all_gather | solution.py:989
  310.4 4.5 collective-permute-start.10
  310.5 14.4 %all-to-all-start.7 = ((bf16[16,128,128]{2,1,0:T(8,128)(2,1)}), bf16[16,128,128]{2,1,0:T(8,128)(2,1)S(1)}, u32[]{:S(2)}, u32[]{:S(2)}) async-start(bf16[16,128,128]{2,1,0:T(8,128)(2,1)} %bitcast.25), calls=%async_computation.7 | async-start | bytes 1048576 | tf_op jit(solution)/shard_map/all_to_all | solution.py:43
  314.1 72.2 %reduce-scatter.3.cloned.1.call-start = ((), (), s32[]{:S(2)}) async-start(), calls=%async_computation.13 | async-start | bytes 2621440 | tf_op jit(solution)/shard_map/reduce_scatter | solution.py:994
  324.9 32.9 %collective-permute-start.14 = (bf16[2,512,1536]{2,1,0:T(8,128)(2,1)}, bf16[2,512,1536]{2,1,0:T(8,128)(2,1)}, u32[]{:S(2)}, u32[]{:S(2)}) collective-permute-start(bf16[2,512,1536]{2,1,0:T(8,128)(2,1)} %get-tuple-element.106.right_ref), channel_id=1, source_target_pairs={{0,1},{1,0},{2,3},{3,2},{4,5},{5,4},{6,7},{7,6},{8,9},{9,8},{10,11... | collective-permute-start | bytes 9437192 | tf_op jit(solution)/shard_map/ppermute | solution.py:39
  348.1 38.1 %all-to-all-start.8 = ((bf16[16,5,128,128]{3,2,1,0:T(8,128)(2,1)}), bf16[16,5,128,128]{3,2,1,0:T(8,128)(2,1)}, u32[]{:S(2)}, u32[]{:S(2)}) async-start(bf16[16,5,128,128]{3,2,1,0:T(8,128)(2,1)} %shard_map.231), calls=%async_computation.9 | async-start | bytes 5242880 | tf_op jit(solution)/shard_map/all_to_all | solution.py:43
  352.7 142.2 %reduce-scatter.5.cloned.1.call-start = ((), (), s32[]{:S(2)}) async-start(), calls=%async_computation.14 | async-start | bytes 11141120 | tf_op jit(solution)/shard_map/reduce_scatter | solution.py:649
  352.8 5.0 collective-permute-start.13
  353.1 20.1 %collective-permute-start.11 = (bf16[4,128,2048]{2,1,0:T(8,128)(2,1)}, bf16[4,128,2048]{2,1,0:T(8,128)(2,1)}, u32[]{:S(2)}, u32[]{:S(2)}) collective-permute-start(bf16[4,128,2048]{2,1,0:T(8,128)(2,1)} %bitcast.69), channel_id=1, source_target_pairs={{0,1},{1,0},{2,3},{3,2},{4,5},{5,4},{6,7},{7,6},{8,9},{9,8},{10,11... | collective-permute-start | bytes 6291464 | tf_op jit(solution)/shard_map/ppermute | solution.py:39
  355.3 17.9 %copy-start.11 = (bf16[2,512,256]{2,1,0:T(8,128)(2,1)}, bf16[2,512,256]{2,1,0:T(8,128)(2,1)S(1)}, u32[]{:S(2)}) copy-start(bf16[2,512,256]{2,1,0:T(8,128)(2,1)S(1)} %reshape.366.right_ref) | copy-start | bytes 1572868
  355.3 17.9 %collective-permute-start.12 = (bf16[2,512,256]{2,1,0:T(8,128)(2,1)S(1)}, bf16[2,512,256]{2,1,0:T(8,128)(2,1)S(1)}, u32[]{:S(2)}, u32[]{:S(2)}) collective-permute-start(bf16[2,512,256]{2,1,0:T(8,128)(2,1)S(1)} %reshape.366.right_ref), channel_id=1, source_target_pairs={{0,1},{1,0},{2,3},{3,2},{4,5},{5,4},{6,7},{7,6},{8,9},{9,8},{10,11... | collective-permute-start | bytes 1572872 | tf_op jit(solution)/shard_map/ppermute | solution.py:39
  387.3 16.5 %collective-permute-start.15 = (bf16[2,2,2,128,128]{4,3,2,1,0:T(8,128)(2,1)S(1)}, bf16[2,2,2,128,128]{4,3,2,1,0:T(8,128)(2,1)S(1)}, u32[]{:S(2)}, u32[]{:S(2)}) collective-permute-start(bf16[2,2,2,128,128]{4,3,2,1,0:T(8,128)(2,1)S(1)} %slice_bitcast_fusion.1), channel_id=1, source_target_pairs={{64,0},{65,1},{66,2},{67,3},{68,4},{69,5},{70,6},{71,7},{72,8},{73... | collective-permute-start | bytes 786440 | tf_op jit(solution)/shard_map/ppermute | solution.py:1006
  408.2 17.3 %collective-permute-start.16 = (bf16[2,512,768]{2,1,0:T(8,128)(2,1)}, bf16[2,512,768]{2,1,0:T(8,128)(2,1)S(1)}, u32[]{:S(2)}, u32[]{:S(2)}) collective-permute-start(bf16[2,512,768]{2,1,0:T(8,128)(2,1)} %get-tuple-element.111.g_ref.right_ref), channel_id=1, source_target_pairs={{0,1},{1,0},{2,3},{3,2},{4,5},{5,4},{6,7},{7,6},{8,9},{9,8},{10,11... | collective-permute-start | bytes 4718600 | tf_op jit(solution)/shard_map/ppermute | solution.py:39
  408.6 9.4 %copy-start.28 = (f32[1,2048]{1,0:T(1,128)S(1)}, f32[1,2048]{1,0:T(1,128)}, u32[]{:S(2)}) copy-start(f32[1,2048]{1,0:T(1,128)} %get-tuple-element.119) | copy-start | bytes 24580
  420.1 15.2 %all-to-all-start.10 = ((f32[128,1,128]{2,1,0:T(1,128)}), f32[128,1,128]{2,1,0:T(1,128)S(1)}, u32[]{:S(2)}, u32[]{:S(2)}) async-start(f32[128,1,128]{2,1,0:T(1,128)} %copy.45), calls=%async_computation.11 | async-start | bytes 131072 | tf_op jit(solution)/shard_map/all_to_all | solution.py:43
  435.3 36.8 %all-to-all-start.9 = ((bf16[4,128,2048]{2,1,0:T(8,128)(2,1)}), bf16[4,128,2048]{2,1,0:T(8,128)(2,1)S(1)}, u32[]{:S(2)}, u32[]{:S(2)}) async-start(bf16[4,128,2048]{2,1,0:T(8,128)(2,1)} %get-tuple-element.114), calls=%async_computation.10 | async-start | bytes 4194304 | tf_op jit(solution)/shard_map/all_to_all | solution.py:43
  439.2 22.1 %collective-permute-start.17 = (bf16[4,128,384]{2,1,0:T(8,128)(2,1)S(1)}, bf16[4,128,384]{2,1,0:T(8,128)(2,1)S(1)}, u32[]{:S(2)}, u32[]{:S(2)}) collective-permute-start(bf16[4,128,384]{2,1,0:T(8,128)(2,1)S(1)} %copy-done.30), channel_id=1, source_target_pairs={{0,2},{2,64},{64,66},{66,0},{1,3},{3,65},{65,67},{67,1},{4,6},{6,6... | collective-permute-start | bytes 1179656 | tf_op jit(solution)/shard_map/ppermute | solution.py:55
  440.7 20.6 %collective-permute-start.18 = (bf16[4,128,384]{2,1,0:T(8,128)(2,1)}, bf16[4,128,384]{2,1,0:T(8,128)(2,1)}, u32[]{:S(2)}, u32[]{:S(2)}) collective-permute-start(bf16[4,128,384]{2,1,0:T(8,128)(2,1)} %get-tuple-element.122), channel_id=1, source_target_pairs={{0,66},{2,0},{64,2},{66,64},{1,67},{3,1},{65,3},{67,65},{4,70},{6,... | collective-permute-start | bytes 1179656 | tf_op jit(solution)/shard_map/ppermute | solution.py:55
  442.4 24.0 %collective-permute-start.19 = (bf16[4,128,384]{2,1,0:T(8,128)(2,1)}, bf16[4,128,384]{2,1,0:T(8,128)(2,1)}, u32[]{:S(2)}, u32[]{:S(2)}) collective-permute-start(bf16[4,128,384]{2,1,0:T(8,128)(2,1)} %get-tuple-element.123), channel_id=1, source_target_pairs={{0,64},{2,66},{64,0},{66,2},{1,65},{3,67},{65,1},{67,3},{4,68},{6,... | collective-permute-start | bytes 1179656 | tf_op jit(solution)/shard_map/ppermute | solution.py:55
  444.3 33.1 %collective-permute-start.23 = (bf16[4,128,384]{2,1,0:T(8,128)(2,1)}, bf16[4,128,384]{2,1,0:T(8,128)(2,1)S(1)}, u32[]{:S(2)}, u32[]{:S(2)}) collective-permute-start(bf16[4,128,384]{2,1,0:T(8,128)(2,1)} %get-tuple-element.129), channel_id=1, source_target_pairs={{0,4},{4,8},{8,12},{12,0},{1,5},{5,9},{9,13},{13,1},{2,6},{6,10},{... | collective-permute-start | bytes 1179656 | tf_op jit(solution)/shard_map/ppermute | solution.py:55
  446.0 32.6 %collective-permute-start.24 = (bf16[4,128,384]{2,1,0:T(8,128)(2,1)}, bf16[4,128,384]{2,1,0:T(8,128)(2,1)S(1)}, u32[]{:S(2)}, u32[]{:S(2)}) collective-permute-start(bf16[4,128,384]{2,1,0:T(8,128)(2,1)} %get-tuple-element.130), channel_id=1, source_target_pairs={{0,12},{4,0},{8,4},{12,8},{1,13},{5,1},{9,5},{13,9},{2,14},{6,2},{... | collective-permute-start | bytes 1179656 | tf_op jit(solution)/shard_map/ppermute | solution.py:55
  461.3 18.4 %collective-permute-start.25 = (bf16[4,128,384]{2,1,0:T(8,128)(2,1)}, bf16[4,128,384]{2,1,0:T(8,128)(2,1)S(1)}, u32[]{:S(2)}, u32[]{:S(2)}) collective-permute-start(bf16[4,128,384]{2,1,0:T(8,128)(2,1)} %get-tuple-element.131), channel_id=1, source_target_pairs={{0,8},{4,12},{8,0},{12,4},{1,9},{5,13},{9,1},{13,5},{2,10},{6,14},... | collective-permute-start | bytes 1179656 | tf_op jit(solution)/shard_map/ppermute | solution.py:55
  468.6 17.3 %collective-permute-start.20 = (bf16[128,384]{1,0:T(8,128)(2,1)}, bf16[128,384]{1,0:T(8,128)(2,1)S(1)}, u32[]{:S(2)}, u32[]{:S(2)}) collective-permute-start(bf16[128,384]{1,0:T(8,128)(2,1)} %get-tuple-element.125), channel_id=1, source_target_pairs={{0,4},{4,8},{8,12},{12,0},{1,5},{5,9},{9,13},{13,1},{2,6},{6,10},{... | collective-permute-start | bytes 294920 | tf_op jit(solution)/shard_map/ppermute | solution.py:55
  469.6 17.6 %collective-permute-start.21 = (bf16[128,384]{1,0:T(8,128)(2,1)}, bf16[128,384]{1,0:T(8,128)(2,1)S(1)}, u32[]{:S(2)}, u32[]{:S(2)}) collective-permute-start(bf16[128,384]{1,0:T(8,128)(2,1)} %get-tuple-element.126), channel_id=1, source_target_pairs={{0,12},{4,0},{8,4},{12,8},{1,13},{5,1},{9,5},{13,9},{2,14},{6,2},{... | collective-permute-start | bytes 294920 | tf_op jit(solution)/shard_map/ppermute | solution.py:55
  477.4 9.9 %collective-permute-start.22 = (bf16[128,384]{1,0:T(8,128)(2,1)}, bf16[128,384]{1,0:T(8,128)(2,1)S(1)}, u32[]{:S(2)}, u32[]{:S(2)}) collective-permute-start(bf16[128,384]{1,0:T(8,128)(2,1)} %get-tuple-element.127), channel_id=1, source_target_pairs={{0,8},{4,12},{8,0},{12,4},{1,9},{5,13},{9,1},{13,5},{2,10},{6,14},... | collective-permute-start | bytes 294920 | tf_op jit(solution)/shard_map/ppermute | solution.py:55
  482.7 6.0 %collective-permute-start.26 = (bf16[128,384]{1,0:T(8,128)(2,1)}, bf16[128,384]{1,0:T(8,128)(2,1)S(1)}, u32[]{:S(2)}, u32[]{:S(2)}) collective-permute-start(bf16[128,384]{1,0:T(8,128)(2,1)} %get-tuple-element.137), channel_id=1, source_target_pairs={{0,2},{2,64},{64,66},{66,0},{1,3},{3,65},{65,67},{67,1},{4,6},{6,6... | collective-permute-start | bytes 294920 | tf_op jit(solution)/shard_map/ppermute | solution.py:55
  483.6 5.8 %collective-permute-start.27 = (bf16[128,384]{1,0:T(8,128)(2,1)}, bf16[128,384]{1,0:T(8,128)(2,1)S(1)}, u32[]{:S(2)}, u32[]{:S(2)}) collective-permute-start(bf16[128,384]{1,0:T(8,128)(2,1)} %get-tuple-element.138), channel_id=1, source_target_pairs={{0,66},{2,0},{64,2},{66,64},{1,67},{3,1},{65,3},{67,65},{4,70},{6,... | collective-permute-start | bytes 294920 | tf_op jit(solution)/shard_map/ppermute | solution.py:55
  485.9 6.3 %collective-permute-start.28 = (bf16[128,384]{1,0:T(8,128)(2,1)}, bf16[128,384]{1,0:T(8,128)(2,1)S(1)}, u32[]{:S(2)}, u32[]{:S(2)}) collective-permute-start(bf16[128,384]{1,0:T(8,128)(2,1)} %get-tuple-element.139), channel_id=1, source_target_pairs={{0,64},{2,66},{64,0},{66,2},{1,65},{3,67},{65,1},{67,3},{4,68},{6,... | collective-permute-start | bytes 294920 | tf_op jit(solution)/shard_map/ppermute | solution.py:55
  (29 other events, 106.7 us)
Sparse Core Ops, SparseCore 0:
  10.8 67.4 all-gather.8
  80.0 37.2 all-gather.10
  133.7 82.3 all-gather.12
  310.5 25.7 all-gather.14
  338.5 29.6 reduce-scatter.2
  386.4 96.2 reduce-scatter.4

commit v3 on v2

--- a/solution.py
+++ b/solution.py
@@ -27,7 +27,7 @@
 BLK = ("z", "yl", "k")
 Y = ("yh", "yl")
 
-VMEM_LIMIT = 60 * 1024 * 1024
+VMEM_LIMIT = 63 * 1024 * 1024
 TINY = pl.CostEstimate(flops=1, bytes_accessed=1, transcendentals=0)
 
 

time: 514 us -> 511 us (level)
  starting transfers between devices: 73.3 us -> 87.6 us
  Pallas kernels: 182 us -> 169 us
  local copies, waits for them, and re-layouts: 21.2 us -> 15 us
    all_to_all x10, starting transfers between devices: 42.9 us -> 57.8 us  [exchange(): return lax.all_to_all(parts, axes, 0, 0, tiled=True)]
    pallas_call x1, Pallas kernels: 22.4 us -> 15.2 us  [attend_back_call(): pl.pallas_call(attend_back_kernel, in_specs=[pl.BlockSpec(memory_space=pl...]
    unnamed x64 -> x40, local copies, waits for them, and re-layouts: 11.2 us -> 4.95 us
    pallas_call x1, Pallas kernels: 17.5 us -> 12 us  [attend_call(): pl.pallas_call(attend_kernel, in_specs=[pl.BlockSpec(memory_space=pltpu.S...]
  transfers between devices with their start and end apart: 45 -> 45, of which waited for: 20 -> 19; matrix products, arithmetic and copies ran while one was open for 4% -> 4% of each run, Pallas kernels for 33% -> 31%
where the time goes in v3:
time: 511 us; the launch traced here: 503 us
  waiting for transfers between devices  193 us (38%)
  Pallas kernels  169 us (33%)
  starting transfers between devices  87.6 us (17%)
  local copies, waits for them, and re-layouts  15 us (3%)
  between operations  15 us (3%)
  blocking collectives  13.8 us (3%)
  other arithmetic  9.37 us (2%)
    all_to_all x10, waiting for transfers between devices, exchange(): return lax.all_to_all(parts, axes, 0, 0, tiled=True)  102 us
    all_to_all x10, starting transfers between devices, exchange(): return lax.all_to_all(parts, axes, 0, 0, tiled=True)  57.8 us
    ppermute x15, waiting for transfers between devices, send(): return lax.ppermute(value, axes, [(i, (i + step) % 4) for i in range(4)])  54.3 us
    pallas_call x1, Pallas kernels, feed_forward_call(): pl.pallas_call(feed_forward_kernel, grid=(2,), in_specs=[tokens_once, tok...  30.4 us
    pallas_call x3, Pallas kernels, plane_grad_call(): pl.pallas_call(plane_grad_kernel, grid=(columns // 256, 2), in_specs=[pl....  30.2 us
    ppermute x15, starting transfers between devices, send(): return lax.ppermute(value, axes, [(i, (i + step) % 4) for i in range(4)])  20.7 us
    ppermute x1, waiting for transfers between devices, local(): before = lax.ppermute(ring[3], ('yh',), [(0, 1)])  20.5 us
    pallas_call x1, Pallas kernels, attend_back_call(): pl.pallas_call(attend_back_kernel, in_specs=[pl.BlockSpec(memory_space=pl...  15.2 us
  transfers between devices with their start and end apart: 45, of which 19 were waited for; matrix products, arithmetic and copies ran while one was open for 4% of the time, Pallas kernels for 31%

profile of v3, /device:TPU:0, one launch (start us, length us, event | category | flops | bytes accessed | tf_op | source)
XLA Modules:
  0.0 503.1 jit_solution(8772563316173522882)
XLA Ops:
  10.3 2.6 broadcast_in_dim.57
  12.9 4.5 all-to-all-start
  18.6 25.2 %all-to-all-done.x_ref = bf16[4,128,2048]{2,1,0:T(8,128)(2,1)S(1)} async-done(((bf16[4,128,2048]{2,1,0:T(8,128)(2,1)}), bf16[4,128,2048]{2,1,0:T(8,128)(2,1)S(1)}, u32[]{:S(2)}, u32[]{:S(2)}) %all-to-all-start) | async-done | bytes 2097184 | tf_op jit(solution)/shard_map/all_to_all | solution.py:43
  45.1 5.2 %collective-permute-start = (bf16[128,2048]{1,0:T(8,128)(2,1)S(1)}, bf16[128,2048]{1,0:T(8,128)(2,1)S(1)}, u32[]{:S(2)}, u32[]{:S(2)}) collective-permute-start(bf16[128,2048]{1,0:T(8,128)(2,1)S(1)} %slice_bitcast_fusion), channel_id=1, source_target_pairs={{0,64},{1,65},{2,66},{3,67},{4,68},{5,69},{6,70},{7,71},{8,72},{9,... | collective-permute-start | bytes 1572872 | tf_op jit(solution)/shard_map/ppermute | solution.py:949
  52.5 20.5 %collective-permute-done.before_ref = bf16[128,2048]{1,0:T(8,128)(2,1)S(1)} collective-permute-done((bf16[128,2048]{1,0:T(8,128)(2,1)S(1)}, bf16[128,2048]{1,0:T(8,128)(2,1)S(1)}, u32[]{:S(2)}, u32[]{:S(2)}) %collective-permute-start) | collective-permute-done | bytes 524320 | tf_op jit(solution)/shard_map/ppermute | solution.py:949
  73.7 5.1 %shard_map.221.unit_ref = bf16[5,128,2048]{2,1,0:T(8,128)(2,1)} custom-call(bf16[4,128,2048]{2,1,0:T(8,128)(2,1)} %copy-done, bf16[128,2048]{1,0:T(8,128)(2,1)} %copy-done.5), custom_call_target="tpu_custom_call" | custom-call | flops 1 | bytes 1 | tf_op jit(solution)/shard_map/pallas_call | solution.py:150
  78.8 13.1 %shard_map.222 = (bf16[4,2,2,5,128,128]{5,4,3,2,1,0:T(8,128)(2,1)}, bf16[4,128,2048]{2,1,0:T(8,128)(2,1)}) custom-call(bf16[5,128,2048]{2,1,0:T(8,128)(2,1)} %shard_map.221.unit_ref, bf16[4,2,4,144,1024]{4,3,2,1,0:T(8,128)(2,1)} %bitcast.55, bf16[4,2,4,144,1024]{4,3,2,1,0:T(8,128)(2,1)} %bitcast.56, f32[640,128]{1,0:T(8,128)} %get-tuple-element.151.cos_ref, ...), custom_call_target="tpu_custom_call" | custom-call | flops 1 | bytes 1 | tf_op jit(solution)/shard_map/pallas_call | solution.py:239
  91.9 5.6 %all-to-all-start.1 = ((bf16[16,5,128,128]{3,2,1,0:T(8,128)(2,1)}), bf16[16,5,128,128]{3,2,1,0:T(8,128)(2,1)}, u32[]{:S(2)}, u32[]{:S(2)}) async-start(bf16[16,5,128,128]{3,2,1,0:T(8,128)(2,1)} %bitcast.68), calls=%async_computation.1 | async-start | bytes 5242880 | tf_op jit(solution)/shard_map/all_to_all | solution.py:43
  98.2 3.7 shard_map.223.refs_0_
  102.6 2.5 collective-permute-start.2
  107.2 26.2 %collective-permute-done.1.refs_1_ = bf16[8,128,512]{2,1,0:T(8,128)(2,1)} collective-permute-done((bf16[8,128,512]{2,1,0:T(8,128)(2,1)}, bf16[8,128,512]{2,1,0:T(8,128)(2,1)}, u32[]{:S(2)}, u32[]{:S(2)}) %collective-permute-start.1) | collective-permute-done | bytes 1048608 | tf_op jit(solution)/shard_map/ppermute | solution.py:55
  135.9 12.0 %shard_map.224 = (f32[16,128,128]{2,1,0:T(8,128)}, bf16[16,128,128]{2,1,0:T(8,128)(2,1)}, f32[8,1,512]{2,1,0:T(1,128)}) custom-call(s32[16]{0:T(128)} %dynamic-slice_subtract_fusion.lo_ref, bf16[16,5,128,128]{3,2,1,0:T(8,128)(2,1)} %all-to-all-done.1.r_ref), custom_call_target="tpu_custom_call" | custom-call | flops 1 | bytes 1 | tf_op jit(solution)/shard_map/pallas_call | solution.py:751
  147.8 11.7 %all-to-all-start.2 = ((bf16[16,128,128]{2,1,0:T(8,128)(2,1)}), bf16[16,128,128]{2,1,0:T(8,128)(2,1)}, u32[]{:S(2)}, u32[]{:S(2)}) async-start(bf16[16,128,128]{2,1,0:T(8,128)(2,1)} %get-tuple-element.83), calls=%async_computation.2 | async-start | bytes 1048576 | tf_op jit(solution)/shard_map/all_to_all | solution.py:43
  160.4 10.0 %all-to-all-done.2 = bf16[16,128,128]{2,1,0:T(8,128)(2,1)} async-done(((bf16[16,128,128]{2,1,0:T(8,128)(2,1)}), bf16[16,128,128]{2,1,0:T(8,128)(2,1)}, u32[]{:S(2)}, u32[]{:S(2)}) %all-to-all-start.2) | async-done | bytes 524320 | tf_op jit(solution)/shard_map/all_to_all | solution.py:43
  170.4 3.5 all-to-all-start.3
  175.3 9.0 %all-to-all-done.3.att_ref = bf16[4,2,2,128,128]{4,3,2,1,0:T(8,128)(2,1)S(1)} async-done(((bf16[4,2,2,128,128]{4,3,2,1,0:T(8,128)(2,1)}), bf16[4,2,2,128,128]{4,3,2,1,0:T(8,128)(2,1)S(1)}, u32[]{:S(2)}, u32[]{:S(2)}) %all-to-all-start.3) | async-done | bytes 524320 | tf_op jit(solution)/shard_map/all_to_all | solution.py:43
  185.1 8.6 %shard_map.225 = (f32[128,2048]{1,0:T(8,128)}, bf16[4,128,2048]{2,1,0:T(8,128)(2,1)}) custom-call(s32[2]{0:T(128)} %pad_add_fusion.1.place_ref, bf16[4,2,2,128,128]{4,3,2,1,0:T(8,128)(2,1)} %copy-done.2, bf16[128,2048]{1,0:T(8,128)(2,1)} %tokens_ref.3, f32[1,2048]{1,0:T(1,128)} %bitcast.79, f32[1,2048]{1,0:T(1,128)} %bitcast.82, ...), custom_call_target="tpu_custom_call" | custom-call | flops 1 | bytes 1 | tf_op jit(solution)/shard_map/pallas_call | solution.py:378
  193.7 4.4 all-to-all-start.4
  198.5 26.2 %all-to-all-done.4.x_ref.left_ref = bf16[4,128,2048]{2,1,0:T(8,128)(2,1)} async-done(((bf16[4,128,2048]{2,1,0:T(8,128)(2,1)}), bf16[4,128,2048]{2,1,0:T(8,128)(2,1)}, u32[]{:S(2)}, u32[]{:S(2)}) %all-to-all-start.4) | async-done | bytes 2097184 | tf_op jit(solution)/shard_map/all_to_all | solution.py:43
  224.7 30.4 %shard_map.227 = (bf16[2,512,768]{2,1,0:T(8,128)(2,1)}, bf16[2,512,1536]{2,1,0:T(8,128)(2,1)}, bf16[4,128,2048]{2,1,0:T(8,128)(2,1)}, bf16[4,128,2048]{2,1,0:T(8,128)(2,1)}) custom-call(bf16[4,128,2048]{2,1,0:T(8,128)(2,1)} %all-to-all-done.4.x_ref.left_ref, bf16[4,128,2048]{2,1,0:T(8,128)(2,1)} %bitcast.66, bf16[4,2,512,2304]{3,2,1,0:T(8,128)(2,1)} %bitcast.61, ...), custom_call_target="tpu_custom_call" | custom-call | flops 1 | bytes 1 | tf_op jit(solution)/shard_map/pallas_call | solution.py:505
  255.2 4.4 all-to-all-start.5
  259.8 9.4 %shard_map.228.refs_0_ = bf16[2,2,4,128,2560]{4,3,2,1,0:T(8,128)(2,1)} custom-call(s32[1]{0:T(128)} %bitcast.1.core_ref, bf16[4,128,2048]{2,1,0:T(8,128)(2,1)} %bitcast.67, bf16[4,128,2048]{2,1,0:T(8,128)(2,1)} %collective-permute-done.8.left_other_ref, bf16[2,512,768]{2,1,0:T(8,128)(2,1)} %get-tuple-element.92.right_ref, ...), custom_call_target="tpu_custom_call" | custom-call | flops 1 | bytes 1 | tf_op jit(solution)/shard_map/pallas_call | solution.py:546
  269.1 17.9 %all-to-all-done.5.came_ref = bf16[4,128,2048]{2,1,0:T(8,128)(2,1)} async-done(((bf16[4,128,2048]{2,1,0:T(8,128)(2,1)}), bf16[4,128,2048]{2,1,0:T(8,128)(2,1)}, u32[]{:S(2)}, u32[]{:S(2)}) %all-to-all-start.5) | async-done | bytes 2097184 | tf_op jit(solution)/shard_map/all_to_all | solution.py:43
  287.0 9.0 %shard_map.229 = (f32[128,2048]{1,0:T(8,128)}, bf16[128,2048]{1,0:T(8,128)(2,1)}, f32[1,2048]{1,0:T(1,128)}, f32[1,2048]{1,0:T(1,128)}, bf16[4,2,2,128,128]{4,3,2,1,0:T(8,128)(2,1)}) custom-call(s32[2]{0:T(128)} %pad_add_fusion.1.place_ref, bf16[4,128,2048]{2,1,0:T(8,128)(2,1)} %all-to-all-done.5.came_ref, f32[128,2048]{1,0:T(8,128)} %get-tuple-element.86.middle_ref, ...), custom_call_target="tpu_custom_call" | custom-call | flops 1 | bytes 1 | tf_op jit(solution)/shard_map/pallas_call | solution.py:439
  296.0 13.8 %all_to_all.59 = bf16[4,2,2,128,128]{4,3,2,1,0:T(8,128)(2,1)} all-to-all(bf16[4,2,2,128,128]{4,3,2,1,0:T(8,128)(2,1)} %get-tuple-element.94), channel_id=1, replica_groups=mesh['yh'=2,'x'=4,'z'=4,'yl'=2,'k'=2] {'x'}, dimensions={0} | all-to-all | bytes 1048576 | tf_op jit(solution)/shard_map/all_to_all | solution.py:43
  310.0 3.6 all-to-all-start.7
  314.5 4.4 shard_map.230.left_ref
  318.9 5.5 %all-to-all-done.7.do_ref = bf16[16,128,128]{2,1,0:T(8,128)(2,1)S(1)} async-done(((bf16[16,128,128]{2,1,0:T(8,128)(2,1)}), bf16[16,128,128]{2,1,0:T(8,128)(2,1)S(1)}, u32[]{:S(2)}, u32[]{:S(2)}) %all-to-all-start.7) | async-done | bytes 524320 | tf_op jit(solution)/shard_map/all_to_all | solution.py:43
  325.2 15.2 %shard_map.231 = bf16[16,5,128,128]{3,2,1,0:T(8,128)(2,1)} custom-call(s32[16]{0:T(128)} %dynamic-slice_subtract_fusion.lo_ref, bf16[16,5,128,128]{3,2,1,0:T(8,128)(2,1)} %all-to-all-done.1.r_ref, bf16[16,128,128]{2,1,0:T(8,128)(2,1)} %copy-done.4, f32[16,128,128]{2,1,0:T(8,128)} %get-tuple-element.98.o32_ref, f32[8,1,512]{2,1,0:T(1,128)} %get-tuple-element.99.lse_ref), custom_call_target="tpu_custom_call" | custom-call | flops 1 | bytes 1 | tf_op jit(solution)/shard_map/pallas_call | solution.py:815
  340.5 10.7 %all-to-all-start.8 = ((bf16[16,5,128,128]{3,2,1,0:T(8,128)(2,1)}), bf16[16,5,128,128]{3,2,1,0:T(8,128)(2,1)}, u32[]{:S(2)}, u32[]{:S(2)}) async-start(bf16[16,5,128,128]{3,2,1,0:T(8,128)(2,1)} %shard_map.231), calls=%async_computation.9 | async-start | bytes 5242880 | tf_op jit(solution)/shard_map/all_to_all | solution.py:43
  355.8 15.4 %shard_map.232.refs_0_ = bf16[2,2,4,128,2560]{4,3,2,1,0:T(8,128)(2,1)} custom-call(s32[1]{0:T(128)} %bitcast.1.core_ref, bf16[4,128,2048]{2,1,0:T(8,128)(2,1)} %all-to-all-done.4.x_ref.left_ref, bf16[4,128,2048]{2,1,0:T(8,128)(2,1)} %collective-permute-done.13.left_other_ref, ...), custom_call_target="tpu_custom_call", output_to_operand_aliasing={{}: (5, {})} | custom-call | flops 1 | bytes 1 | tf_op jit(solution)/shard_map/pallas_call | solution.py:546
  371.2 5.4 %shard_map.233 = bf16[2,2,4,128,2560]{4,3,2,1,0:T(8,128)(2,1)} custom-call(s32[1]{0:T(128)} %bitcast.1.core_ref, bf16[4,128,2048]{2,1,0:T(8,128)(2,1)} %bitcast.70, bf16[4,128,2048]{2,1,0:T(8,128)(2,1)} %collective-permute-done.11.left_other_ref, bf16[2,512,256]{2,1,0:T(8,128)(2,1)} %copy-done.3, ...), custom_call_target="tpu_custom_call", output_to_operand_aliasing={{}: (5, {})} | custom-call | flops 1 | bytes 1 | tf_op jit(solution)/shard_map/pallas_call | solution.py:546
  376.6 8.1 %all-to-all-done.8 = bf16[16,5,128,128]{3,2,1,0:T(8,128)(2,1)} async-done(((bf16[16,5,128,128]{3,2,1,0:T(8,128)(2,1)}), bf16[16,5,128,128]{3,2,1,0:T(8,128)(2,1)}, u32[]{:S(2)}, u32[]{:S(2)}) %all-to-all-start.8) | async-done | bytes 2621472 | tf_op jit(solution)/shard_map/all_to_all | solution.py:43
  389.1 13.3 %collective-permute-done.15.halo_ref = bf16[2,2,2,128,128]{4,3,2,1,0:T(8,128)(2,1)S(1)} collective-permute-done((bf16[2,2,2,128,128]{4,3,2,1,0:T(8,128)(2,1)S(1)}, bf16[2,2,2,128,128]{4,3,2,1,0:T(8,128)(2,1)S(1)}, u32[]{:S(2)}, u32[]{:S(2)}) %collective-permute-start.15) | collective-permute-done | bytes 262176 | tf_op jit(solution)/shard_map/ppermute | solution.py:1006
  403.1 3.7 shard_map.234
  407.1 9.0 %shard_map.235 = (bf16[4,128,2048]{2,1,0:T(8,128)(2,1)}, f32[1,2048]{1,0:T(1,128)}, f32[1,2048]{1,0:T(1,128)}) custom-call(bf16[2,512,768]{2,1,0:T(8,128)(2,1)} %get-tuple-element.111.g_ref.right_ref, bf16[5,128,2048]{2,1,0:T(8,128)(2,1)} %shard_map.221.unit_ref, bf16[4,2,4,144,1024]{4,3,2,1,0:T(8,128)(2,1)} %bitcast.60), custom_call_target="tpu_custom_call" | custom-call | flops 1 | bytes 1 | tf_op jit(solution)/shard_map/pallas_call | solution.py:906
  418.6 4.8 all-to-all-start.10
  424.0 8.6 %shard_map.236 = (bf16[4,128,384]{2,1,0:T(8,128)(2,1)}, bf16[4,128,384]{2,1,0:T(8,128)(2,1)}, bf16[4,128,384]{2,1,0:T(8,128)(2,1)}, bf16[4,128,384]{2,1,0:T(8,12...) custom-call(s32[4,16]{1,0:T(4,128)} %pad_add_fusion.place_ref, ...), custom_call_target="tpu_custom_call" | custom-call | flops 1 | bytes 1 | tf_op jit(solution)/shard_map/pallas_call | solution.py:602
  432.7 4.6 all-to-all-start.9
  438.3 2.4 collective-permute-start.18
  445.3 15.4 %collective-permute-done.17.b_ref = bf16[4,128,384]{2,1,0:T(8,128)(2,1)} collective-permute-done((bf16[4,128,384]{2,1,0:T(8,128)(2,1)S(1)}, bf16[4,128,384]{2,1,0:T(8,128)(2,1)}, u32[]{:S(2)}, u32[]{:S(2)}) %collective-permute-start.17) | collective-permute-done | bytes 393248 | tf_op jit(solution)/shard_map/ppermute | solution.py:55
  460.8 3.2 collective-permute-done.19.d_ref
  467.3 2.3 collective-permute-start.21
  469.6 3.9 shard_map.237
  474.6 4.5 collective-permute-done.25.d_ref
  481.2 3.2 collective-permute-start.27
  488.0 2.8 collective-permute-done.28.refs_7_
  493.5 2.3 shard_map.241
  (161 shorter events, 51.2 us)
Async XLA Ops:
  7.2 71.6 %all-gather.9.cloned.1.call-start = ((), (), s32[]{:S(2)}) async-start(), calls=%async_computation.15 | async-start | bytes 9732096 | tf_op jit(solution)/shard_map/all_gather | solution.py:946
  12.9 30.8 %all-to-all-start = ((bf16[4,128,2048]{2,1,0:T(8,128)(2,1)}), bf16[4,128,2048]{2,1,0:T(8,128)(2,1)S(1)}, u32[]{:S(2)}, u32[]{:S(2)}) async-start(bf16[4,128,2048]{2,1,0:T(8,128)(2,1)} %broadcast_in_dim.57), calls=%async_computation | async-start | bytes 4194304 | tf_op jit(solution)/shard_map/all_to_all | solution.py:43
  17.4 180.8 %all-gather.11.cloned.1.call-start = ((), (), s32[]{:S(2)}) async-start(), calls=%async_computation.16 | async-start | bytes 2621440 | tf_op jit(solution)/shard_map/all_gather | solution.py:950
  45.1 27.8 %collective-permute-start = (bf16[128,2048]{1,0:T(8,128)(2,1)S(1)}, bf16[128,2048]{1,0:T(8,128)(2,1)S(1)}, u32[]{:S(2)}, u32[]{:S(2)}) collective-permute-start(bf16[128,2048]{1,0:T(8,128)(2,1)S(1)} %slice_bitcast_fusion), channel_id=1, source_target_pairs={{0,64},{1,65},{2,66},{3,67},{4,68},{5,69},{6,70},{7,71},{8,72},{9,... | collective-permute-start | bytes 1572872 | tf_op jit(solution)/shard_map/ppermute | solution.py:949
  91.9 41.5 %all-to-all-start.1 = ((bf16[16,5,128,128]{3,2,1,0:T(8,128)(2,1)}), bf16[16,5,128,128]{3,2,1,0:T(8,128)(2,1)}, u32[]{:S(2)}, u32[]{:S(2)}) async-start(bf16[16,5,128,128]{3,2,1,0:T(8,128)(2,1)} %bitcast.68), calls=%async_computation.1 | async-start | bytes 5242880 | tf_op jit(solution)/shard_map/all_to_all | solution.py:43
  97.5 127.2 %all-gather.13.cloned.1.call-start = ((), (), s32[]{:S(2)}) async-start(), calls=%async_computation.17 | async-start | bytes 19464192 | tf_op jit(solution)/shard_map/all_gather | solution.py:971
  101.8 31.6 %collective-permute-start.1 = (bf16[8,128,512]{2,1,0:T(8,128)(2,1)}, bf16[8,128,512]{2,1,0:T(8,128)(2,1)}, u32[]{:S(2)}, u32[]{:S(2)}) collective-permute-start(bf16[8,128,512]{2,1,0:T(8,128)(2,1)} %shard_map.223.refs_0_), channel_id=1, source_target_pairs={{0,16},{16,32},{32,48},{48,0},{1,17},{17,33},{33,49},{49,1},{2,18}... | collective-permute-start | bytes 3145736 | tf_op jit(solution)/shard_map/ppermute | solution.py:55
  102.6 30.8 %collective-permute-start.2 = (bf16[8,128,512]{2,1,0:T(8,128)(2,1)}, bf16[8,128,512]{2,1,0:T(8,128)(2,1)}, u32[]{:S(2)}, u32[]{:S(2)}) collective-permute-start(bf16[8,128,512]{2,1,0:T(8,128)(2,1)} %shard_map.223.refs_0_), channel_id=1, source_target_pairs={{0,48},{16,0},{32,16},{48,32},{1,49},{17,1},{33,17},{49,33},{2,50}... | collective-permute-start | bytes 3145736 | tf_op jit(solution)/shard_map/ppermute | solution.py:55
  133.5 37.0 %collective-permute-start.3 = (bf16[8,128,512]{2,1,0:T(8,128)(2,1)}, bf16[8,128,512]{2,1,0:T(8,128)(2,1)}, u32[]{:S(2)}, u32[]{:S(2)}) collective-permute-start(bf16[8,128,512]{2,1,0:T(8,128)(2,1)} %shard_map.223.refs_0_), channel_id=1, source_target_pairs={{0,32},{16,48},{32,0},{48,16},{1,33},{17,49},{33,1},{49,17},{2,34}... | collective-permute-start | bytes 3145736 | tf_op jit(solution)/shard_map/ppermute | solution.py:55
  147.8 22.6 %all-to-all-start.2 = ((bf16[16,128,128]{2,1,0:T(8,128)(2,1)}), bf16[16,128,128]{2,1,0:T(8,128)(2,1)}, u32[]{:S(2)}, u32[]{:S(2)}) async-start(bf16[16,128,128]{2,1,0:T(8,128)(2,1)} %get-tuple-element.83), calls=%async_computation.2 | async-start | bytes 1048576 | tf_op jit(solution)/shard_map/all_to_all | solution.py:43
  159.5 15.8 %collective-permute-start.4 = (bf16[8,128,512]{2,1,0:T(8,128)(2,1)}, bf16[8,128,512]{2,1,0:T(8,128)(2,1)}, u32[]{:S(2)}, u32[]{:S(2)}) collective-permute-start(bf16[8,128,512]{2,1,0:T(8,128)(2,1)} %shard_map.223.refs_0_), channel_id=1, source_target_pairs={{0,1},{1,0},{2,3},{3,2},{4,5},{5,4},{6,7},{7,6},{8,9},{9,8},{10,11... | collective-permute-start | bytes 3145736 | tf_op jit(solution)/shard_map/ppermute | solution.py:39
  159.9 15.4 %collective-permute-start.5 = (bf16[8,128,512]{2,1,0:T(8,128)(2,1)}, bf16[8,128,512]{2,1,0:T(8,128)(2,1)}, u32[]{:S(2)}, u32[]{:S(2)}) collective-permute-start(bf16[8,128,512]{2,1,0:T(8,128)(2,1)} %collective-permute-done.1.refs_1_), channel_id=1, source_target_pairs={{0,1},{1,0},{2,3},{3,2},{4,5},{5,4},{6,7},{7,6},{8,9},{9,8},{10,11... | collective-permute-start | bytes 3145736 | tf_op jit(solution)/shard_map/ppermute | solution.py:39
  160.1 15.2 %collective-permute-start.7 = (bf16[8,128,512]{2,1,0:T(8,128)(2,1)}, bf16[8,128,512]{2,1,0:T(8,128)(2,1)}, u32[]{:S(2)}, u32[]{:S(2)}) collective-permute-start(bf16[8,128,512]{2,1,0:T(8,128)(2,1)} %collective-permute-done.2.refs_3_), channel_id=1, source_target_pairs={{0,1},{1,0},{2,3},{3,2},{4,5},{5,4},{6,7},{7,6},{8,9},{9,8},{10,11... | collective-permute-start | bytes 3145736 | tf_op jit(solution)/shard_map/ppermute | solution.py:39
  170.4 13.9 %collective-permute-start.6 = (bf16[8,128,512]{2,1,0:T(8,128)(2,1)}, bf16[8,128,512]{2,1,0:T(8,128)(2,1)}, u32[]{:S(2)}, u32[]{:S(2)}) collective-permute-start(bf16[8,128,512]{2,1,0:T(8,128)(2,1)} %collective-permute-done.3.refs_2_), channel_id=1, source_target_pairs={{0,1},{1,0},{2,3},{3,2},{4,5},{5,4},{6,7},{7,6},{8,9},{9,8},{10,11... | collective-permute-start | bytes 3145736 | tf_op jit(solution)/shard_map/ppermute | solution.py:39
  170.4 13.9 %all-to-all-start.3 = ((bf16[4,2,2,128,128]{4,3,2,1,0:T(8,128)(2,1)}), bf16[4,2,2,128,128]{4,3,2,1,0:T(8,128)(2,1)S(1)}, u32[]{:S(2)}, u32[]{:S(2)}) async-start(bf16[4,2,2,128,128]{4,3,2,1,0:T(8,128)(2,1)} %bitcast.15), calls=%async_computation.3 | async-start | bytes 1048576 | tf_op jit(solution)/shard_map/all_to_all | solution.py:43
  193.7 31.0 %all-to-all-start.4 = ((bf16[4,128,2048]{2,1,0:T(8,128)(2,1)}), bf16[4,128,2048]{2,1,0:T(8,128)(2,1)}, u32[]{:S(2)}, u32[]{:S(2)}) async-start(bf16[4,128,2048]{2,1,0:T(8,128)(2,1)} %get-tuple-element.87), calls=%async_computation.4 | async-start | bytes 4194304 | tf_op jit(solution)/shard_map/all_to_all | solution.py:43
  198.2 61.5 %collective-permute-start.8 = (bf16[4,128,2048]{2,1,0:T(8,128)(2,1)}, bf16[4,128,2048]{2,1,0:T(8,128)(2,1)}, u32[]{:S(2)}, u32[]{:S(2)}) collective-permute-start(bf16[4,128,2048]{2,1,0:T(8,128)(2,1)} %bitcast.65), channel_id=1, source_target_pairs={{0,1},{1,0},{2,3},{3,2},{4,5},{5,4},{6,7},{7,6},{8,9},{9,8},{10,11... | collective-permute-start | bytes 6291464 | tf_op jit(solution)/shard_map/ppermute | solution.py:39
  255.1 4.6 collective-permute-start.9
  255.2 31.8 %all-to-all-start.5 = ((bf16[4,128,2048]{2,1,0:T(8,128)(2,1)}), bf16[4,128,2048]{2,1,0:T(8,128)(2,1)}, u32[]{:S(2)}, u32[]{:S(2)}) async-start(bf16[4,128,2048]{2,1,0:T(8,128)(2,1)} %get-tuple-element.91), calls=%async_computation.5 | async-start | bytes 4194304 | tf_op jit(solution)/shard_map/all_to_all | solution.py:43
  259.7 92.0 %all-gather.15.cloned.1.call-start = ((), (), s32[]{:S(2)}) async-start(), calls=%async_computation.18 | async-start | bytes 2621440 | tf_op jit(solution)/shard_map/all_gather | solution.py:989
  309.9 4.6 collective-permute-start.10
  310.0 14.4 %all-to-all-start.7 = ((bf16[16,128,128]{2,1,0:T(8,128)(2,1)}), bf16[16,128,128]{2,1,0:T(8,128)(2,1)S(1)}, u32[]{:S(2)}, u32[]{:S(2)}) async-start(bf16[16,128,128]{2,1,0:T(8,128)(2,1)} %bitcast.25), calls=%async_computation.7 | async-start | bytes 1048576 | tf_op jit(solution)/shard_map/all_to_all | solution.py:43
  313.6 71.2 %reduce-scatter.3.cloned.1.call-start = ((), (), s32[]{:S(2)}) async-start(), calls=%async_computation.13 | async-start | bytes 2621440 | tf_op jit(solution)/shard_map/reduce_scatter | solution.py:994
  324.4 31.4 %collective-permute-start.14 = (bf16[2,512,1536]{2,1,0:T(8,128)(2,1)}, bf16[2,512,1536]{2,1,0:T(8,128)(2,1)}, u32[]{:S(2)}, u32[]{:S(2)}) collective-permute-start(bf16[2,512,1536]{2,1,0:T(8,128)(2,1)} %get-tuple-element.106.right_ref), channel_id=1, source_target_pairs={{0,1},{1,0},{2,3},{3,2},{4,5},{5,4},{6,7},{7,6},{8,9},{9,8},{10,11... | collective-permute-start | bytes 9437192 | tf_op jit(solution)/shard_map/ppermute | solution.py:39
  340.5 44.3 %all-to-all-start.8 = ((bf16[16,5,128,128]{3,2,1,0:T(8,128)(2,1)}), bf16[16,5,128,128]{3,2,1,0:T(8,128)(2,1)}, u32[]{:S(2)}, u32[]{:S(2)}) async-start(bf16[16,5,128,128]{3,2,1,0:T(8,128)(2,1)} %shard_map.231), calls=%async_computation.9 | async-start | bytes 5242880 | tf_op jit(solution)/shard_map/all_to_all | solution.py:43
  351.2 142.3 %reduce-scatter.5.cloned.1.call-start = ((), (), s32[]{:S(2)}) async-start(), calls=%async_computation.14 | async-start | bytes 11141120 | tf_op jit(solution)/shard_map/reduce_scatter | solution.py:649
  351.2 4.6 collective-permute-start.13
  351.7 19.6 %collective-permute-start.11 = (bf16[4,128,2048]{2,1,0:T(8,128)(2,1)}, bf16[4,128,2048]{2,1,0:T(8,128)(2,1)}, u32[]{:S(2)}, u32[]{:S(2)}) collective-permute-start(bf16[4,128,2048]{2,1,0:T(8,128)(2,1)} %bitcast.69), channel_id=1, source_target_pairs={{0,1},{1,0},{2,3},{3,2},{4,5},{5,4},{6,7},{7,6},{8,9},{9,8},{10,11... | collective-permute-start | bytes 6291464 | tf_op jit(solution)/shard_map/ppermute | solution.py:39
  353.7 17.5 %copy-start.3 = (bf16[2,512,256]{2,1,0:T(8,128)(2,1)}, bf16[2,512,256]{2,1,0:T(8,128)(2,1)S(1)}, u32[]{:S(2)}) copy-start(bf16[2,512,256]{2,1,0:T(8,128)(2,1)S(1)} %reshape.366.right_ref) | copy-start | bytes 1572868
  353.8 17.5 %collective-permute-start.12 = (bf16[2,512,256]{2,1,0:T(8,128)(2,1)S(1)}, bf16[2,512,256]{2,1,0:T(8,128)(2,1)}, u32[]{:S(2)}, u32[]{:S(2)}) collective-permute-start(bf16[2,512,256]{2,1,0:T(8,128)(2,1)S(1)} %reshape.366.right_ref), channel_id=1, source_target_pairs={{0,1},{1,0},{2,3},{3,2},{4,5},{5,4},{6,7},{7,6},{8,9},{9,8},{10,11... | collective-permute-start | bytes 1572872 | tf_op jit(solution)/shard_map/ppermute | solution.py:39
  385.8 16.6 %collective-permute-start.15 = (bf16[2,2,2,128,128]{4,3,2,1,0:T(8,128)(2,1)S(1)}, bf16[2,2,2,128,128]{4,3,2,1,0:T(8,128)(2,1)S(1)}, u32[]{:S(2)}, u32[]{:S(2)}) collective-permute-start(bf16[2,2,2,128,128]{4,3,2,1,0:T(8,128)(2,1)S(1)} %slice_bitcast_fusion.1), channel_id=1, source_target_pairs={{64,0},{65,1},{66,2},{67,3},{68,4},{69,5},{70,6},{71,7},{72,8},{73... | collective-permute-start | bytes 786440 | tf_op jit(solution)/shard_map/ppermute | solution.py:1006
  406.8 17.2 %collective-permute-start.16 = (bf16[2,512,768]{2,1,0:T(8,128)(2,1)}, bf16[2,512,768]{2,1,0:T(8,128)(2,1)}, u32[]{:S(2)}, u32[]{:S(2)}) collective-permute-start(bf16[2,512,768]{2,1,0:T(8,128)(2,1)} %get-tuple-element.111.g_ref.right_ref), channel_id=1, source_target_pairs={{0,1},{1,0},{2,3},{3,2},{4,5},{5,4},{6,7},{7,6},{8,9},{9,8},{10,11... | collective-permute-start | bytes 4718600 | tf_op jit(solution)/shard_map/ppermute | solution.py:39
  407.1 9.4 %copy-start.13 = (f32[1,2048]{1,0:T(1,128)S(1)}, f32[1,2048]{1,0:T(1,128)}, u32[]{:S(2)}) copy-start(f32[1,2048]{1,0:T(1,128)} %get-tuple-element.118) | copy-start | bytes 24580
  407.1 9.4 %copy-start.14 = (f32[1,2048]{1,0:T(1,128)S(1)}, f32[1,2048]{1,0:T(1,128)}, u32[]{:S(2)}) copy-start(f32[1,2048]{1,0:T(1,128)} %get-tuple-element.119) | copy-start | bytes 24580
  418.6 14.1 %all-to-all-start.10 = ((f32[128,1,128]{2,1,0:T(1,128)}), f32[128,1,128]{2,1,0:T(1,128)S(1)}, u32[]{:S(2)}, u32[]{:S(2)}) async-start(f32[128,1,128]{2,1,0:T(1,128)} %copy.45), calls=%async_computation.11 | async-start | bytes 131072 | tf_op jit(solution)/shard_map/all_to_all | solution.py:43
  432.7 36.9 %all-to-all-start.9 = ((bf16[4,128,2048]{2,1,0:T(8,128)(2,1)}), bf16[4,128,2048]{2,1,0:T(8,128)(2,1)}, u32[]{:S(2)}, u32[]{:S(2)}) async-start(bf16[4,128,2048]{2,1,0:T(8,128)(2,1)} %get-tuple-element.114), calls=%async_computation.10 | async-start | bytes 4194304 | tf_op jit(solution)/shard_map/all_to_all | solution.py:43
  437.3 23.4 %collective-permute-start.17 = (bf16[4,128,384]{2,1,0:T(8,128)(2,1)S(1)}, bf16[4,128,384]{2,1,0:T(8,128)(2,1)}, u32[]{:S(2)}, u32[]{:S(2)}) collective-permute-start(bf16[4,128,384]{2,1,0:T(8,128)(2,1)S(1)} %copy-done.18), channel_id=1, source_target_pairs={{0,2},{2,64},{64,66},{66,0},{1,3},{3,65},{65,67},{67,1},{4,6},{6,6... | collective-permute-start | bytes 1179656 | tf_op jit(solution)/shard_map/ppermute | solution.py:55
  438.3 22.5 %collective-permute-start.18 = (bf16[4,128,384]{2,1,0:T(8,128)(2,1)S(1)}, bf16[4,128,384]{2,1,0:T(8,128)(2,1)}, u32[]{:S(2)}, u32[]{:S(2)}) collective-permute-start(bf16[4,128,384]{2,1,0:T(8,128)(2,1)S(1)} %copy-done.17), channel_id=1, source_target_pairs={{0,66},{2,0},{64,2},{66,64},{1,67},{3,1},{65,3},{67,65},{4,70},{6,... | collective-permute-start | bytes 1179656 | tf_op jit(solution)/shard_map/ppermute | solution.py:55
  440.6 23.3 %collective-permute-start.19 = (bf16[4,128,384]{2,1,0:T(8,128)(2,1)S(1)}, bf16[4,128,384]{2,1,0:T(8,128)(2,1)}, u32[]{:S(2)}, u32[]{:S(2)}) collective-permute-start(bf16[4,128,384]{2,1,0:T(8,128)(2,1)S(1)} %copy-done.16), channel_id=1, source_target_pairs={{0,64},{2,66},{64,0},{66,2},{1,65},{3,67},{65,1},{67,3},{4,68},{6,... | collective-permute-start | bytes 1179656 | tf_op jit(solution)/shard_map/ppermute | solution.py:55
  441.9 31.7 %collective-permute-start.23 = (bf16[4,128,384]{2,1,0:T(8,128)(2,1)}, bf16[4,128,384]{2,1,0:T(8,128)(2,1)S(1)}, u32[]{:S(2)}, u32[]{:S(2)}) collective-permute-start(bf16[4,128,384]{2,1,0:T(8,128)(2,1)} %get-tuple-element.129), channel_id=1, source_target_pairs={{0,4},{4,8},{8,12},{12,0},{1,5},{5,9},{9,13},{13,1},{2,6},{6,10},{... | collective-permute-start | bytes 1179656 | tf_op jit(solution)/shard_map/ppermute | solution.py:55
  443.5 31.0 %collective-permute-start.24 = (bf16[4,128,384]{2,1,0:T(8,128)(2,1)}, bf16[4,128,384]{2,1,0:T(8,128)(2,1)S(1)}, u32[]{:S(2)}, u32[]{:S(2)}) collective-permute-start(bf16[4,128,384]{2,1,0:T(8,128)(2,1)} %get-tuple-element.130), channel_id=1, source_target_pairs={{0,12},{4,0},{8,4},{12,8},{1,13},{5,1},{9,5},{13,9},{2,14},{6,2},{... | collective-permute-start | bytes 1179656 | tf_op jit(solution)/shard_map/ppermute | solution.py:55
  460.8 18.3 %collective-permute-start.25 = (bf16[4,128,384]{2,1,0:T(8,128)(2,1)}, bf16[4,128,384]{2,1,0:T(8,128)(2,1)}, u32[]{:S(2)}, u32[]{:S(2)}) collective-permute-start(bf16[4,128,384]{2,1,0:T(8,128)(2,1)} %get-tuple-element.131), channel_id=1, source_target_pairs={{0,8},{4,12},{8,0},{12,4},{1,9},{5,13},{9,1},{13,5},{2,10},{6,14},... | collective-permute-start | bytes 1179656 | tf_op jit(solution)/shard_map/ppermute | solution.py:55
  466.2 18.3 %collective-permute-start.20 = (bf16[128,384]{1,0:T(8,128)(2,1)}, bf16[128,384]{1,0:T(8,128)(2,1)S(1)}, u32[]{:S(2)}, u32[]{:S(2)}) collective-permute-start(bf16[128,384]{1,0:T(8,128)(2,1)} %get-tuple-element.125), channel_id=1, source_target_pairs={{0,4},{4,8},{8,12},{12,0},{1,5},{5,9},{9,13},{13,1},{2,6},{6,10},{... | collective-permute-start | bytes 294920 | tf_op jit(solution)/shard_map/ppermute | solution.py:55
  467.3 18.6 %collective-permute-start.21 = (bf16[128,384]{1,0:T(8,128)(2,1)}, bf16[128,384]{1,0:T(8,128)(2,1)}, u32[]{:S(2)}, u32[]{:S(2)}) collective-permute-start(bf16[128,384]{1,0:T(8,128)(2,1)} %get-tuple-element.126), channel_id=1, source_target_pairs={{0,12},{4,0},{8,4},{12,8},{1,13},{5,1},{9,5},{13,9},{2,14},{6,2},{... | collective-permute-start | bytes 294920 | tf_op jit(solution)/shard_map/ppermute | solution.py:55
  473.5 12.3 %collective-permute-start.22 = (bf16[128,384]{1,0:T(8,128)(2,1)}, bf16[128,384]{1,0:T(8,128)(2,1)}, u32[]{:S(2)}, u32[]{:S(2)}) collective-permute-start(bf16[128,384]{1,0:T(8,128)(2,1)} %get-tuple-element.127), channel_id=1, source_target_pairs={{0,8},{4,12},{8,0},{12,4},{1,9},{5,13},{9,1},{13,5},{2,10},{6,14},... | collective-permute-start | bytes 294920 | tf_op jit(solution)/shard_map/ppermute | solution.py:55
  481.2 6.0 %collective-permute-start.26 = (bf16[128,384]{1,0:T(8,128)(2,1)}, bf16[128,384]{1,0:T(8,128)(2,1)S(1)}, u32[]{:S(2)}, u32[]{:S(2)}) collective-permute-start(bf16[128,384]{1,0:T(8,128)(2,1)} %get-tuple-element.137), channel_id=1, source_target_pairs={{0,2},{2,64},{64,66},{66,0},{1,3},{3,65},{65,67},{67,1},{4,6},{6,6... | collective-permute-start | bytes 294920 | tf_op jit(solution)/shard_map/ppermute | solution.py:55
  481.2 6.8 %collective-permute-start.27 = (bf16[128,384]{1,0:T(8,128)(2,1)}, bf16[128,384]{1,0:T(8,128)(2,1)S(1)}, u32[]{:S(2)}, u32[]{:S(2)}) collective-permute-start(bf16[128,384]{1,0:T(8,128)(2,1)} %get-tuple-element.138), channel_id=1, source_target_pairs={{0,66},{2,0},{64,2},{66,64},{1,67},{3,1},{65,3},{67,65},{4,70},{6,... | collective-permute-start | bytes 294920 | tf_op jit(solution)/shard_map/ppermute | solution.py:55
  484.5 6.3 %collective-permute-start.28 = (bf16[128,384]{1,0:T(8,128)(2,1)}, bf16[128,384]{1,0:T(8,128)(2,1)S(1)}, u32[]{:S(2)}, u32[]{:S(2)}) collective-permute-start(bf16[128,384]{1,0:T(8,128)(2,1)} %get-tuple-element.139), channel_id=1, source_target_pairs={{0,64},{2,66},{64,0},{66,2},{1,65},{3,67},{65,1},{67,3},{4,68},{6,... | collective-permute-start | bytes 294920 | tf_op jit(solution)/shard_map/ppermute | solution.py:55
  (17 other events, 62.4 us)
Sparse Core Ops, SparseCore 0:
  10.8 67.4 all-gather.8
  80.0 35.8 all-gather.10
  133.6 77.5 all-gather.12
  310.0 26.6 all-gather.14
  339.0 29.6 reduce-scatter.2
  384.9 96.6 reduce-scatter.4
